TPU v7x, 256 devices: a whole 4x4x8 slice. The times are simulated.
256 devices in a mesh: dp: 64 (over y, z, x_lo), tensor: 4 (over x_hi, core).
Axes of the slice: x: 4 (x_hi: 2, x_lo: 2; x = x_hi * 2 + x_lo), y: 4, z: 8, core: 2. Of those that a mesh axis runs over, the one named last changes fastest.
Arguments:
- pooled: bfloat16 [2, 8192, 1152], P(None, 'dp', 'tensor'), may hold values from -6 to 6
- ln_gain: bfloat16 [2, 1152], replicated, may hold values from 0.5 to 1.5
- ln_bias: bfloat16 [2, 1152], replicated, may hold values from -3 to 3
- fc1: bfloat16 [2, 1152, 4304], P(None, None, 'tensor'), may hold values from -0.1875 to 0.1875
- fc1_bias: bfloat16 [2, 4304], P(None, 'tensor'), may hold values from -3 to 3
- fc2: bfloat16 [2, 4304, 1152], P(None, 'tensor'), may hold values from -0.09375 to 0.09375
- fc2_bias: bfloat16 [2, 1152], replicated, may hold values from -1.1953125 to 1.1953125
- logit_scale: float32 [], replicated, may hold values from 8 to 12
- logit_bias: float32 [], replicated, may hold values from -3 to -1
- loss_scale: float32 [], replicated, may hold values from 8192 to 65536
Outputs:
- pooled_grad: bfloat16 [2, 8192, 1152], P(None, 'dp', 'tensor')
All inputs are finite; a program needn't handle non-finite values.
Results may differ from a plain program's by a relative error of at most 0.0075.
Values may be sent and summed in bfloat16 or wider, within the bound.
No kernel may reach another device: no remote copies, remote signals or barrier semaphores. Data moves between devices by JAX's collectives and lax.ppermute only.
A program may use at most 128 MiB of HBM per device.

v0:
```python
import jax
import jax.numpy as jnp
from jax import lax
from jax.sharding import PartitionSpec as P


def layer_stats(inputs):
    centred = inputs - jnp.mean(inputs, axis=-1, keepdims=True)
    inverse = lax.rsqrt(jnp.mean(centred * centred, axis=-1, keepdims=True) + 1e-06)
    return (centred * inverse, inverse)


def gelu_tanh(values):
    return jax.nn.gelu(values, approximate=True)


def on_device(
    pooled, ln_gain, ln_bias, fc1, fc1_bias, fc2, fc2_bias, logit_scale, logit_bias, loss_scale
):
    width = pooled.shape[2]
    rows = pooled.shape[1]
    groups = lax.axis_size("tensor")
    member = lax.axis_index("tensor")
    place = lax.axis_index("dp")
    count_dp = lax.axis_size("dp")
    part_rows = rows // groups
    tokens_all = rows * count_dp
    whole_inputs = lax.all_gather(pooled, "tensor", axis=2, tiled=True)
    inputs = whole_inputs.astype(jnp.float32)
    standard, inverse = layer_stats(inputs)
    gains = ln_gain.astype(jnp.float32)[:, None, :]
    normed = (standard * gains + ln_bias.astype(jnp.float32)[:, None, :]).astype(jnp.bfloat16)
    preact = jnp.einsum("ktd,kdf->ktf", normed, fc1, preferred_element_type=jnp.float32)
    preact = preact + fc1_bias.astype(jnp.float32)[:, None, :]
    hidden = gelu_tanh(preact).astype(jnp.bfloat16)
    partial_value = jnp.einsum("ktf,kfe->kte", hidden, fc2, preferred_element_type=jnp.float32)
    blocks = inputs + lax.psum(partial_value, "tensor") + fc2_bias.astype(jnp.float32)[:, None, :]
    lengths = jnp.sqrt(jnp.sum(blocks * blocks, axis=-1, keepdims=True) + 1e-06)
    units = (blocks / lengths).astype(jnp.bfloat16)
    images = units[0]
    texts_own = lax.dynamic_slice_in_dim(units[1], member * part_rows, part_rows, 0)
    factor = loss_scale * logit_scale / tokens_all
    image_ids = place * rows + jnp.arange(rows, dtype=jnp.int32)
    piece = lax.all_gather(texts_own, "dp", axis=0, tiled=True)
    position = jnp.arange(piece.shape[0], dtype=jnp.int32)
    text_ids = position // part_rows * rows + member * part_rows + position % part_rows
    scores = jnp.einsum("id,jd->ij", images, piece, preferred_element_type=jnp.float32)
    logits = logit_scale * scores + logit_bias
    diagonal = (image_ids[:, None] == text_ids[None, :]).astype(jnp.float32)
    weights = (factor * (jax.nn.sigmoid(logits) - diagonal)).astype(jnp.bfloat16)
    image_acc = jnp.dot(weights, piece, preferred_element_type=jnp.float32)
    term = jnp.einsum("ij,id->jd", weights, images, preferred_element_type=jnp.float32)
    text_own = lax.psum_scatter(term, "dp", scatter_dimension=0, tiled=True)
    image_grad = lax.psum(image_acc, "tensor")
    text_grad = lax.all_gather(text_own, "tensor", axis=0, tiled=True)
    unit_grad = jnp.stack([image_grad, text_grad])
    unit_float = units.astype(jnp.float32)
    along = jnp.sum(unit_float * unit_grad, axis=-1, keepdims=True)
    block_grad = (unit_grad - unit_float * along) / lengths
    hidden_grad = jnp.einsum(
        "kte,kfe->ktf", block_grad.astype(jnp.bfloat16), fc2, preferred_element_type=jnp.float32
    )
    _, gelu_back = jax.vjp(gelu_tanh, preact)
    preact_grad = gelu_back(hidden_grad)[0].astype(jnp.bfloat16)
    normed_grad = jnp.einsum("ktf,kdf->ktd", preact_grad, fc1, preferred_element_type=jnp.float32)
    scaled = normed_grad * gains
    norm_term = (
        scaled
        - jnp.mean(scaled, axis=-1, keepdims=True)
        - standard * jnp.mean(scaled * standard, axis=-1, keepdims=True)
    ) * inverse
    norm_share = lax.psum_scatter(norm_term, "tensor", scatter_dimension=2, tiled=True)
    block_share_grad = lax.dynamic_slice_in_dim(block_grad, member * width, width, 2)
    return (block_share_grad + norm_share).astype(jnp.bfloat16)


def solution(mesh):
    in_specs = (
        P(None, "dp", "tensor"),
        P(),
        P(),
        P(None, None, "tensor"),
        P(None, "tensor"),
        P(None, "tensor", None),
        P(),
        P(),
        P(),
        P(),
    )
    out_specs = P(None, "dp", "tensor")
    return jax.shard_map(
        on_device, mesh=mesh, in_specs=in_specs, out_specs=out_specs, check_vma=False
    )
```

profile of v0, /device:TPU:1, one launch (start us, length us, event | category | flops | bytes accessed | tf_op | source)
XLA Modules:
  0.0 854.6 jit_solution(8503142726177308414)
XLA Ops:
  6.5 0.7 convert_element_type.43
  7.2 0.7 convert_element_type.44
  7.9 0.7 convert_element_type.46
  8.6 1.0 copy.40
  9.6 11.3 %all_gather.9 = bf16[2,128,1152]{1,0,2:T(2,128)(2,1)S(1)} all-gather(bf16[2,128,288]{1,0,2:T(2,128)(2,1)S(1)} %copy.40), channel_id=1, replica_groups=mesh['dp'=64,'tensor'=4] {'tensor'}, dimensions={2}, use_global_device_ids=true | all-gather | bytes 737280 | tf_op jit(solution)/shard_map/all_gather | solution.py:28
  21.3 5.8 fusion.16
  27.1 1.0 copy-done.5
  28.1 3.3 fusion.7
  32.0 52.6 %all-reduce.5.cloned.1.call-done = f32[2,128,1152]{1,2,0:T(8,128)} async-done(((f32[2,128,1152]{1,2,0:T(8,128)}), f32[2,128,1152]{1,2,0:T(8,128)}) %all-reduce.5.cloned.1.call-update) | async-done | bytes 1179664 | tf_op jit(solution)/shard_map/psum | solution.py:37
  84.7 1.7 multiply_reduce_fusion
  87.1 0.8 copy.46
  89.9 261.5 %all-gather.3.cloned.1.call-done = bf16[1,2048,1152]{2,1,0:T(8,128)(2,1)} async-done(((bf16[1,32,1152]{2,1,0:T(8,128)(2,1)}), bf16[1,2048,1152]{2,1,0:T(8,128)(2,1)}) %all-gather.3.cloned.1.call-update) | async-done | bytes 4718608 | tf_op jit(solution)/shard_map/all_gather | solution.py:44
  351.4 4.1 fusion.49
  355.5 5.1 fusion.92
  360.6 5.1 fusion.22
  365.8 323.6 %reduce-scatter.4.cloned.1.call-done = f32[32,1152]{1,0:T(8,128)} async-done(((f32[2048,1152]{1,0:T(8,128)}), f32[32,1152]{1,0:T(8,128)}) %reduce-scatter.4.cloned.1.call-update) | async-done | bytes 147472 | tf_op jit(solution)/shard_map/reduce_scatter | solution.py:53
  689.5 56.8 %all_gather.11 = f32[128,1152]{1,0:T(8,128)S(1)} all-gather(f32[32,1152]{1,0:T(8,128)} %reduce-scatter.4.cloned.1.call-done), channel_id=1, replica_groups=mesh['dp'=64,'tensor'=4] {'tensor'}, dimensions={0}, use_global_device_ids=true | all-gather | bytes 737280 | tf_op jit(solution)/shard_map/all_gather | solution.py:55
  746.5 34.1 %all-reduce.7.cloned.1.call-done = f32[1,128,1152]{1,2,0:T(8,128)} async-done(((f32[1,128,1152]{1,2,0:T(8,128)}), f32[1,128,1152]{1,2,0:T(8,128)}) %all-reduce.7.cloned.1.call-update) | async-done | bytes 589840 | tf_op jit(solution)/shard_map/psum | solution.py:54
  780.6 1.6 fusion.15
  782.2 7.8 fusion.115
  790.3 5.1 copy.55
  797.3 49.1 %all-reduce.9.cloned.1.call-done = f32[2,128,1152]{1,0,2:T(2,128)} async-done(((f32[2,128,1152]{1,0,2:T(2,128)}), f32[2,128,1152]{1,0,2:T(2,128)}) %all-reduce.9.cloned.1.call-update) | async-done | bytes 1179664
  846.4 1.0 constant_dynamic-slice_fusion
  847.4 0.7 fusion.91
  (41 shorter events, 3.6 us)
Async XLA Ops:
  6.5 78.1 %all-reduce.5.cloned.1.call-start = ((), (), s32[]{:S(2)}) async-start(), calls=%async_computation.1 | async-start | bytes 2359296 | tf_op jit(solution)/shard_map/psum | solution.py:37
  21.1 7.0 slice-start
  21.3 5.8 copy-start.2
  21.3 6.8 slice-start.1
  27.1 1.0 copy-start.5
  31.3 0.7 copy-start.1
  31.4 320.0 %all-gather.3.cloned.1.call-start = ((), (), s32[]{:S(2)}) async-start(), calls=%async_computation.3 | async-start | bytes 4792320 | tf_op jit(solution)/shard_map/all_gather | solution.py:44
  84.7 1.8 copy-start
  87.9 601.6 %reduce-scatter.4.cloned.1.call-start = ((), (), s32[]{:S(2)}) async-start(), calls=%async_computation.4 | async-start | bytes 9584640 | tf_op jit(solution)/shard_map/reduce_scatter | solution.py:53
  360.6 420.0 %all-reduce.7.cloned.1.call-start = ((), (), s32[]{:S(2)}) async-start(), calls=%async_computation.2 | async-start | bytes 1179648 | tf_op jit(solution)/shard_map/psum | solution.py:54
  365.8 480.6 %all-reduce.9.cloned.1.call-start = ((), (), s32[]{:S(2)}) async-start(), calls=%async_computation.5 | async-start | bytes 2359296
  782.2 7.8 copy-start.3
  795.4 0.7 copy-start.4
Sparse Core Ops, SparseCore 0:
  31.5 53.1 all-reduce.4
  88.0 263.3 all-gather.2
  360.7 328.7 reduce-scatter.3
  692.0 88.5 all-reduce.6
  795.5 50.8 all-reduce.8
where the time goes:
time: 855 us
  waiting for transfers between devices  721 us (84%)
  blocking collectives  68 us (8%)
  matrix products  31 us (4%)
  between operations  15.9 us (2%)
  local copies, waits for them, and re-layouts  11.2 us (1%)
    reduce_scatter x1, waiting for transfers between devices, on_device(): text_own = lax.psum_scatter(term, 'dp', scatter_dimension=0, tiled=True)  324 us
    all_gather x1, waiting for transfers between devices, on_device(): piece = lax.all_gather(texts_own, 'dp', axis=0, tiled=True)  261 us
    all_gather x1, blocking collectives, on_device(): text_grad = lax.all_gather(text_own, 'tensor', axis=0, tiled=True)  56.8 us
    psum x1, waiting for transfers between devices, on_device(): lax.psum(partial_value, 'tensor')  52.6 us
    unnamed x6, waiting for transfers between devices  49.2 us
    psum x1, waiting for transfers between devices, on_device(): image_grad = lax.psum(image_acc, 'tensor')  34.1 us
  transfers between devices with their start and end apart: 5, of which 5 were waited for; matrix products, arithmetic and copies ran while one was open for 1% of the time, Pallas kernels for 0%

commit v1 on v0

v1 whole, which is shorter than its diff:
```python
import functools

import jax
import jax.numpy as jnp
from jax import lax
from jax.experimental import pallas as pl
from jax.experimental.layout import Layout, with_layout_constraint
from jax.experimental.pallas import tpu as pltpu
from jax.sharding import Mesh
from jax.sharding import PartitionSpec as P

TENSOR = ("xh", "c")
DP = ("y", "z", "xl")
PLANE = ("y", "xl", "xh")
BF = jnp.bfloat16
F32 = jnp.float32


def layer_stats(inputs):
    centred = inputs - jnp.mean(inputs, axis=-1, keepdims=True)
    inverse = lax.rsqrt(jnp.mean(centred * centred, axis=-1, keepdims=True) + 1e-06)
    return (centred * inverse, inverse)


def gelu_tanh(values):
    return jax.nn.gelu(values, approximate=True)


def normalise(blocks):
    lengths = jnp.sqrt(jnp.sum(blocks * blocks, axis=-1, keepdims=True) + 1e-06)
    return (as_lies((blocks / lengths).astype(BF)), lengths)


def through_normalise(unit_grad, units, lengths):
    unit_grad = as_lies(unit_grad)
    units = units.astype(F32)
    along = jnp.sum(units * unit_grad, axis=-1, keepdims=True)
    return ((unit_grad - units * along) / lengths).astype(BF)


def as_lies(array):
    return with_layout_constraint(array, Layout(tuple(range(array.ndim))))


def hop(block, places):
    size = lax.axis_size("z")
    pairs = [
        ((z + (places, -places)[core]) % size * 2 + core, z * 2 + core)
        for z in range(size)
        for core in range(2)
    ]
    return as_lies(lax.ppermute(as_lies(block), ("z", "c"), pairs))


def exchange(parts, axes):
    return lax.all_to_all(parts, axes, 0, 0, tiled=True)


def swap(block, axis):
    return as_lies(lax.ppermute(as_lies(block), axis, [(0, 1), (1, 0)]))


def pick(array, index, axis):
    return lax.dynamic_index_in_dim(array, index, axis, keepdims=False)


def swap_sum(parts, name, axis):
    me = lax.axis_index(name)
    got = swap(pick(parts, 1 - me, axis).astype(BF), name)
    return pick(parts, me, axis).astype(F32) + got.astype(F32)


def in_order(own, other, name, axis):
    first = lax.axis_index(name) == 0
    return jnp.concatenate(
        [jnp.where(first, own, other), jnp.where(first, other, own)], axis=axis
    )


def swap_join(own, name, axis):
    return in_order(own, swap(own, name), name, axis)


def gather_ring(own, texts):
    half = own.shape[0]
    chip = swap_join(own, "c", 0)
    one, two = hop(chip, 1), hop(chip, 2)
    three = hop(two, 1)
    four = hop(lax.dynamic_slice_in_dim(two, lax.axis_index("c") * half, half, 0), 2)
    fetched = jnp.concatenate([one, two, three, four], axis=0)
    fetched, texts = lax.optimization_barrier((fetched, texts))
    return jnp.concatenate([chip, fetched, swap(fetched, "c")], axis=0), texts


def sum_ring(chip, fetched, other, texts):
    half = chip.shape[0] // 2
    fetched = fetched + swap(other, "c").astype(F32)
    one, two, three, four = jnp.split(fetched, [2 * half, 4 * half, 6 * half], axis=0)
    three = hop(three.astype(BF), -1).astype(F32)
    four = hop(four.astype(BF), -2).astype(F32)
    one = hop(one.astype(BF), -1).astype(F32)
    first = lax.axis_index("c") == 0
    none = jnp.zeros_like(four)
    two = two + three
    two = two + jnp.concatenate([jnp.where(first, four, none), jnp.where(first, none, four)])
    two = hop(two.astype(BF), -2).astype(F32)
    own, texts = lax.optimization_barrier((chip + one + two, texts))
    return swap_sum(own.reshape(2, half, -1), "c", 0), texts


def loss_kernel(
    part_rows, scalars, first, images, texts, chip, fetched, other, text_part, image_sum
):
    tile = 256
    for start in range(0, texts.shape[0], tile):
        block = texts[pl.ds(start, tile), :]
        scores = lax.dot_general(
            images[...], block, (((1,), (1,)), ((), ())), preferred_element_type=F32
        )
        logits = scalars[0] * scores + scalars[1]
        at_image = lax.broadcasted_iota(jnp.int32, scores.shape, 0) - first[0]
        at_text = lax.broadcasted_iota(jnp.int32, scores.shape, 1) + (start - first[1])
        diagonal = (at_image == at_text) & (at_image >= 0) & (at_image < part_rows)
        diagonal = diagonal.astype(F32)
        weights = (scalars[2] * (jax.nn.sigmoid(logits) - diagonal)).astype(BF)
        text_part[pl.ds(start, tile), :] = lax.dot_general(
            weights, images[...], (((0,), (0,)), ((), ())), preferred_element_type=F32
        ).astype(BF)
        product = jnp.dot(weights, block, preferred_element_type=F32)
        if start == 0:
            image_sum[...] = product
        else:
            image_sum[...] += product
    at_fetched, at_other = chip.shape[0], chip.shape[0] + fetched.shape[0]
    chip[...] = image_sum[:at_fetched, :]
    fetched[...] = image_sum[at_fetched:at_other, :]
    other[...] = image_sum[at_other:, :].astype(BF)


def loss_block(scalars, first, images, texts, part_rows):
    rows, dim = images.shape
    fetched = rows // 2 - part_rows
    whole = pl.BlockSpec(memory_space=pltpu.VMEM)
    small = pl.BlockSpec(memory_space=pltpu.SMEM)
    return pl.pallas_call(
        functools.partial(loss_kernel, part_rows),
        in_specs=[small, small, whole, whole],
        out_specs=[whole] * 4,
        out_shape=[
            jax.ShapeDtypeStruct((2 * part_rows, dim), F32),
            jax.ShapeDtypeStruct((fetched, dim), F32),
            jax.ShapeDtypeStruct((fetched, dim), BF),
            jax.ShapeDtypeStruct(texts.shape, BF),
        ],
        scratch_shapes=[pltpu.VMEM((rows, dim), F32)],
        compiler_params=pltpu.CompilerParams(vmem_limit_bytes=20 * 1024 * 1024),
        cost_estimate=pl.CostEstimate(
            flops=6 * rows * texts.shape[0] * dim,
            bytes_accessed=10 * rows * dim,
            transcendentals=rows * texts.shape[0],
        ),
    )(scalars, first, images, texts)


def on_device(
    pooled, ln_gain, ln_bias, fc1, fc1_bias, fc2, fc2_bias, logit_scale, logit_bias, loss_scale
):
    rows, width = pooled.shape[1], pooled.shape[2]
    member = lax.axis_index(TENSOR)
    part_rows = rows // lax.axis_size(TENSOR)
    tokens_all = rows * lax.axis_size(DP)

    own = jnp.swapaxes(pooled, 1, 2)
    far = swap(own, "xh")
    whole = in_order(own[:, None, None], far[:, None, None], "xh", 1)
    whole = swap_join(whole, "c", 2).reshape(2, 4 * width, rows)
    whole, ln_gain, ln_bias, fc1_bias, fc2_bias = lax.optimization_barrier(
        (whole, ln_gain, ln_bias, fc1_bias, fc2_bias)
    )
    inputs = jnp.swapaxes(whole, 1, 2).astype(F32)
    dim = inputs.shape[2]
    standard, inverse = layer_stats(inputs)
    gains = ln_gain.astype(F32)[:, None, :]
    normed = (standard * gains + ln_bias.astype(F32)[:, None, :]).astype(BF)
    preact = jnp.einsum("ktd,kdf->ktf", normed, fc1, preferred_element_type=F32)
    preact = preact + fc1_bias.astype(F32)[:, None, :]
    hidden = gelu_tanh(preact).astype(BF)
    partial = as_lies(jnp.einsum("ktf,kfe->kte", hidden, fc2, preferred_element_type=F32))

    quarter = lax.axis_index("c") * 2 + lax.axis_index("xh")
    partial = swap_sum(partial.reshape(2, 2, 2 * part_rows, dim), "c", 1)
    summed = swap_sum(partial.reshape(2, 2, part_rows, dim), "xh", 1)
    own_inputs = as_lies(lax.dynamic_slice_in_dim(inputs, quarter * part_rows, part_rows, 1))
    units, lengths = normalise(own_inputs + summed + fc2_bias.astype(F32)[:, None, :])

    n_text = lax.axis_size(PLANE)
    texts = exchange(jnp.broadcast_to(units[1], (n_text, part_rows, dim)), PLANE)
    texts = texts.reshape(n_text * part_rows, dim)
    images, texts = gather_ring(units[0], texts)
    factor = loss_scale * logit_scale / tokens_all
    scalars = jnp.stack([logit_scale, logit_bias, factor]).astype(F32)
    first = jnp.stack([lax.axis_index("c"), lax.axis_index(PLANE)]).astype(jnp.int32) * part_rows
    chip_part, fetched_part, other_part, text_part = loss_block(
        scalars, first, images, texts, part_rows
    )
    text_part = exchange(text_part.reshape(n_text, part_rows, dim), PLANE)
    image_grad, text_part = sum_ring(chip_part, fetched_part, other_part, text_part)
    text_grad = jnp.sum(text_part.astype(F32), axis=0)

    block_own = through_normalise(jnp.stack([image_grad, text_grad]), units, lengths)
    block_own = as_lies(block_own)
    block_low = as_lies(swap_join(as_lies(swap_join(block_own, "xh", 1)), "c", 1))
    hidden_grad = jnp.einsum("kte,kfe->ktf", block_low, fc2, preferred_element_type=F32)
    _, gelu_back = jax.vjp(gelu_tanh, preact)
    preact_grad = lax.optimization_barrier(gelu_back(hidden_grad)[0].astype(BF))
    normed_grad = jnp.einsum("ktf,kdf->ktd", preact_grad, fc1, preferred_element_type=F32)
    scaled = normed_grad * gains
    norm_term = (
        scaled
        - jnp.mean(scaled, axis=-1, keepdims=True)
        - standard * jnp.mean(scaled * standard, axis=-1, keepdims=True)
    ) * inverse
    norm_parts = as_lies(jnp.swapaxes(norm_term, 1, 2)).reshape(2, 2, 2, width, rows)
    norm_parts = as_lies(swap_sum(norm_parts, "c", 2))
    norm_share = as_lies(swap_sum(norm_parts, "xh", 1))
    block_share = as_lies(lax.dynamic_slice_in_dim(block_low, member * width, width, 2))
    block_share = as_lies(jnp.swapaxes(block_share, 1, 2)).astype(F32)
    return jnp.swapaxes(as_lies((block_share + norm_share).astype(BF)), 1, 2)


def solution(mesh):
    fine = Mesh(mesh.devices.reshape(4, 8, 2, 2, 2), ("y", "z", "xl", "xh", "c"))
    in_specs = (
        P(None, DP, TENSOR),
        P(),
        P(),
        P(None, None, TENSOR),
        P(None, TENSOR),
        P(None, TENSOR, None),
        P(),
        P(),
        P(),
        P(),
    )
    return jax.shard_map(
        on_device, mesh=fine, in_specs=in_specs, out_specs=P(None, DP, TENSOR), check_vma=False
    )
```

time: 855 us -> 117 us (0.14)
  waiting for transfers between devices: 721 us -> 40.3 us
  blocking collectives: 68 us -> 0 us
  starting transfers between devices: 0.17 us -> 48.9 us
  matrix products: 31 us -> 12.8 us
  between operations: 15.9 us -> 2.42 us
  local copies, waits for them, and re-layouts: 11.2 us -> 2.57 us
    reduce_scatter x1 -> x0, waiting for transfers between devices: 324 us -> none  [on_device(): text_own = lax.psum_scatter(term, 'dp', scatter_dimension=0, tiled=True)]
    all_gather x1 -> x0, waiting for transfers between devices: 261 us -> none  [on_device(): piece = lax.all_gather(texts_own, 'dp', axis=0, tiled=True)]
    psum x2 -> x0, waiting for transfers between devices: 86.8 us -> none  [the longest x1 52.6 us: on_device(): lax.psum(partial_value, 'tensor')]
    all_gather x2 -> x0, blocking collectives: 68 us -> none  [the longest x1 56.8 us: on_device(): text_grad = lax.all_gather(text_own, 'tensor', axis=0, tiled=True)]
    unnamed x6 -> x0, waiting for transfers between devices: 49.2 us -> none
    ppermute x0 -> x20, waiting for transfers between devices: none -> 40.3 us  [the longest x8 20.5 us: hop(): return as_lies(lax.ppermute(as_lies(block), ('z', 'c'), pairs))]
    ppermute x0 -> x20, starting transfers between devices: none -> 36.5 us  [the longest x12 23 us: swap(): return as_lies(lax.ppermute(as_lies(block), axis, [(0, 1), (1, 0)]))]
    dot_general x5 -> x4, matrix products: 26 us -> 12.8 us  [the longest x1 4.63 us: on_device(): jnp.einsum('kte,kfe->ktf', block_low, fc2, preferred_element_type=F32)]
  transfers between devices with their start and end apart: 5 -> 22, of which waited for: 5 -> 15; matrix products, arithmetic and copies ran while one was open for 1% -> 3% of each run, Pallas kernels for 0% -> 0%
where the time goes in v1:
time: 117 us
  starting transfers between devices  48.9 us (42%)
  waiting for transfers between devices  40.3 us (34%)
  matrix products  12.8 us (11%)
  other arithmetic  5.13 us (4%)
  Pallas kernels  4.47 us (4%)
  local copies, waits for them, and re-layouts  2.57 us (2%)
  between operations  2.42 us (2%)
    ppermute x12, starting transfers between devices, swap(): return as_lies(lax.ppermute(as_lies(block), axis, [(0, 1), (1, 0)]))  23 us
    ppermute x8, waiting for transfers between devices, hop(): return as_lies(lax.ppermute(as_lies(block), ('z', 'c'), pairs))  20.5 us
    ppermute x12, waiting for transfers between devices, swap(): return as_lies(lax.ppermute(as_lies(block), axis, [(0, 1), (1, 0)]))  19.8 us
    ppermute x8, starting transfers between devices, hop(): return as_lies(lax.ppermute(as_lies(block), ('z', 'c'), pairs))  13.5 us
    all_to_all x2, starting transfers between devices, exchange(): return lax.all_to_all(parts, axes, 0, 0, tiled=True)  12.4 us
    dot_general x1, matrix products, on_device(): jnp.einsum('kte,kfe->ktf', block_low, fc2, preferred_element_type=F32)  4.63 us
    pallas_call x1, Pallas kernels, loss_block(): pl.pallas_call(functools.partial(loss_kernel, part_rows), in_specs=[small...  4.47 us
    dot_general x1, matrix products, on_device(): preact = jnp.einsum('ktd,kdf->ktf', normed, fc1, preferred_element_type=F32)  4.45 us
  transfers between devices with their start and end apart: 22, of which 15 were waited for; matrix products, arithmetic and copies ran while one was open for 3% of the time, Pallas kernels for 0%

profile of v1, /device:TPU:1, one launch (start us, length us, event | category | flops | bytes accessed | tf_op | source)
XLA Modules:
  0.0 116.5 jit_solution(16044721897453011924)
XLA Ops:
  0.0 3.6 %collective-permute-start = (bf16[2,288,128]{2,1,0:T(8,128)(2,1)}, bf16[2,288,128]{2,1,0:T(8,128)(2,1)S(1)}, u32[]{:S(2)}, u32[]{:S(2)}) collective-permute-start(bf16[2,288,128]{2,1,0:T(8,128)(2,1)} %bitcast.125), channel_id=1, source_target_pairs={{0,2},{2,0},{1,3},{3,1},{4,6},{6,4},{5,7},{7,5},{8,10},{10,8},{9,1... | collective-permute-start | bytes 442376 | tf_op jit(solution)/shard_map/ppermute | solution.py:60
  3.6 2.8 %collective-permute-done = bf16[2,288,128]{2,1,0:T(8,128)(2,1)S(1)} collective-permute-done((bf16[2,288,128]{2,1,0:T(8,128)(2,1)}, bf16[2,288,128]{2,1,0:T(8,128)(2,1)S(1)}, u32[]{:S(2)}, u32[]{:S(2)}) %collective-permute-start) | collective-permute-done | bytes 147488 | tf_op jit(solution)/shard_map/ppermute | solution.py:60
  7.4 3.8 %collective-permute-start.1 = (bf16[2,2,1,288,128]{4,3,2,1,0:T(8,128)(2,1)S(1)}, bf16[2,2,1,288,128]{4,3,2,1,0:T(8,128)(2,1)S(1)}, u32[]{:S(2)}, u32[]{:S(2)}) collective-permute-start(bf16[2,2,1,288,128]{4,3,2,1,0:T(8,128)(2,1)S(1)} %pad_maximum_fusion.5), channel_id=1, source_target_pairs={{0,1},{1,0},{2,3},{3,2},{4,5},{5,4},{6,7},{7,6},{8,9},{9,8},{10,11... | collective-permute-start | bytes 884744 | tf_op jit(solution)/shard_map/ppermute | solution.py:60
  13.2 4.4 %fusion.9 = f32[2,128,1076]{1,2,0:T(8,128)S(1)} fusion(bf16[2,1152,1076]{1,0,2:T(2,128)(2,1)} %param.13, bf16[2,1152,128]{2,1,0:T(8,128)(2,1)S(1)} %bitcast.112, f32[2,1152]{1,0:T(2,128)S(1)} %convert_element_type.115, f32[2,1152]{1,0:T(2,128)S(1)} %convert_element_type.114, f32[2,128]{1,0:T(2,128)S(1)} %add_rsqrt_fusion, ...), kind=kOutput, calls=%fused_computation.9 | convolution fusion | flops 636695552 | bytes 6678944 | tf_op jit(solution)/shard_map/ktd,kdf->ktf/dot_general | solution.py:185
  23.0 4.4 %collective-permute-done.3 = bf16[2,32,1152]{2,1,0:T(8,128)(2,1)S(1)} collective-permute-done((bf16[2,32,1152]{2,1,0:T(8,128)(2,1)S(1)}, bf16[2,32,1152]{2,1,0:T(8,128)(2,1)S(1)}, u32[]{:S(2)}, u32[]{:S(2)}) %collective-permute-start.3) | collective-permute-done | bytes 147488 | tf_op jit(solution)/shard_map/ppermute | solution.py:60
  30.1 5.5 %all-to-all-start = ((bf16[16,32,1152]{2,1,0:T(8,128)(2,1)}), bf16[16,32,1152]{2,1,0:T(8,128)(2,1)S(1)}, u32[]{:S(2)}, u32[]{:S(2)}) async-start(bf16[16,32,1152]{2,1,0:T(8,128)(2,1)} %broadcast_in_dim.4), calls=%async_computation | async-start | bytes 2359296 | tf_op jit(solution)/shard_map/all_to_all | solution.py:56
  35.6 3.1 %collective-permute-start.6 = (bf16[64,1152]{1,0:T(8,128)(2,1)S(1)}, bf16[64,1152]{1,0:T(8,128)(2,1)S(1)}, u32[]{:S(2)}, u32[]{:S(2)}) collective-permute-start(bf16[64,1152]{1,0:T(8,128)(2,1)S(1)} %pad_maximum_fusion.9), channel_id=1, source_target_pairs={{16,0},{49,1},{24,8},{57,9},{32,16},{1,17},{40,24},{9,25},{48,32},... | collective-permute-start | bytes 442376 | tf_op jit(solution)/shard_map/ppermute | solution.py:52
  38.7 1.6 %collective-permute-start.5 = (bf16[64,1152]{1,0:T(8,128)(2,1)S(1)}, bf16[64,1152]{1,0:T(8,128)(2,1)S(1)}, u32[]{:S(2)}, u32[]{:S(2)}) collective-permute-start(bf16[64,1152]{1,0:T(8,128)(2,1)S(1)} %pad_maximum_fusion.9), channel_id=1, source_target_pairs={{8,0},{57,1},{16,8},{1,9},{24,16},{9,17},{32,24},{17,25},{40,32},{... | collective-permute-start | bytes 442376 | tf_op jit(solution)/shard_map/ppermute | solution.py:52
  40.3 4.3 %collective-permute-done.6 = bf16[64,1152]{1,0:T(8,128)(2,1)S(1)} collective-permute-done((bf16[64,1152]{1,0:T(8,128)(2,1)S(1)}, bf16[64,1152]{1,0:T(8,128)(2,1)S(1)}, u32[]{:S(2)}, u32[]{:S(2)}) %collective-permute-start.6) | collective-permute-done | bytes 147488 | tf_op jit(solution)/shard_map/ppermute | solution.py:52
  44.6 2.3 %collective-permute-start.7 = (bf16[64,1152]{1,0:T(8,128)(2,1)S(1)}, bf16[64,1152]{1,0:T(8,128)(2,1)S(1)}, u32[]{:S(2)}, u32[]{:S(2)}) collective-permute-start(bf16[64,1152]{1,0:T(8,128)(2,1)S(1)} %collective-permute-done.6), channel_id=1, source_target_pairs={{8,0},{57,1},{16,8},{1,9},{24,16},{9,17},{32,24},{17,25},{40,32},{... | collective-permute-start | bytes 442376 | tf_op jit(solution)/shard_map/ppermute | solution.py:52
  47.3 6.1 %collective-permute-done.8 = bf16[32,1152]{1,0:T(8,128)(2,1)S(1)} collective-permute-done((bf16[32,1152]{1,0:T(8,128)(2,1)S(1)}, bf16[32,1152]{1,0:T(8,128)(2,1)S(1)}, u32[]{:S(2)}, u32[]{:S(2)}) %collective-permute-start.8) | collective-permute-done | bytes 73760 | tf_op jit(solution)/shard_map/ppermute | solution.py:52
  57.0 4.5 %shard_map.100 = (f32[64,1152]{1,0:T(8,128)S(1)}, f32[224,1152]{1,0:T(8,128)S(1)}, bf16[224,1152]{1,0:T(8,128)(2,1)S(1)}, bf16[512,1152]{1,0:T(8,128)(2,1)}) custom-call(f32[3]{0:T(128)S(1)} %pad_maximum_fusion.10.scalars, s32[2]{0:T(128)S(1)} %add_multiply_fusion.first, bf16[512,1152]{1,0:T(8,128)(2,1)S(1)} %pad_maximum_fusion.images, ...), custom_call_target="tpu_custom_call" | custom-call | flops 1811939328 | bytes 5898240 | tf_op jit(solution)/shard_map/pallas_call | solution.py:145
  61.5 6.9 %all-to-all-start.1 = ((bf16[16,32,1152]{2,1,0:T(8,128)(2,1)}), bf16[16,32,1152]{2,1,0:T(8,128)(2,1)S(1)}, u32[]{:S(2)}, u32[]{:S(2)}) async-start(bf16[16,32,1152]{2,1,0:T(8,128)(2,1)} %bitcast.21), calls=%async_computation.1 | async-start | bytes 2359296 | tf_op jit(solution)/shard_map/all_to_all | solution.py:56
  69.6 3.3 %collective-permute-start.13 = (bf16[32,1152]{1,0:T(8,128)(2,1)S(1)}, bf16[32,1152]{1,0:T(8,128)(2,1)S(1)}, u32[]{:S(2)}, u32[]{:S(2)}) collective-permute-start(bf16[32,1152]{1,0:T(8,128)(2,1)S(1)} %split.22), channel_id=1, source_target_pairs={{48,0},{17,1},{56,8},{25,9},{0,16},{33,17},{8,24},{41,25},{16,32},... | collective-permute-start | bytes 221192 | tf_op jit(solution)/shard_map/ppermute | solution.py:52
  74.9 4.6 %collective-permute-done.12 = bf16[64,1152]{1,0:T(8,128)(2,1)S(1)} collective-permute-done((bf16[64,1152]{1,0:T(8,128)(2,1)S(1)}, bf16[64,1152]{1,0:T(8,128)(2,1)S(1)}, u32[]{:S(2)}, u32[]{:S(2)}) %collective-permute-start.12) | collective-permute-done | bytes 147488 | tf_op jit(solution)/shard_map/ppermute | solution.py:52
  79.5 1.7 %collective-permute-start.14 = (bf16[64,1152]{1,0:T(8,128)(2,1)S(1)}, bf16[64,1152]{1,0:T(8,128)(2,1)S(1)}, u32[]{:S(2)}, u32[]{:S(2)}) collective-permute-start(bf16[64,1152]{1,0:T(8,128)(2,1)S(1)} %fusion.42), channel_id=1, source_target_pairs={{48,0},{17,1},{56,8},{25,9},{0,16},{33,17},{8,24},{41,25},{16,32},... | collective-permute-start | bytes 442376 | tf_op jit(solution)/shard_map/ppermute | solution.py:52
  81.3 4.8 %collective-permute-done.14 = bf16[64,1152]{1,0:T(8,128)(2,1)S(1)} collective-permute-done((bf16[64,1152]{1,0:T(8,128)(2,1)S(1)}, bf16[64,1152]{1,0:T(8,128)(2,1)S(1)}, u32[]{:S(2)}, u32[]{:S(2)}) %collective-permute-start.14) | collective-permute-done | bytes 147488 | tf_op jit(solution)/shard_map/ppermute | solution.py:52
  86.1 2.9 %collective-permute-start.15 = (bf16[32,1152]{1,0:T(8,128)(2,1)S(1)}, bf16[32,1152]{1,0:T(8,128)(2,1)S(1)}, u32[]{:S(2)}, u32[]{:S(2)}) collective-permute-start(bf16[32,1152]{1,0:T(8,128)(2,1)S(1)} %fusion.52), channel_id=1, source_target_pairs={{0,1},{1,0},{2,3},{3,2},{4,5},{5,4},{6,7},{7,6},{8,9},{9,8},{10,11... | collective-permute-start | bytes 221192 | tf_op jit(solution)/shard_map/ppermute | solution.py:60
  90.1 3.2 %collective-permute-start.16 = (bf16[2,32,1152]{2,1,0:T(8,128)(2,1)S(1)}, bf16[2,32,1152]{2,1,0:T(8,128)(2,1)S(1)}, u32[]{:S(2)}, u32[]{:S(2)}) collective-permute-start(bf16[2,32,1152]{2,1,0:T(8,128)(2,1)S(1)} %fusion.18), channel_id=1, source_target_pairs={{0,2},{2,0},{1,3},{3,1},{4,6},{6,4},{5,7},{7,5},{8,10},{10,8},{9,1... | collective-permute-start | bytes 442376 | tf_op jit(solution)/shard_map/ppermute | solution.py:60
  93.4 3.8 %collective-permute-done.16 = bf16[2,32,1152]{2,1,0:T(8,128)(2,1)S(1)} collective-permute-done((bf16[2,32,1152]{2,1,0:T(8,128)(2,1)S(1)}, bf16[2,32,1152]{2,1,0:T(8,128)(2,1)S(1)}, u32[]{:S(2)}, u32[]{:S(2)}) %collective-permute-start.16) | collective-permute-done | bytes 147488 | tf_op jit(solution)/shard_map/ppermute | solution.py:60
  99.9 4.6 %fusion.27 = bf16[2,128,1076]{1,2,0:T(8,128)(2,1)S(1)} fusion(f32[2,128,1076]{1,2,0:T(8,128)S(1)} %copy-done.7, bf16[2,1076,1152]{2,0,1:T(2,128)(2,1)} %param.15, bf16[2,64,1152]{2,1,0:T(8,128)(2,1)S(1)} %get-tuple-element.36, bf16[2,64,1152]{2,1,0:T(8,128)(2,1)S(1)} %get-tuple-element.35), kind=kOutput, calls=%fused_computation.34 | convolution fusion | flops 641339392 | bytes 7200768 | tf_op jit(solution)/shard_map/kte,kfe->ktf/dot_general | solution.py:213
  104.6 2.4 %fusion.59 = (f32[2,128]{1,0:T(2,128)S(1)}, f32[2,128]{1,0:T(2,128)S(1)}, f32[2,128,1152]{1,2,0:T(8,128)S(1)}) fusion(f32[2,128]{1,0:T(2,128)S(1)} %add_rsqrt_fusion, f32[2,128]{1,0:T(2,128)S(1)} %broadcast_multiply_fusion.2, bf16[2,1152,128]{2,1,0:T(8,128)(2,1)S(1)} %bitcast.114, f32[2,1152]{1,0:T(2,128)S(1)} %convert_element_type.114, ...), kind=kOutput, calls=%fused_computation.112 | convolution fusion | flops 636714496 | bytes 7291904 | tf_op jit(solution)/shard_map/ktf,kdf->ktd/dot_general | solution.py:216
  109.2 3.1 %collective-permute-start.19 = (bf16[2,288,128]{2,1,0:T(8,128)(2,1)S(1)}, bf16[2,288,128]{2,1,0:T(8,128)(2,1)S(1)}, u32[]{:S(2)}, u32[]{:S(2)}) collective-permute-start(bf16[2,288,128]{2,1,0:T(8,128)(2,1)S(1)} %fusion.50), channel_id=1, source_target_pairs={{0,2},{2,0},{1,3},{3,1},{4,6},{6,4},{5,7},{7,5},{8,10},{10,8},{9,1... | collective-permute-start | bytes 442376 | tf_op jit(solution)/shard_map/ppermute | solution.py:60
  112.5 3.3 %collective-permute-done.19 = bf16[2,288,128]{2,1,0:T(8,128)(2,1)S(1)} collective-permute-done((bf16[2,288,128]{2,1,0:T(8,128)(2,1)S(1)}, bf16[2,288,128]{2,1,0:T(8,128)(2,1)S(1)}, u32[]{:S(2)}, u32[]{:S(2)}) %collective-permute-start.19) | collective-permute-done | bytes 147488 | tf_op jit(solution)/shard_map/ppermute | solution.py:60
  (102 shorter events, 23.2 us)
Async XLA Ops:
  0.0 6.4 %collective-permute-start = (bf16[2,288,128]{2,1,0:T(8,128)(2,1)}, bf16[2,288,128]{2,1,0:T(8,128)(2,1)S(1)}, u32[]{:S(2)}, u32[]{:S(2)}) collective-permute-start(bf16[2,288,128]{2,1,0:T(8,128)(2,1)} %bitcast.125), channel_id=1, source_target_pairs={{0,2},{2,0},{1,3},{3,1},{4,6},{6,4},{5,7},{7,5},{8,10},{10,8},{9,1... | collective-permute-start | bytes 442376 | tf_op jit(solution)/shard_map/ppermute | solution.py:60
  7.4 5.0 %collective-permute-start.1 = (bf16[2,2,1,288,128]{4,3,2,1,0:T(8,128)(2,1)S(1)}, bf16[2,2,1,288,128]{4,3,2,1,0:T(8,128)(2,1)S(1)}, u32[]{:S(2)}, u32[]{:S(2)}) collective-permute-start(bf16[2,2,1,288,128]{4,3,2,1,0:T(8,128)(2,1)S(1)} %pad_maximum_fusion.5), channel_id=1, source_target_pairs={{0,1},{1,0},{2,3},{3,2},{4,5},{5,4},{6,7},{7,6},{8,9},{9,8},{10,11... | collective-permute-start | bytes 884744 | tf_op jit(solution)/shard_map/ppermute | solution.py:60
  12.5 6.9 %copy-start = (bf16[2,2,2,288,128]{4,3,2,1,0:T(8,128)(2,1)}, bf16[2,2,2,288,128]{4,3,2,1,0:T(8,128)(2,1)S(1)}, u32[]{:S(2)}) copy-start(bf16[2,2,2,288,128]{4,3,2,1,0:T(8,128)(2,1)S(1)} %pad_maximum_fusion.3) | copy-start | bytes 1769476
  19.0 1.7 %collective-permute-start.2 = (bf16[2,64,1152]{2,1,0:T(8,128)(2,1)S(1)}, bf16[2,64,1152]{2,1,0:T(8,128)(2,1)S(1)}, u32[]{:S(2)}, u32[]{:S(2)}) collective-permute-start(bf16[2,64,1152]{2,1,0:T(8,128)(2,1)S(1)} %fusion.39), channel_id=1, source_target_pairs={{0,1},{1,0},{2,3},{3,2},{4,5},{5,4},{6,7},{7,6},{8,9},{9,8},{10,11... | collective-permute-start | bytes 884744 | tf_op jit(solution)/shard_map/ppermute | solution.py:60
  20.7 6.7 %collective-permute-start.3 = (bf16[2,32,1152]{2,1,0:T(8,128)(2,1)S(1)}, bf16[2,32,1152]{2,1,0:T(8,128)(2,1)S(1)}, u32[]{:S(2)}, u32[]{:S(2)}) collective-permute-start(bf16[2,32,1152]{2,1,0:T(8,128)(2,1)S(1)} %fusion.49), channel_id=1, source_target_pairs={{0,2},{2,0},{1,3},{3,1},{4,6},{6,4},{5,7},{7,5},{8,10},{10,8},{9,1... | collective-permute-start | bytes 442376 | tf_op jit(solution)/shard_map/ppermute | solution.py:60
  27.7 7.9 %collective-permute-start.4 = (bf16[32,1152]{1,0:T(8,128)(2,1)S(1)}, bf16[32,1152]{1,0:T(8,128)(2,1)S(1)}, u32[]{:S(2)}, u32[]{:S(2)}) collective-permute-start(bf16[32,1152]{1,0:T(8,128)(2,1)S(1)} %get-tuple-element.48), channel_id=1, source_target_pairs={{0,1},{1,0},{2,3},{3,2},{4,5},{5,4},{6,7},{7,6},{8,9},{9,8},{10,11... | collective-permute-start | bytes 221192 | tf_op jit(solution)/shard_map/ppermute | solution.py:60
  30.1 23.3 %all-to-all-start = ((bf16[16,32,1152]{2,1,0:T(8,128)(2,1)}), bf16[16,32,1152]{2,1,0:T(8,128)(2,1)S(1)}, u32[]{:S(2)}, u32[]{:S(2)}) async-start(bf16[16,32,1152]{2,1,0:T(8,128)(2,1)} %broadcast_in_dim.4), calls=%async_computation | async-start | bytes 2359296 | tf_op jit(solution)/shard_map/all_to_all | solution.py:56
  35.6 9.0 %collective-permute-start.6 = (bf16[64,1152]{1,0:T(8,128)(2,1)S(1)}, bf16[64,1152]{1,0:T(8,128)(2,1)S(1)}, u32[]{:S(2)}, u32[]{:S(2)}) collective-permute-start(bf16[64,1152]{1,0:T(8,128)(2,1)S(1)} %pad_maximum_fusion.9), channel_id=1, source_target_pairs={{16,0},{49,1},{24,8},{57,9},{32,16},{1,17},{40,24},{9,25},{48,32},... | collective-permute-start | bytes 442376 | tf_op jit(solution)/shard_map/ppermute | solution.py:52
  38.7 8.6 %collective-permute-start.5 = (bf16[64,1152]{1,0:T(8,128)(2,1)S(1)}, bf16[64,1152]{1,0:T(8,128)(2,1)S(1)}, u32[]{:S(2)}, u32[]{:S(2)}) collective-permute-start(bf16[64,1152]{1,0:T(8,128)(2,1)S(1)} %pad_maximum_fusion.9), channel_id=1, source_target_pairs={{8,0},{57,1},{16,8},{1,9},{24,16},{9,17},{32,24},{17,25},{40,32},{... | collective-permute-start | bytes 442376 | tf_op jit(solution)/shard_map/ppermute | solution.py:52
  44.6 8.7 %collective-permute-start.7 = (bf16[64,1152]{1,0:T(8,128)(2,1)S(1)}, bf16[64,1152]{1,0:T(8,128)(2,1)S(1)}, u32[]{:S(2)}, u32[]{:S(2)}) collective-permute-start(bf16[64,1152]{1,0:T(8,128)(2,1)S(1)} %collective-permute-done.6), channel_id=1, source_target_pairs={{8,0},{57,1},{16,8},{1,9},{24,16},{9,17},{32,24},{17,25},{40,32},{... | collective-permute-start | bytes 442376 | tf_op jit(solution)/shard_map/ppermute | solution.py:52
  46.9 6.5 %collective-permute-start.8 = (bf16[32,1152]{1,0:T(8,128)(2,1)S(1)}, bf16[32,1152]{1,0:T(8,128)(2,1)S(1)}, u32[]{:S(2)}, u32[]{:S(2)}) collective-permute-start(bf16[32,1152]{1,0:T(8,128)(2,1)S(1)} %constant_dynamic-slice_fusion), channel_id=1, source_target_pairs={{16,0},{49,1},{24,8},{57,9},{32,16},{1,17},{40,24},{9,25},{48,32},... | collective-permute-start | bytes 221192 | tf_op jit(solution)/shard_map/ppermute | solution.py:52
  53.4 3.5 %collective-permute-start.9 = (bf16[224,1152]{1,0:T(8,128)(2,1)S(1)}, bf16[224,1152]{1,0:T(8,128)(2,1)S(1)}, u32[]{:S(2)}, u32[]{:S(2)}) collective-permute-start(bf16[224,1152]{1,0:T(8,128)(2,1)S(1)} %pad_maximum_fusion.4), channel_id=1, source_target_pairs={{0,1},{1,0},{2,3},{3,2},{4,5},{5,4},{6,7},{7,6},{8,9},{9,8},{10,11... | collective-permute-start | bytes 1548296 | tf_op jit(solution)/shard_map/ppermute | solution.py:60
  61.5 7.0 %collective-permute-start.10 = (bf16[224,1152]{1,0:T(8,128)(2,1)S(1)}, bf16[224,1152]{1,0:T(8,128)(2,1)}, u32[]{:S(2)}, u32[]{:S(2)}) collective-permute-start(bf16[224,1152]{1,0:T(8,128)(2,1)S(1)} %get-tuple-element.27), channel_id=1, source_target_pairs={{0,1},{1,0},{2,3},{3,2},{4,5},{5,4},{6,7},{7,6},{8,9},{9,8},{10,11... | collective-permute-start | bytes 1548296 | tf_op jit(solution)/shard_map/ppermute | solution.py:60
  61.5 24.6 %all-to-all-start.1 = ((bf16[16,32,1152]{2,1,0:T(8,128)(2,1)}), bf16[16,32,1152]{2,1,0:T(8,128)(2,1)S(1)}, u32[]{:S(2)}, u32[]{:S(2)}) async-start(bf16[16,32,1152]{2,1,0:T(8,128)(2,1)} %bitcast.21), calls=%async_computation.1 | async-start | bytes 2359296 | tf_op jit(solution)/shard_map/all_to_all | solution.py:56
  69.6 5.3 %collective-permute-start.13 = (bf16[32,1152]{1,0:T(8,128)(2,1)S(1)}, bf16[32,1152]{1,0:T(8,128)(2,1)S(1)}, u32[]{:S(2)}, u32[]{:S(2)}) collective-permute-start(bf16[32,1152]{1,0:T(8,128)(2,1)S(1)} %split.22), channel_id=1, source_target_pairs={{48,0},{17,1},{56,8},{25,9},{0,16},{33,17},{8,24},{41,25},{16,32},... | collective-permute-start | bytes 221192 | tf_op jit(solution)/shard_map/ppermute | solution.py:52
  72.9 8.4 %collective-permute-start.11 = (bf16[64,1152]{1,0:T(8,128)(2,1)S(1)}, bf16[64,1152]{1,0:T(8,128)(2,1)S(1)}, u32[]{:S(2)}, u32[]{:S(2)}) collective-permute-start(bf16[64,1152]{1,0:T(8,128)(2,1)S(1)} %get-tuple-element.39), channel_id=1, source_target_pairs={{56,0},{9,1},{0,8},{17,9},{8,16},{25,17},{16,24},{33,25},{24,32},{... | collective-permute-start | bytes 442376 | tf_op jit(solution)/shard_map/ppermute | solution.py:52
  74.1 5.4 %collective-permute-start.12 = (bf16[64,1152]{1,0:T(8,128)(2,1)S(1)}, bf16[64,1152]{1,0:T(8,128)(2,1)S(1)}, u32[]{:S(2)}, u32[]{:S(2)}) collective-permute-start(bf16[64,1152]{1,0:T(8,128)(2,1)S(1)} %get-tuple-element.40), channel_id=1, source_target_pairs={{56,0},{9,1},{0,8},{17,9},{8,16},{25,17},{16,24},{33,25},{24,32},{... | collective-permute-start | bytes 442376 | tf_op jit(solution)/shard_map/ppermute | solution.py:52
  79.5 6.5 %collective-permute-start.14 = (bf16[64,1152]{1,0:T(8,128)(2,1)S(1)}, bf16[64,1152]{1,0:T(8,128)(2,1)S(1)}, u32[]{:S(2)}, u32[]{:S(2)}) collective-permute-start(bf16[64,1152]{1,0:T(8,128)(2,1)S(1)} %fusion.42), channel_id=1, source_target_pairs={{48,0},{17,1},{56,8},{25,9},{0,16},{33,17},{8,24},{41,25},{16,32},... | collective-permute-start | bytes 442376 | tf_op jit(solution)/shard_map/ppermute | solution.py:52
  86.1 3.8 %collective-permute-start.15 = (bf16[32,1152]{1,0:T(8,128)(2,1)S(1)}, bf16[32,1152]{1,0:T(8,128)(2,1)S(1)}, u32[]{:S(2)}, u32[]{:S(2)}) collective-permute-start(bf16[32,1152]{1,0:T(8,128)(2,1)S(1)} %fusion.52), channel_id=1, source_target_pairs={{0,1},{1,0},{2,3},{3,2},{4,5},{5,4},{6,7},{7,6},{8,9},{9,8},{10,11... | collective-permute-start | bytes 221192 | tf_op jit(solution)/shard_map/ppermute | solution.py:60
  90.1 9.7 %copy-start.7 = (f32[2,128,1076]{1,2,0:T(8,128)S(1)}, f32[2,128,1076]{1,2,0:T(8,128)}, u32[]{:S(2)}) copy-start(f32[2,128,1076]{1,2,0:T(8,128)} %copy-done.6) | copy-start | bytes 3305476
  90.1 7.1 %collective-permute-start.16 = (bf16[2,32,1152]{2,1,0:T(8,128)(2,1)S(1)}, bf16[2,32,1152]{2,1,0:T(8,128)(2,1)S(1)}, u32[]{:S(2)}, u32[]{:S(2)}) collective-permute-start(bf16[2,32,1152]{2,1,0:T(8,128)(2,1)S(1)} %fusion.18), channel_id=1, source_target_pairs={{0,2},{2,0},{1,3},{3,1},{4,6},{6,4},{5,7},{7,5},{8,10},{10,8},{9,1... | collective-permute-start | bytes 442376 | tf_op jit(solution)/shard_map/ppermute | solution.py:60
  97.3 2.5 %collective-permute-start.17 = (bf16[2,64,1152]{2,1,0:T(8,128)(2,1)S(1)}, bf16[2,64,1152]{2,1,0:T(8,128)(2,1)S(1)}, u32[]{:S(2)}, u32[]{:S(2)}) collective-permute-start(bf16[2,64,1152]{2,1,0:T(8,128)(2,1)S(1)} %pad_maximum_fusion.7), channel_id=1, source_target_pairs={{0,1},{1,0},{2,3},{3,2},{4,5},{5,4},{6,7},{7,6},{8,9},{9,8},{10,11... | collective-permute-start | bytes 884744 | tf_op jit(solution)/shard_map/ppermute | solution.py:60
  107.4 1.7 %collective-permute-start.18 = (bf16[2,2,288,128]{3,2,1,0:T(8,128)(2,1)S(1)}, bf16[2,2,288,128]{3,2,1,0:T(8,128)(2,1)S(1)}, u32[]{:S(2)}, u32[]{:S(2)}) collective-permute-start(bf16[2,2,288,128]{3,2,1,0:T(8,128)(2,1)S(1)} %fusion.40), channel_id=1, source_target_pairs={{0,1},{1,0},{2,3},{3,2},{4,5},{5,4},{6,7},{7,6},{8,9},{9,8},{10,11... | collective-permute-start | bytes 884744 | tf_op jit(solution)/shard_map/ppermute | solution.py:60
  109.2 6.7 %collective-permute-start.19 = (bf16[2,288,128]{2,1,0:T(8,128)(2,1)S(1)}, bf16[2,288,128]{2,1,0:T(8,128)(2,1)S(1)}, u32[]{:S(2)}, u32[]{:S(2)}) collective-permute-start(bf16[2,288,128]{2,1,0:T(8,128)(2,1)S(1)} %fusion.50), channel_id=1, source_target_pairs={{0,2},{2,0},{1,3},{3,1},{4,6},{6,4},{5,7},{7,5},{8,10},{10,8},{9,1... | collective-permute-start | bytes 442376 | tf_op jit(solution)/shard_map/ppermute | solution.py:60
  (10 other events, 27.6 us)

commit v2 on v1

--- a/solution.py
+++ b/solution.py
@@ -108,33 +108,23 @@
     return swap_sum(own.reshape(2, half, -1), "c", 0), texts
 
 
-def loss_kernel(
-    part_rows, scalars, first, images, texts, chip, fetched, other, text_part, image_sum
-):
-    tile = 256
-    for start in range(0, texts.shape[0], tile):
-        block = texts[pl.ds(start, tile), :]
-        scores = lax.dot_general(
-            images[...], block, (((1,), (1,)), ((), ())), preferred_element_type=F32
-        )
-        logits = scalars[0] * scores + scalars[1]
-        at_image = lax.broadcasted_iota(jnp.int32, scores.shape, 0) - first[0]
-        at_text = lax.broadcasted_iota(jnp.int32, scores.shape, 1) + (start - first[1])
-        diagonal = (at_image == at_text) & (at_image >= 0) & (at_image < part_rows)
-        diagonal = diagonal.astype(F32)
-        weights = (scalars[2] * (jax.nn.sigmoid(logits) - diagonal)).astype(BF)
-        text_part[pl.ds(start, tile), :] = lax.dot_general(
-            weights, images[...], (((0,), (0,)), ((), ())), preferred_element_type=F32
-        ).astype(BF)
-        product = jnp.dot(weights, block, preferred_element_type=F32)
-        if start == 0:
-            image_sum[...] = product
-        else:
-            image_sum[...] += product
+def loss_kernel(part_rows, scalars, first, images, texts, chip, fetched, other, text_part):
+    scores = lax.dot_general(
+        images[...], texts[...], (((1,), (1,)), ((), ())), preferred_element_type=F32
+    )
+    logits = scalars[0] * scores + scalars[1]
+    at_image = lax.broadcasted_iota(jnp.int32, scores.shape, 0) - first[0]
+    at_text = lax.broadcasted_iota(jnp.int32, scores.shape, 1) - first[1]
+    diagonal = (at_image == at_text) & (at_image >= 0) & (at_image < part_rows)
+    weights = (scalars[2] * (jax.nn.sigmoid(logits) - diagonal.astype(F32))).astype(BF)
+    text_part[...] = lax.dot_general(
+        weights, images[...], (((0,), (0,)), ((), ())), preferred_element_type=F32
+    ).astype(BF)
+    image_part = jnp.dot(weights, texts[...], preferred_element_type=F32)
     at_fetched, at_other = chip.shape[0], chip.shape[0] + fetched.shape[0]
-    chip[...] = image_sum[:at_fetched, :]
-    fetched[...] = image_sum[at_fetched:at_other, :]
-    other[...] = image_sum[at_other:, :].astype(BF)
+    chip[...] = image_part[:at_fetched, :]
+    fetched[...] = image_part[at_fetched:at_other, :]
+    other[...] = image_part[at_other:, :].astype(BF)
 
 
 def loss_block(scalars, first, images, texts, part_rows):
@@ -152,7 +142,6 @@
             jax.ShapeDtypeStruct((fetched, dim), BF),
             jax.ShapeDtypeStruct(texts.shape, BF),
         ],
-        scratch_shapes=[pltpu.VMEM((rows, dim), F32)],
         compiler_params=pltpu.CompilerParams(vmem_limit_bytes=20 * 1024 * 1024),
         cost_estimate=pl.CostEstimate(
             flops=6 * rows * texts.shape[0] * dim,
@@ -172,7 +161,10 @@
 
     own = jnp.swapaxes(pooled, 1, 2)
     far = swap(own, "xh")
-    whole = in_order(own[:, None, None], far[:, None, None], "xh", 1)
+    none = jnp.zeros_like(own)
+    mine = in_order(own[:, None, None], none[:, None, None], "xh", 1)
+    far, mine = lax.optimization_barrier((far, mine))
+    whole = mine + in_order(none[:, None, None], far[:, None, None], "xh", 1)
     whole = swap_join(whole, "c", 2).reshape(2, 4 * width, rows)
     whole, ln_gain, ln_bias, fc1_bias, fc2_bias = lax.optimization_barrier(
         (whole, ln_gain, ln_bias, fc1_bias, fc2_bias)

time: 117 us -> 115 us (0.983)
  transfers between devices with their start and end apart: 22 -> 22, of which waited for: 15 -> 15; matrix products, arithmetic and copies ran while one was open for 3% -> 4% of each run, Pallas kernels for 0% -> 0%
where the time goes in v2:
time: 115 us
  starting transfers between devices  48.7 us (42%)
  waiting for transfers between devices  39.3 us (34%)
  matrix products  12.8 us (11%)
  other arithmetic  5.24 us (5%)
  Pallas kernels  3.92 us (3%)
  local copies, waits for them, and re-layouts  2.57 us (2%)
  between operations  2.43 us (2%)
    ppermute x12, starting transfers between devices, swap(): return as_lies(lax.ppermute(as_lies(block), axis, [(0, 1), (1, 0)]))  22.8 us
    ppermute x8, waiting for transfers between devices, hop(): return as_lies(lax.ppermute(as_lies(block), ('z', 'c'), pairs))  20.5 us
    ppermute x12, waiting for transfers between devices, swap(): return as_lies(lax.ppermute(as_lies(block), axis, [(0, 1), (1, 0)]))  18.8 us
    ppermute x8, starting transfers between devices, hop(): return as_lies(lax.ppermute(as_lies(block), ('z', 'c'), pairs))  13.5 us
    all_to_all x2, starting transfers between devices, exchange(): return lax.all_to_all(parts, axes, 0, 0, tiled=True)  12.4 us
    dot_general x1, matrix products, on_device(): jnp.einsum('kte,kfe->ktf', block_low, fc2, preferred_element_type=F32)  4.63 us
    dot_general x1, matrix products, on_device(): preact = jnp.einsum('ktd,kdf->ktf', normed, fc1, preferred_element_type=F32)  4.45 us
    pallas_call x1, Pallas kernels, loss_block(): pl.pallas_call(functools.partial(loss_kernel, part_rows), in_specs=[small...  3.92 us
  transfers between devices with their start and end apart: 22, of which 15 were waited for; matrix products, arithmetic and copies ran while one was open for 4% of the time, Pallas kernels for 0%

profile of v2, /device:TPU:1, one launch (start us, length us, event | category | flops | bytes accessed | tf_op | source)
XLA Modules:
  0.0 114.9 jit_solution(953276029529424326)
XLA Ops:
  0.0 3.6 %collective-permute-start = (bf16[2,288,128]{2,1,0:T(8,128)(2,1)}, bf16[2,288,128]{2,1,0:T(8,128)(2,1)S(1)}, u32[]{:S(2)}, u32[]{:S(2)}) collective-permute-start(bf16[2,288,128]{2,1,0:T(8,128)(2,1)} %bitcast.129), channel_id=1, source_target_pairs={{0,2},{2,0},{1,3},{3,1},{4,6},{6,4},{5,7},{7,5},{8,10},{10,8},{9,1... | collective-permute-start | bytes 442376 | tf_op jit(solution)/shard_map/ppermute | solution.py:60
  4.6 1.8 %collective-permute-done = bf16[2,288,128]{2,1,0:T(8,128)(2,1)S(1)} collective-permute-done((bf16[2,288,128]{2,1,0:T(8,128)(2,1)}, bf16[2,288,128]{2,1,0:T(8,128)(2,1)S(1)}, u32[]{:S(2)}, u32[]{:S(2)}) %collective-permute-start) | collective-permute-done | bytes 147488 | tf_op jit(solution)/shard_map/ppermute | solution.py:60
  6.5 3.8 %collective-permute-start.1 = (bf16[2,2,1,288,128]{4,3,2,1,0:T(8,128)(2,1)S(1)}, bf16[2,2,1,288,128]{4,3,2,1,0:T(8,128)(2,1)S(1)}, u32[]{:S(2)}, u32[]{:S(2)}) collective-permute-start(bf16[2,2,1,288,128]{4,3,2,1,0:T(8,128)(2,1)S(1)} %maximum_add_fusion), channel_id=1, source_target_pairs={{0,1},{1,0},{2,3},{3,2},{4,5},{5,4},{6,7},{7,6},{8,9},{9,8},{10,11... | collective-permute-start | bytes 884744 | tf_op jit(solution)/shard_map/ppermute | solution.py:60
  12.3 4.4 %fusion.9 = f32[2,128,1076]{1,2,0:T(8,128)S(1)} fusion(bf16[2,1152,1076]{1,0,2:T(2,128)(2,1)} %param.13, bf16[2,1152,128]{2,1,0:T(8,128)(2,1)S(1)} %bitcast.116, f32[2,1152]{1,0:T(2,128)S(1)} %convert_element_type.115, f32[2,1152]{1,0:T(2,128)S(1)} %convert_element_type.114, f32[2,128]{1,0:T(2,128)S(1)} %add_rsqrt_fusion, ...), kind=kOutput, calls=%fused_computation.9 | convolution fusion | flops 636695552 | bytes 6678944 | tf_op jit(solution)/shard_map/ktd,kdf->ktf/dot_general | solution.py:177
  22.1 4.4 %collective-permute-done.3 = bf16[2,32,1152]{2,1,0:T(8,128)(2,1)S(1)} collective-permute-done((bf16[2,32,1152]{2,1,0:T(8,128)(2,1)S(1)}, bf16[2,32,1152]{2,1,0:T(8,128)(2,1)S(1)}, u32[]{:S(2)}, u32[]{:S(2)}) %collective-permute-start.3) | collective-permute-done | bytes 147488 | tf_op jit(solution)/shard_map/ppermute | solution.py:60
  29.2 5.5 %all-to-all-start = ((bf16[16,32,1152]{2,1,0:T(8,128)(2,1)}), bf16[16,32,1152]{2,1,0:T(8,128)(2,1)S(1)}, u32[]{:S(2)}, u32[]{:S(2)}) async-start(bf16[16,32,1152]{2,1,0:T(8,128)(2,1)} %broadcast_in_dim.4), calls=%async_computation | async-start | bytes 2359296 | tf_op jit(solution)/shard_map/all_to_all | solution.py:56
  34.7 3.1 %collective-permute-start.6 = (bf16[64,1152]{1,0:T(8,128)(2,1)S(1)}, bf16[64,1152]{1,0:T(8,128)(2,1)S(1)}, u32[]{:S(2)}, u32[]{:S(2)}) collective-permute-start(bf16[64,1152]{1,0:T(8,128)(2,1)S(1)} %pad_maximum_fusion.9), channel_id=1, source_target_pairs={{16,0},{49,1},{24,8},{57,9},{32,16},{1,17},{40,24},{9,25},{48,32},... | collective-permute-start | bytes 442376 | tf_op jit(solution)/shard_map/ppermute | solution.py:52
  37.8 1.6 %collective-permute-start.5 = (bf16[64,1152]{1,0:T(8,128)(2,1)S(1)}, bf16[64,1152]{1,0:T(8,128)(2,1)S(1)}, u32[]{:S(2)}, u32[]{:S(2)}) collective-permute-start(bf16[64,1152]{1,0:T(8,128)(2,1)S(1)} %pad_maximum_fusion.9), channel_id=1, source_target_pairs={{8,0},{57,1},{16,8},{1,9},{24,16},{9,17},{32,24},{17,25},{40,32},{... | collective-permute-start | bytes 442376 | tf_op jit(solution)/shard_map/ppermute | solution.py:52
  39.4 4.3 %collective-permute-done.6 = bf16[64,1152]{1,0:T(8,128)(2,1)S(1)} collective-permute-done((bf16[64,1152]{1,0:T(8,128)(2,1)S(1)}, bf16[64,1152]{1,0:T(8,128)(2,1)S(1)}, u32[]{:S(2)}, u32[]{:S(2)}) %collective-permute-start.6) | collective-permute-done | bytes 147488 | tf_op jit(solution)/shard_map/ppermute | solution.py:52
  43.7 2.3 %collective-permute-start.7 = (bf16[64,1152]{1,0:T(8,128)(2,1)S(1)}, bf16[64,1152]{1,0:T(8,128)(2,1)S(1)}, u32[]{:S(2)}, u32[]{:S(2)}) collective-permute-start(bf16[64,1152]{1,0:T(8,128)(2,1)S(1)} %collective-permute-done.6), channel_id=1, source_target_pairs={{8,0},{57,1},{16,8},{1,9},{24,16},{9,17},{32,24},{17,25},{40,32},{... | collective-permute-start | bytes 442376 | tf_op jit(solution)/shard_map/ppermute | solution.py:52
  46.4 6.1 %collective-permute-done.8 = bf16[32,1152]{1,0:T(8,128)(2,1)S(1)} collective-permute-done((bf16[32,1152]{1,0:T(8,128)(2,1)S(1)}, bf16[32,1152]{1,0:T(8,128)(2,1)S(1)}, u32[]{:S(2)}, u32[]{:S(2)}) %collective-permute-start.8) | collective-permute-done | bytes 73760 | tf_op jit(solution)/shard_map/ppermute | solution.py:52
  56.1 3.9 %shard_map.100 = (f32[64,1152]{1,0:T(8,128)S(1)}, f32[224,1152]{1,0:T(8,128)S(1)}, bf16[224,1152]{1,0:T(8,128)(2,1)S(1)}, bf16[512,1152]{1,0:T(8,128)(2,1)}) custom-call(f32[3]{0:T(128)S(1)} %pad_maximum_fusion.10.scalars, s32[2]{0:T(128)S(1)} %add_multiply_fusion.first, bf16[512,1152]{1,0:T(8,128)(2,1)S(1)} %pad_maximum_fusion.images, ...), custom_call_target="tpu_custom_call" | custom-call | flops 1811939328 | bytes 5898240 | tf_op jit(solution)/shard_map/pallas_call | solution.py:135
  60.0 6.9 %all-to-all-start.1 = ((bf16[16,32,1152]{2,1,0:T(8,128)(2,1)}), bf16[16,32,1152]{2,1,0:T(8,128)(2,1)S(1)}, u32[]{:S(2)}, u32[]{:S(2)}) async-start(bf16[16,32,1152]{2,1,0:T(8,128)(2,1)} %bitcast.23), calls=%async_computation.1 | async-start | bytes 2359296 | tf_op jit(solution)/shard_map/all_to_all | solution.py:56
  68.2 3.3 %collective-permute-start.13 = (bf16[32,1152]{1,0:T(8,128)(2,1)S(1)}, bf16[32,1152]{1,0:T(8,128)(2,1)S(1)}, u32[]{:S(2)}, u32[]{:S(2)}) collective-permute-start(bf16[32,1152]{1,0:T(8,128)(2,1)S(1)} %split.22), channel_id=1, source_target_pairs={{48,0},{17,1},{56,8},{25,9},{0,16},{33,17},{8,24},{41,25},{16,32},... | collective-permute-start | bytes 221192 | tf_op jit(solution)/shard_map/ppermute | solution.py:52
  73.5 4.6 %collective-permute-done.12 = bf16[64,1152]{1,0:T(8,128)(2,1)S(1)} collective-permute-done((bf16[64,1152]{1,0:T(8,128)(2,1)S(1)}, bf16[64,1152]{1,0:T(8,128)(2,1)S(1)}, u32[]{:S(2)}, u32[]{:S(2)}) %collective-permute-start.12) | collective-permute-done | bytes 147488 | tf_op jit(solution)/shard_map/ppermute | solution.py:52
  78.1 1.7 %collective-permute-start.14 = (bf16[64,1152]{1,0:T(8,128)(2,1)S(1)}, bf16[64,1152]{1,0:T(8,128)(2,1)S(1)}, u32[]{:S(2)}, u32[]{:S(2)}) collective-permute-start(bf16[64,1152]{1,0:T(8,128)(2,1)S(1)} %fusion.42), channel_id=1, source_target_pairs={{48,0},{17,1},{56,8},{25,9},{0,16},{33,17},{8,24},{41,25},{16,32},... | collective-permute-start | bytes 442376 | tf_op jit(solution)/shard_map/ppermute | solution.py:52
  79.8 4.8 %collective-permute-done.14 = bf16[64,1152]{1,0:T(8,128)(2,1)S(1)} collective-permute-done((bf16[64,1152]{1,0:T(8,128)(2,1)S(1)}, bf16[64,1152]{1,0:T(8,128)(2,1)S(1)}, u32[]{:S(2)}, u32[]{:S(2)}) %collective-permute-start.14) | collective-permute-done | bytes 147488 | tf_op jit(solution)/shard_map/ppermute | solution.py:52
  84.7 2.9 %collective-permute-start.15 = (bf16[32,1152]{1,0:T(8,128)(2,1)S(1)}, bf16[32,1152]{1,0:T(8,128)(2,1)S(1)}, u32[]{:S(2)}, u32[]{:S(2)}) collective-permute-start(bf16[32,1152]{1,0:T(8,128)(2,1)S(1)} %fusion.52), channel_id=1, source_target_pairs={{0,1},{1,0},{2,3},{3,2},{4,5},{5,4},{6,7},{7,6},{8,9},{9,8},{10,11... | collective-permute-start | bytes 221192 | tf_op jit(solution)/shard_map/ppermute | solution.py:60
  88.7 3.2 %collective-permute-start.16 = (bf16[2,32,1152]{2,1,0:T(8,128)(2,1)S(1)}, bf16[2,32,1152]{2,1,0:T(8,128)(2,1)S(1)}, u32[]{:S(2)}, u32[]{:S(2)}) collective-permute-start(bf16[2,32,1152]{2,1,0:T(8,128)(2,1)S(1)} %fusion.18), channel_id=1, source_target_pairs={{0,2},{2,0},{1,3},{3,1},{4,6},{6,4},{5,7},{7,5},{8,10},{10,8},{9,1... | collective-permute-start | bytes 442376 | tf_op jit(solution)/shard_map/ppermute | solution.py:60
  91.9 3.8 %collective-permute-done.16 = bf16[2,32,1152]{2,1,0:T(8,128)(2,1)S(1)} collective-permute-done((bf16[2,32,1152]{2,1,0:T(8,128)(2,1)S(1)}, bf16[2,32,1152]{2,1,0:T(8,128)(2,1)S(1)}, u32[]{:S(2)}, u32[]{:S(2)}) %collective-permute-start.16) | collective-permute-done | bytes 147488 | tf_op jit(solution)/shard_map/ppermute | solution.py:60
  98.3 4.6 %fusion.27 = bf16[2,128,1076]{1,2,0:T(8,128)(2,1)S(1)} fusion(f32[2,128,1076]{1,2,0:T(8,128)S(1)} %copy-done.7, bf16[2,1076,1152]{2,0,1:T(2,128)(2,1)} %param.15, bf16[2,64,1152]{2,1,0:T(8,128)(2,1)S(1)} %get-tuple-element.40, bf16[2,64,1152]{2,1,0:T(8,128)(2,1)S(1)} %get-tuple-element.39), kind=kOutput, calls=%fused_computation.34 | convolution fusion | flops 641339392 | bytes 7200768 | tf_op jit(solution)/shard_map/kte,kfe->ktf/dot_general | solution.py:205
  102.9 2.4 %fusion.59 = (f32[2,128]{1,0:T(2,128)S(1)}, f32[2,128]{1,0:T(2,128)S(1)}, f32[2,128,1152]{1,2,0:T(8,128)S(1)}) fusion(f32[2,128]{1,0:T(2,128)S(1)} %add_rsqrt_fusion, f32[2,128]{1,0:T(2,128)S(1)} %broadcast_multiply_fusion.2, bf16[2,1152,128]{2,1,0:T(8,128)(2,1)S(1)} %bitcast.118, f32[2,1152]{1,0:T(2,128)S(1)} %convert_element_type.114, ...), kind=kOutput, calls=%fused_computation.115 | convolution fusion | flops 636714496 | bytes 7291904 | tf_op jit(solution)/shard_map/ktf,kdf->ktd/dot_general | solution.py:208
  107.5 3.1 %collective-permute-start.19 = (bf16[2,288,128]{2,1,0:T(8,128)(2,1)S(1)}, bf16[2,288,128]{2,1,0:T(8,128)(2,1)S(1)}, u32[]{:S(2)}, u32[]{:S(2)}) collective-permute-start(bf16[2,288,128]{2,1,0:T(8,128)(2,1)S(1)} %fusion.50), channel_id=1, source_target_pairs={{0,2},{2,0},{1,3},{3,1},{4,6},{6,4},{5,7},{7,5},{8,10},{10,8},{9,1... | collective-permute-start | bytes 442376 | tf_op jit(solution)/shard_map/ppermute | solution.py:60
  110.9 3.3 %collective-permute-done.19 = bf16[2,288,128]{2,1,0:T(8,128)(2,1)S(1)} collective-permute-done((bf16[2,288,128]{2,1,0:T(8,128)(2,1)S(1)}, bf16[2,288,128]{2,1,0:T(8,128)(2,1)S(1)}, u32[]{:S(2)}, u32[]{:S(2)}) %collective-permute-start.19) | collective-permute-done | bytes 147488 | tf_op jit(solution)/shard_map/ppermute | solution.py:60
  (104 shorter events, 23.0 us)
Async XLA Ops:
  0.0 6.4 %collective-permute-start = (bf16[2,288,128]{2,1,0:T(8,128)(2,1)}, bf16[2,288,128]{2,1,0:T(8,128)(2,1)S(1)}, u32[]{:S(2)}, u32[]{:S(2)}) collective-permute-start(bf16[2,288,128]{2,1,0:T(8,128)(2,1)} %bitcast.129), channel_id=1, source_target_pairs={{0,2},{2,0},{1,3},{3,1},{4,6},{6,4},{5,7},{7,5},{8,10},{10,8},{9,1... | collective-permute-start | bytes 442376 | tf_op jit(solution)/shard_map/ppermute | solution.py:60
  6.5 5.0 %collective-permute-start.1 = (bf16[2,2,1,288,128]{4,3,2,1,0:T(8,128)(2,1)S(1)}, bf16[2,2,1,288,128]{4,3,2,1,0:T(8,128)(2,1)S(1)}, u32[]{:S(2)}, u32[]{:S(2)}) collective-permute-start(bf16[2,2,1,288,128]{4,3,2,1,0:T(8,128)(2,1)S(1)} %maximum_add_fusion), channel_id=1, source_target_pairs={{0,1},{1,0},{2,3},{3,2},{4,5},{5,4},{6,7},{7,6},{8,9},{9,8},{10,11... | collective-permute-start | bytes 884744 | tf_op jit(solution)/shard_map/ppermute | solution.py:60
  11.6 6.9 %copy-start = (bf16[2,2,2,288,128]{4,3,2,1,0:T(8,128)(2,1)}, bf16[2,2,2,288,128]{4,3,2,1,0:T(8,128)(2,1)S(1)}, u32[]{:S(2)}) copy-start(bf16[2,2,2,288,128]{4,3,2,1,0:T(8,128)(2,1)S(1)} %pad_maximum_fusion.3) | copy-start | bytes 1769476
  18.1 1.7 %collective-permute-start.2 = (bf16[2,64,1152]{2,1,0:T(8,128)(2,1)S(1)}, bf16[2,64,1152]{2,1,0:T(8,128)(2,1)S(1)}, u32[]{:S(2)}, u32[]{:S(2)}) collective-permute-start(bf16[2,64,1152]{2,1,0:T(8,128)(2,1)S(1)} %fusion.39), channel_id=1, source_target_pairs={{0,1},{1,0},{2,3},{3,2},{4,5},{5,4},{6,7},{7,6},{8,9},{9,8},{10,11... | collective-permute-start | bytes 884744 | tf_op jit(solution)/shard_map/ppermute | solution.py:60
  19.9 6.7 %collective-permute-start.3 = (bf16[2,32,1152]{2,1,0:T(8,128)(2,1)S(1)}, bf16[2,32,1152]{2,1,0:T(8,128)(2,1)S(1)}, u32[]{:S(2)}, u32[]{:S(2)}) collective-permute-start(bf16[2,32,1152]{2,1,0:T(8,128)(2,1)S(1)} %fusion.49), channel_id=1, source_target_pairs={{0,2},{2,0},{1,3},{3,1},{4,6},{6,4},{5,7},{7,5},{8,10},{10,8},{9,1... | collective-permute-start | bytes 442376 | tf_op jit(solution)/shard_map/ppermute | solution.py:60
  26.8 7.9 %collective-permute-start.4 = (bf16[32,1152]{1,0:T(8,128)(2,1)S(1)}, bf16[32,1152]{1,0:T(8,128)(2,1)S(1)}, u32[]{:S(2)}, u32[]{:S(2)}) collective-permute-start(bf16[32,1152]{1,0:T(8,128)(2,1)S(1)} %get-tuple-element.50), channel_id=1, source_target_pairs={{0,1},{1,0},{2,3},{3,2},{4,5},{5,4},{6,7},{7,6},{8,9},{9,8},{10,11... | collective-permute-start | bytes 221192 | tf_op jit(solution)/shard_map/ppermute | solution.py:60
  29.2 23.3 %all-to-all-start = ((bf16[16,32,1152]{2,1,0:T(8,128)(2,1)}), bf16[16,32,1152]{2,1,0:T(8,128)(2,1)S(1)}, u32[]{:S(2)}, u32[]{:S(2)}) async-start(bf16[16,32,1152]{2,1,0:T(8,128)(2,1)} %broadcast_in_dim.4), calls=%async_computation | async-start | bytes 2359296 | tf_op jit(solution)/shard_map/all_to_all | solution.py:56
  34.7 9.0 %collective-permute-start.6 = (bf16[64,1152]{1,0:T(8,128)(2,1)S(1)}, bf16[64,1152]{1,0:T(8,128)(2,1)S(1)}, u32[]{:S(2)}, u32[]{:S(2)}) collective-permute-start(bf16[64,1152]{1,0:T(8,128)(2,1)S(1)} %pad_maximum_fusion.9), channel_id=1, source_target_pairs={{16,0},{49,1},{24,8},{57,9},{32,16},{1,17},{40,24},{9,25},{48,32},... | collective-permute-start | bytes 442376 | tf_op jit(solution)/shard_map/ppermute | solution.py:52
  37.8 8.6 %collective-permute-start.5 = (bf16[64,1152]{1,0:T(8,128)(2,1)S(1)}, bf16[64,1152]{1,0:T(8,128)(2,1)S(1)}, u32[]{:S(2)}, u32[]{:S(2)}) collective-permute-start(bf16[64,1152]{1,0:T(8,128)(2,1)S(1)} %pad_maximum_fusion.9), channel_id=1, source_target_pairs={{8,0},{57,1},{16,8},{1,9},{24,16},{9,17},{32,24},{17,25},{40,32},{... | collective-permute-start | bytes 442376 | tf_op jit(solution)/shard_map/ppermute | solution.py:52
  43.7 8.7 %collective-permute-start.7 = (bf16[64,1152]{1,0:T(8,128)(2,1)S(1)}, bf16[64,1152]{1,0:T(8,128)(2,1)S(1)}, u32[]{:S(2)}, u32[]{:S(2)}) collective-permute-start(bf16[64,1152]{1,0:T(8,128)(2,1)S(1)} %collective-permute-done.6), channel_id=1, source_target_pairs={{8,0},{57,1},{16,8},{1,9},{24,16},{9,17},{32,24},{17,25},{40,32},{... | collective-permute-start | bytes 442376 | tf_op jit(solution)/shard_map/ppermute | solution.py:52
  46.0 6.5 %collective-permute-start.8 = (bf16[32,1152]{1,0:T(8,128)(2,1)S(1)}, bf16[32,1152]{1,0:T(8,128)(2,1)S(1)}, u32[]{:S(2)}, u32[]{:S(2)}) collective-permute-start(bf16[32,1152]{1,0:T(8,128)(2,1)S(1)} %constant_dynamic-slice_fusion), channel_id=1, source_target_pairs={{16,0},{49,1},{24,8},{57,9},{32,16},{1,17},{40,24},{9,25},{48,32},... | collective-permute-start | bytes 221192 | tf_op jit(solution)/shard_map/ppermute | solution.py:52
  52.5 3.5 %collective-permute-start.9 = (bf16[224,1152]{1,0:T(8,128)(2,1)S(1)}, bf16[224,1152]{1,0:T(8,128)(2,1)S(1)}, u32[]{:S(2)}, u32[]{:S(2)}) collective-permute-start(bf16[224,1152]{1,0:T(8,128)(2,1)S(1)} %pad_maximum_fusion.4), channel_id=1, source_target_pairs={{0,1},{1,0},{2,3},{3,2},{4,5},{5,4},{6,7},{7,6},{8,9},{9,8},{10,11... | collective-permute-start | bytes 1548296 | tf_op jit(solution)/shard_map/ppermute | solution.py:60
  60.0 7.0 %collective-permute-start.10 = (bf16[224,1152]{1,0:T(8,128)(2,1)S(1)}, bf16[224,1152]{1,0:T(8,128)(2,1)}, u32[]{:S(2)}, u32[]{:S(2)}) collective-permute-start(bf16[224,1152]{1,0:T(8,128)(2,1)S(1)} %get-tuple-element.31), channel_id=1, source_target_pairs={{0,1},{1,0},{2,3},{3,2},{4,5},{5,4},{6,7},{7,6},{8,9},{9,8},{10,11... | collective-permute-start | bytes 1548296 | tf_op jit(solution)/shard_map/ppermute | solution.py:60
  60.0 24.7 %all-to-all-start.1 = ((bf16[16,32,1152]{2,1,0:T(8,128)(2,1)}), bf16[16,32,1152]{2,1,0:T(8,128)(2,1)S(1)}, u32[]{:S(2)}, u32[]{:S(2)}) async-start(bf16[16,32,1152]{2,1,0:T(8,128)(2,1)} %bitcast.23), calls=%async_computation.1 | async-start | bytes 2359296 | tf_op jit(solution)/shard_map/all_to_all | solution.py:56
  68.2 5.3 %collective-permute-start.13 = (bf16[32,1152]{1,0:T(8,128)(2,1)S(1)}, bf16[32,1152]{1,0:T(8,128)(2,1)S(1)}, u32[]{:S(2)}, u32[]{:S(2)}) collective-permute-start(bf16[32,1152]{1,0:T(8,128)(2,1)S(1)} %split.22), channel_id=1, source_target_pairs={{48,0},{17,1},{56,8},{25,9},{0,16},{33,17},{8,24},{41,25},{16,32},... | collective-permute-start | bytes 221192 | tf_op jit(solution)/shard_map/ppermute | solution.py:52
  71.5 8.4 %collective-permute-start.11 = (bf16[64,1152]{1,0:T(8,128)(2,1)S(1)}, bf16[64,1152]{1,0:T(8,128)(2,1)S(1)}, u32[]{:S(2)}, u32[]{:S(2)}) collective-permute-start(bf16[64,1152]{1,0:T(8,128)(2,1)S(1)} %get-tuple-element.43), channel_id=1, source_target_pairs={{56,0},{9,1},{0,8},{17,9},{8,16},{25,17},{16,24},{33,25},{24,32},{... | collective-permute-start | bytes 442376 | tf_op jit(solution)/shard_map/ppermute | solution.py:52
  72.6 5.4 %collective-permute-start.12 = (bf16[64,1152]{1,0:T(8,128)(2,1)S(1)}, bf16[64,1152]{1,0:T(8,128)(2,1)S(1)}, u32[]{:S(2)}, u32[]{:S(2)}) collective-permute-start(bf16[64,1152]{1,0:T(8,128)(2,1)S(1)} %get-tuple-element.44), channel_id=1, source_target_pairs={{56,0},{9,1},{0,8},{17,9},{8,16},{25,17},{16,24},{33,25},{24,32},{... | collective-permute-start | bytes 442376 | tf_op jit(solution)/shard_map/ppermute | solution.py:52
  78.1 6.5 %collective-permute-start.14 = (bf16[64,1152]{1,0:T(8,128)(2,1)S(1)}, bf16[64,1152]{1,0:T(8,128)(2,1)S(1)}, u32[]{:S(2)}, u32[]{:S(2)}) collective-permute-start(bf16[64,1152]{1,0:T(8,128)(2,1)S(1)} %fusion.42), channel_id=1, source_target_pairs={{48,0},{17,1},{56,8},{25,9},{0,16},{33,17},{8,24},{41,25},{16,32},... | collective-permute-start | bytes 442376 | tf_op jit(solution)/shard_map/ppermute | solution.py:52
  84.7 3.8 %collective-permute-start.15 = (bf16[32,1152]{1,0:T(8,128)(2,1)S(1)}, bf16[32,1152]{1,0:T(8,128)(2,1)S(1)}, u32[]{:S(2)}, u32[]{:S(2)}) collective-permute-start(bf16[32,1152]{1,0:T(8,128)(2,1)S(1)} %fusion.52), channel_id=1, source_target_pairs={{0,1},{1,0},{2,3},{3,2},{4,5},{5,4},{6,7},{7,6},{8,9},{9,8},{10,11... | collective-permute-start | bytes 221192 | tf_op jit(solution)/shard_map/ppermute | solution.py:60
  88.7 9.5 %copy-start.7 = (f32[2,128,1076]{1,2,0:T(8,128)S(1)}, f32[2,128,1076]{1,2,0:T(8,128)}, u32[]{:S(2)}) copy-start(f32[2,128,1076]{1,2,0:T(8,128)} %copy-done.6) | copy-start | bytes 3305476
  88.7 7.1 %collective-permute-start.16 = (bf16[2,32,1152]{2,1,0:T(8,128)(2,1)S(1)}, bf16[2,32,1152]{2,1,0:T(8,128)(2,1)S(1)}, u32[]{:S(2)}, u32[]{:S(2)}) collective-permute-start(bf16[2,32,1152]{2,1,0:T(8,128)(2,1)S(1)} %fusion.18), channel_id=1, source_target_pairs={{0,2},{2,0},{1,3},{3,1},{4,6},{6,4},{5,7},{7,5},{8,10},{10,8},{9,1... | collective-permute-start | bytes 442376 | tf_op jit(solution)/shard_map/ppermute | solution.py:60
  95.8 2.3 %collective-permute-start.17 = (bf16[2,64,1152]{2,1,0:T(8,128)(2,1)S(1)}, bf16[2,64,1152]{2,1,0:T(8,128)(2,1)S(1)}, u32[]{:S(2)}, u32[]{:S(2)}) collective-permute-start(bf16[2,64,1152]{2,1,0:T(8,128)(2,1)S(1)} %pad_maximum_fusion.7), channel_id=1, source_target_pairs={{0,1},{1,0},{2,3},{3,2},{4,5},{5,4},{6,7},{7,6},{8,9},{9,8},{10,11... | collective-permute-start | bytes 884744 | tf_op jit(solution)/shard_map/ppermute | solution.py:60
  105.7 1.7 %collective-permute-start.18 = (bf16[2,2,288,128]{3,2,1,0:T(8,128)(2,1)S(1)}, bf16[2,2,288,128]{3,2,1,0:T(8,128)(2,1)S(1)}, u32[]{:S(2)}, u32[]{:S(2)}) collective-permute-start(bf16[2,2,288,128]{3,2,1,0:T(8,128)(2,1)S(1)} %fusion.40), channel_id=1, source_target_pairs={{0,1},{1,0},{2,3},{3,2},{4,5},{5,4},{6,7},{7,6},{8,9},{9,8},{10,11... | collective-permute-start | bytes 884744 | tf_op jit(solution)/shard_map/ppermute | solution.py:60
  107.5 6.7 %collective-permute-start.19 = (bf16[2,288,128]{2,1,0:T(8,128)(2,1)S(1)}, bf16[2,288,128]{2,1,0:T(8,128)(2,1)S(1)}, u32[]{:S(2)}, u32[]{:S(2)}) collective-permute-start(bf16[2,288,128]{2,1,0:T(8,128)(2,1)S(1)} %fusion.50), channel_id=1, source_target_pairs={{0,2},{2,0},{1,3},{3,1},{4,6},{6,4},{5,7},{7,5},{8,10},{10,8},{9,1... | collective-permute-start | bytes 442376 | tf_op jit(solution)/shard_map/ppermute | solution.py:60
  (10 other events, 27.6 us)

commit v3 on v2

--- a/solution.py
+++ b/solution.py
@@ -94,11 +94,13 @@
 
 def sum_ring(chip, fetched, other, texts):
     half = chip.shape[0] // 2
-    fetched = fetched + swap(other, "c").astype(F32)
+    fetched = fetched.astype(F32) + swap(other, "c").astype(F32)
     one, two, three, four = jnp.split(fetched, [2 * half, 4 * half, 6 * half], axis=0)
     three = hop(three.astype(BF), -1).astype(F32)
-    four = hop(four.astype(BF), -2).astype(F32)
-    one = hop(one.astype(BF), -1).astype(F32)
+    four = hop(four.astype(BF), -2)
+    one, four = lax.optimization_barrier((one.astype(BF), four))
+    one = hop(one, -1).astype(F32)
+    four = four.astype(F32)
     first = lax.axis_index("c") == 0
     none = jnp.zeros_like(four)
     two = two + three
@@ -123,7 +125,7 @@
     image_part = jnp.dot(weights, texts[...], preferred_element_type=F32)
     at_fetched, at_other = chip.shape[0], chip.shape[0] + fetched.shape[0]
     chip[...] = image_part[:at_fetched, :]
-    fetched[...] = image_part[at_fetched:at_other, :]
+    fetched[...] = image_part[at_fetched:at_other, :].astype(BF)
     other[...] = image_part[at_other:, :].astype(BF)
 
 
@@ -138,7 +140,7 @@
         out_specs=[whole] * 4,
         out_shape=[
             jax.ShapeDtypeStruct((2 * part_rows, dim), F32),
-            jax.ShapeDtypeStruct((fetched, dim), F32),
+            jax.ShapeDtypeStruct((fetched, dim), BF),
             jax.ShapeDtypeStruct((fetched, dim), BF),
             jax.ShapeDtypeStruct(texts.shape, BF),
         ],

time: 115 us -> 114 us (level)
  waiting for transfers between devices: 39.3 us -> 35.9 us
  starting transfers between devices: 48.7 us -> 51 us
    ppermute x8, waiting for transfers between devices: 20.5 us -> 17.1 us  [hop(): return as_lies(lax.ppermute(as_lies(block), ('z', 'c'), pairs))]
    ppermute x8, starting transfers between devices: 13.5 us -> 16.2 us  [hop(): return as_lies(lax.ppermute(as_lies(block), ('z', 'c'), pairs))]
where the time goes in v3:
time: 114 us; the launch traced here: 113 us
  starting transfers between devices  51 us (45%)
  waiting for transfers between devices  35.9 us (31%)
  matrix products  12.7 us (11%)
  other arithmetic  5.28 us (5%)
  Pallas kernels  3.51 us (3%)
  local copies, waits for them, and re-layouts  2.58 us (2%)
  between operations  2.41 us (2%)
    ppermute x12, starting transfers between devices, swap(): return as_lies(lax.ppermute(as_lies(block), axis, [(0, 1), (1, 0)]))  22.4 us
    ppermute x12, waiting for transfers between devices, swap(): return as_lies(lax.ppermute(as_lies(block), axis, [(0, 1), (1, 0)]))  18.8 us
    ppermute x8, waiting for transfers between devices, hop(): return as_lies(lax.ppermute(as_lies(block), ('z', 'c'), pairs))  17.1 us
    ppermute x8, starting transfers between devices, hop(): return as_lies(lax.ppermute(as_lies(block), ('z', 'c'), pairs))  16.2 us
    all_to_all x2, starting transfers between devices, exchange(): return lax.all_to_all(parts, axes, 0, 0, tiled=True)  12.4 us
    dot_general x1, matrix products, on_device(): jnp.einsum('kte,kfe->ktf', block_low, fc2, preferred_element_type=F32)  4.63 us
    dot_general x1, matrix products, on_device(): preact = jnp.einsum('ktd,kdf->ktf', normed, fc1, preferred_element_type=F32)  4.41 us
    pallas_call x1, Pallas kernels, loss_block(): pl.pallas_call(functools.partial(loss_kernel, part_rows), in_specs=[small...  3.51 us
  transfers between devices with their start and end apart: 22, of which 15 were waited for; matrix products, arithmetic and copies ran while one was open for 4% of the time, Pallas kernels for 0%

profile of v3, /device:TPU:1, one launch (start us, length us, event | category | flops | bytes accessed | tf_op | source)
XLA Modules:
  0.0 113.4 jit_solution(2570537433413003588)
XLA Ops:
  0.0 3.6 %collective-permute-start = (bf16[2,288,128]{2,1,0:T(8,128)(2,1)}, bf16[2,288,128]{2,1,0:T(8,128)(2,1)S(1)}, u32[]{:S(2)}, u32[]{:S(2)}) collective-permute-start(bf16[2,288,128]{2,1,0:T(8,128)(2,1)} %bitcast.129), channel_id=1, source_target_pairs={{0,2},{2,0},{1,3},{3,1},{4,6},{6,4},{5,7},{7,5},{8,10},{10,8},{9,1... | collective-permute-start | bytes 442376 | tf_op jit(solution)/shard_map/ppermute | solution.py:60
  4.6 1.8 %collective-permute-done = bf16[2,288,128]{2,1,0:T(8,128)(2,1)S(1)} collective-permute-done((bf16[2,288,128]{2,1,0:T(8,128)(2,1)}, bf16[2,288,128]{2,1,0:T(8,128)(2,1)S(1)}, u32[]{:S(2)}, u32[]{:S(2)}) %collective-permute-start) | collective-permute-done | bytes 147488 | tf_op jit(solution)/shard_map/ppermute | solution.py:60
  6.5 3.8 %collective-permute-start.1 = (bf16[2,2,1,288,128]{4,3,2,1,0:T(8,128)(2,1)S(1)}, bf16[2,2,1,288,128]{4,3,2,1,0:T(8,128)(2,1)S(1)}, u32[]{:S(2)}, u32[]{:S(2)}) collective-permute-start(bf16[2,2,1,288,128]{4,3,2,1,0:T(8,128)(2,1)S(1)} %maximum_add_fusion), channel_id=1, source_target_pairs={{0,1},{1,0},{2,3},{3,2},{4,5},{5,4},{6,7},{7,6},{8,9},{9,8},{10,11... | collective-permute-start | bytes 884744 | tf_op jit(solution)/shard_map/ppermute | solution.py:60
  12.3 4.4 %fusion.9 = f32[2,128,1076]{1,2,0:T(8,128)S(1)} fusion(bf16[2,1152,1076]{1,0,2:T(2,128)(2,1)} %param.13, bf16[2,1152,128]{2,1,0:T(8,128)(2,1)S(1)} %bitcast.116, f32[2,1152]{1,0:T(2,128)S(1)} %convert_element_type.118, f32[2,1152]{1,0:T(2,128)S(1)} %convert_element_type.117, f32[2,128]{1,0:T(2,128)S(1)} %add_rsqrt_fusion, ...), kind=kOutput, calls=%fused_computation.9 | convolution fusion | flops 636695552 | bytes 6678944 | tf_op jit(solution)/shard_map/ktd,kdf->ktf/dot_general | solution.py:179
  19.8 1.5 %collective-permute-start.3 = (bf16[2,32,1152]{2,1,0:T(8,128)(2,1)S(1)}, bf16[2,32,1152]{2,1,0:T(8,128)(2,1)S(1)}, u32[]{:S(2)}, u32[]{:S(2)}) collective-permute-start(bf16[2,32,1152]{2,1,0:T(8,128)(2,1)S(1)} %fusion.49), channel_id=1, source_target_pairs={{0,2},{2,0},{1,3},{3,1},{4,6},{6,4},{5,7},{7,5},{8,10},{10,8},{9,1... | collective-permute-start | bytes 442376 | tf_op jit(solution)/shard_map/ppermute | solution.py:60
  22.1 4.4 %collective-permute-done.3 = bf16[2,32,1152]{2,1,0:T(8,128)(2,1)S(1)} collective-permute-done((bf16[2,32,1152]{2,1,0:T(8,128)(2,1)S(1)}, bf16[2,32,1152]{2,1,0:T(8,128)(2,1)S(1)}, u32[]{:S(2)}, u32[]{:S(2)}) %collective-permute-start.3) | collective-permute-done | bytes 147488 | tf_op jit(solution)/shard_map/ppermute | solution.py:60
  29.2 5.5 %all-to-all-start = ((bf16[16,32,1152]{2,1,0:T(8,128)(2,1)}), bf16[16,32,1152]{2,1,0:T(8,128)(2,1)S(1)}, u32[]{:S(2)}, u32[]{:S(2)}) async-start(bf16[16,32,1152]{2,1,0:T(8,128)(2,1)} %broadcast_in_dim.4), calls=%async_computation | async-start | bytes 2359296 | tf_op jit(solution)/shard_map/all_to_all | solution.py:56
  34.7 3.1 %collective-permute-start.6 = (bf16[64,1152]{1,0:T(8,128)(2,1)S(1)}, bf16[64,1152]{1,0:T(8,128)(2,1)S(1)}, u32[]{:S(2)}, u32[]{:S(2)}) collective-permute-start(bf16[64,1152]{1,0:T(8,128)(2,1)S(1)} %pad_maximum_fusion.9), channel_id=1, source_target_pairs={{16,0},{49,1},{24,8},{57,9},{32,16},{1,17},{40,24},{9,25},{48,32},... | collective-permute-start | bytes 442376 | tf_op jit(solution)/shard_map/ppermute | solution.py:52
  37.8 1.6 %collective-permute-start.5 = (bf16[64,1152]{1,0:T(8,128)(2,1)S(1)}, bf16[64,1152]{1,0:T(8,128)(2,1)S(1)}, u32[]{:S(2)}, u32[]{:S(2)}) collective-permute-start(bf16[64,1152]{1,0:T(8,128)(2,1)S(1)} %pad_maximum_fusion.9), channel_id=1, source_target_pairs={{8,0},{57,1},{16,8},{1,9},{24,16},{9,17},{32,24},{17,25},{40,32},{... | collective-permute-start | bytes 442376 | tf_op jit(solution)/shard_map/ppermute | solution.py:52
  39.4 4.3 %collective-permute-done.6 = bf16[64,1152]{1,0:T(8,128)(2,1)S(1)} collective-permute-done((bf16[64,1152]{1,0:T(8,128)(2,1)S(1)}, bf16[64,1152]{1,0:T(8,128)(2,1)S(1)}, u32[]{:S(2)}, u32[]{:S(2)}) %collective-permute-start.6) | collective-permute-done | bytes 147488 | tf_op jit(solution)/shard_map/ppermute | solution.py:52
  43.7 2.3 %collective-permute-start.7 = (bf16[64,1152]{1,0:T(8,128)(2,1)S(1)}, bf16[64,1152]{1,0:T(8,128)(2,1)S(1)}, u32[]{:S(2)}, u32[]{:S(2)}) collective-permute-start(bf16[64,1152]{1,0:T(8,128)(2,1)S(1)} %collective-permute-done.6), channel_id=1, source_target_pairs={{8,0},{57,1},{16,8},{1,9},{24,16},{9,17},{32,24},{17,25},{40,32},{... | collective-permute-start | bytes 442376 | tf_op jit(solution)/shard_map/ppermute | solution.py:52
  46.3 6.1 %collective-permute-done.8 = bf16[32,1152]{1,0:T(8,128)(2,1)S(1)} collective-permute-done((bf16[32,1152]{1,0:T(8,128)(2,1)S(1)}, bf16[32,1152]{1,0:T(8,128)(2,1)S(1)}, u32[]{:S(2)}, u32[]{:S(2)}) %collective-permute-start.8) | collective-permute-done | bytes 73760 | tf_op jit(solution)/shard_map/ppermute | solution.py:52
  56.1 3.5 %shard_map.100 = (f32[64,1152]{1,0:T(8,128)S(1)}, bf16[224,1152]{1,0:T(8,128)(2,1)S(1)}, bf16[224,1152]{1,0:T(8,128)(2,1)S(1)}, bf16[512,1152]{1,0:T(8,128)(2,1)}) custom-call(f32[3]{0:T(128)S(1)} %pad_maximum_fusion.10.scalars, s32[2]{0:T(128)S(1)} %add_multiply_fusion.first, bf16[512,1152]{1,0:T(8,128)(2,1)S(1)} %pad_maximum_fusion.images, ...), custom_call_target="tpu_custom_call" | custom-call | flops 1811939328 | bytes 5898240 | tf_op jit(solution)/shard_map/pallas_call | solution.py:137
  59.6 6.9 %all-to-all-start.1 = ((bf16[16,32,1152]{2,1,0:T(8,128)(2,1)}), bf16[16,32,1152]{2,1,0:T(8,128)(2,1)S(1)}, u32[]{:S(2)}, u32[]{:S(2)}) async-start(bf16[16,32,1152]{2,1,0:T(8,128)(2,1)} %bitcast.23), calls=%async_computation.1 | async-start | bytes 2359296 | tf_op jit(solution)/shard_map/all_to_all | solution.py:56
  67.8 3.3 %collective-permute-start.11 = (bf16[32,1152]{1,0:T(8,128)(2,1)S(1)}, bf16[32,1152]{1,0:T(8,128)(2,1)S(1)}, u32[]{:S(2)}, u32[]{:S(2)}) collective-permute-start(bf16[32,1152]{1,0:T(8,128)(2,1)S(1)} %split.20), channel_id=1, source_target_pairs={{48,0},{17,1},{56,8},{25,9},{0,16},{33,17},{8,24},{41,25},{16,32},... | collective-permute-start | bytes 221192 | tf_op jit(solution)/shard_map/ppermute | solution.py:52
  73.0 3.8 %collective-permute-start.12 = (bf16[64,1152]{1,0:T(8,128)(2,1)S(1)}, bf16[64,1152]{1,0:T(8,128)(2,1)S(1)}, u32[]{:S(2)}, u32[]{:S(2)}) collective-permute-start(bf16[64,1152]{1,0:T(8,128)(2,1)S(1)} %get-tuple-element.34), channel_id=1, source_target_pairs={{56,0},{9,1},{0,8},{17,9},{8,16},{25,17},{16,24},{33,25},{24,32},{... | collective-permute-start | bytes 442376 | tf_op jit(solution)/shard_map/ppermute | solution.py:52
  79.0 4.5 %collective-permute-done.14 = bf16[64,1152]{1,0:T(8,128)(2,1)S(1)} collective-permute-done((bf16[64,1152]{1,0:T(8,128)(2,1)S(1)}, bf16[64,1152]{1,0:T(8,128)(2,1)S(1)}, u32[]{:S(2)}, u32[]{:S(2)}) %collective-permute-start.14) | collective-permute-done | bytes 147488 | tf_op jit(solution)/shard_map/ppermute | solution.py:52
  83.6 2.5 %collective-permute-start.15 = (bf16[32,1152]{1,0:T(8,128)(2,1)S(1)}, bf16[32,1152]{1,0:T(8,128)(2,1)S(1)}, u32[]{:S(2)}, u32[]{:S(2)}) collective-permute-start(bf16[32,1152]{1,0:T(8,128)(2,1)S(1)} %fusion.52), channel_id=1, source_target_pairs={{0,1},{1,0},{2,3},{3,2},{4,5},{5,4},{6,7},{7,6},{8,9},{9,8},{10,11... | collective-permute-start | bytes 221192 | tf_op jit(solution)/shard_map/ppermute | solution.py:60
  87.2 3.2 %collective-permute-start.16 = (bf16[2,32,1152]{2,1,0:T(8,128)(2,1)S(1)}, bf16[2,32,1152]{2,1,0:T(8,128)(2,1)S(1)}, u32[]{:S(2)}, u32[]{:S(2)}) collective-permute-start(bf16[2,32,1152]{2,1,0:T(8,128)(2,1)S(1)} %fusion.18), channel_id=1, source_target_pairs={{0,2},{2,0},{1,3},{3,1},{4,6},{6,4},{5,7},{7,5},{8,10},{10,8},{9,1... | collective-permute-start | bytes 442376 | tf_op jit(solution)/shard_map/ppermute | solution.py:60
  90.5 3.8 %collective-permute-done.16 = bf16[2,32,1152]{2,1,0:T(8,128)(2,1)S(1)} collective-permute-done((bf16[2,32,1152]{2,1,0:T(8,128)(2,1)S(1)}, bf16[2,32,1152]{2,1,0:T(8,128)(2,1)S(1)}, u32[]{:S(2)}, u32[]{:S(2)}) %collective-permute-start.16) | collective-permute-done | bytes 147488 | tf_op jit(solution)/shard_map/ppermute | solution.py:60
  96.8 4.6 %fusion.27 = bf16[2,128,1076]{1,2,0:T(8,128)(2,1)S(1)} fusion(f32[2,128,1076]{1,2,0:T(8,128)S(1)} %copy-done.5, bf16[2,1076,1152]{2,0,1:T(2,128)(2,1)} %param.15, bf16[2,64,1152]{2,1,0:T(8,128)(2,1)S(1)} %get-tuple-element.44, bf16[2,64,1152]{2,1,0:T(8,128)(2,1)S(1)} %get-tuple-element.43), kind=kOutput, calls=%fused_computation.34 | convolution fusion | flops 641339392 | bytes 7200768 | tf_op jit(solution)/shard_map/kte,kfe->ktf/dot_general | solution.py:207
  101.4 2.4 %fusion.60 = (f32[2,128]{1,0:T(2,128)S(1)}, f32[2,128]{1,0:T(2,128)S(1)}, f32[2,128,1152]{1,2,0:T(8,128)S(1)}) fusion(f32[2,128]{1,0:T(2,128)S(1)} %add_rsqrt_fusion, f32[2,128]{1,0:T(2,128)S(1)} %broadcast_multiply_fusion.2, bf16[2,1152,128]{2,1,0:T(8,128)(2,1)S(1)} %bitcast.118, f32[2,1152]{1,0:T(2,128)S(1)} %convert_element_type.117, ...), kind=kOutput, calls=%fused_computation.116 | convolution fusion | flops 636714496 | bytes 7291904 | tf_op jit(solution)/shard_map/ktf,kdf->ktd/dot_general | solution.py:210
  106.0 3.1 %collective-permute-start.19 = (bf16[2,288,128]{2,1,0:T(8,128)(2,1)S(1)}, bf16[2,288,128]{2,1,0:T(8,128)(2,1)S(1)}, u32[]{:S(2)}, u32[]{:S(2)}) collective-permute-start(bf16[2,288,128]{2,1,0:T(8,128)(2,1)S(1)} %fusion.50), channel_id=1, source_target_pairs={{0,2},{2,0},{1,3},{3,1},{4,6},{6,4},{5,7},{7,5},{8,10},{10,8},{9,1... | collective-permute-start | bytes 442376 | tf_op jit(solution)/shard_map/ppermute | solution.py:60
  109.4 3.3 %collective-permute-done.19 = bf16[2,288,128]{2,1,0:T(8,128)(2,1)S(1)} collective-permute-done((bf16[2,288,128]{2,1,0:T(8,128)(2,1)S(1)}, bf16[2,288,128]{2,1,0:T(8,128)(2,1)S(1)}, u32[]{:S(2)}, u32[]{:S(2)}) %collective-permute-start.19) | collective-permute-done | bytes 147488 | tf_op jit(solution)/shard_map/ppermute | solution.py:60
  (100 shorter events, 23.6 us)
Async XLA Ops:
  0.0 6.4 %collective-permute-start = (bf16[2,288,128]{2,1,0:T(8,128)(2,1)}, bf16[2,288,128]{2,1,0:T(8,128)(2,1)S(1)}, u32[]{:S(2)}, u32[]{:S(2)}) collective-permute-start(bf16[2,288,128]{2,1,0:T(8,128)(2,1)} %bitcast.129), channel_id=1, source_target_pairs={{0,2},{2,0},{1,3},{3,1},{4,6},{6,4},{5,7},{7,5},{8,10},{10,8},{9,1... | collective-permute-start | bytes 442376 | tf_op jit(solution)/shard_map/ppermute | solution.py:60
  6.5 5.0 %collective-permute-start.1 = (bf16[2,2,1,288,128]{4,3,2,1,0:T(8,128)(2,1)S(1)}, bf16[2,2,1,288,128]{4,3,2,1,0:T(8,128)(2,1)S(1)}, u32[]{:S(2)}, u32[]{:S(2)}) collective-permute-start(bf16[2,2,1,288,128]{4,3,2,1,0:T(8,128)(2,1)S(1)} %maximum_add_fusion), channel_id=1, source_target_pairs={{0,1},{1,0},{2,3},{3,2},{4,5},{5,4},{6,7},{7,6},{8,9},{9,8},{10,11... | collective-permute-start | bytes 884744 | tf_op jit(solution)/shard_map/ppermute | solution.py:60
  11.8 4.9 %slice-start = ((s8[4958208]{0:T(1024)(128)(4,1)}), s8[4194304]{0:T(1024)(128)(4,1)S(1)}, s32[]{:S(2)}) async-start(s8[4958208]{0:T(1024)(128)(4,1)} %bitcast.131), calls=%async_computation.2 | async-start | bytes 8388608
  18.1 1.7 %collective-permute-start.2 = (bf16[2,64,1152]{2,1,0:T(8,128)(2,1)S(1)}, bf16[2,64,1152]{2,1,0:T(8,128)(2,1)S(1)}, u32[]{:S(2)}, u32[]{:S(2)}) collective-permute-start(bf16[2,64,1152]{2,1,0:T(8,128)(2,1)S(1)} %fusion.39), channel_id=1, source_target_pairs={{0,1},{1,0},{2,3},{3,2},{4,5},{5,4},{6,7},{7,6},{8,9},{9,8},{10,11... | collective-permute-start | bytes 884744 | tf_op jit(solution)/shard_map/ppermute | solution.py:60
  19.8 6.7 %collective-permute-start.3 = (bf16[2,32,1152]{2,1,0:T(8,128)(2,1)S(1)}, bf16[2,32,1152]{2,1,0:T(8,128)(2,1)S(1)}, u32[]{:S(2)}, u32[]{:S(2)}) collective-permute-start(bf16[2,32,1152]{2,1,0:T(8,128)(2,1)S(1)} %fusion.49), channel_id=1, source_target_pairs={{0,2},{2,0},{1,3},{3,1},{4,6},{6,4},{5,7},{7,5},{8,10},{10,8},{9,1... | collective-permute-start | bytes 442376 | tf_op jit(solution)/shard_map/ppermute | solution.py:60
  26.8 7.9 %collective-permute-start.4 = (bf16[32,1152]{1,0:T(8,128)(2,1)S(1)}, bf16[32,1152]{1,0:T(8,128)(2,1)S(1)}, u32[]{:S(2)}, u32[]{:S(2)}) collective-permute-start(bf16[32,1152]{1,0:T(8,128)(2,1)S(1)} %get-tuple-element.54), channel_id=1, source_target_pairs={{0,1},{1,0},{2,3},{3,2},{4,5},{5,4},{6,7},{7,6},{8,9},{9,8},{10,11... | collective-permute-start | bytes 221192 | tf_op jit(solution)/shard_map/ppermute | solution.py:60
  29.2 23.3 %all-to-all-start = ((bf16[16,32,1152]{2,1,0:T(8,128)(2,1)}), bf16[16,32,1152]{2,1,0:T(8,128)(2,1)S(1)}, u32[]{:S(2)}, u32[]{:S(2)}) async-start(bf16[16,32,1152]{2,1,0:T(8,128)(2,1)} %broadcast_in_dim.4), calls=%async_computation | async-start | bytes 2359296 | tf_op jit(solution)/shard_map/all_to_all | solution.py:56
  34.7 9.0 %collective-permute-start.6 = (bf16[64,1152]{1,0:T(8,128)(2,1)S(1)}, bf16[64,1152]{1,0:T(8,128)(2,1)S(1)}, u32[]{:S(2)}, u32[]{:S(2)}) collective-permute-start(bf16[64,1152]{1,0:T(8,128)(2,1)S(1)} %pad_maximum_fusion.9), channel_id=1, source_target_pairs={{16,0},{49,1},{24,8},{57,9},{32,16},{1,17},{40,24},{9,25},{48,32},... | collective-permute-start | bytes 442376 | tf_op jit(solution)/shard_map/ppermute | solution.py:52
  37.8 8.6 %collective-permute-start.5 = (bf16[64,1152]{1,0:T(8,128)(2,1)S(1)}, bf16[64,1152]{1,0:T(8,128)(2,1)S(1)}, u32[]{:S(2)}, u32[]{:S(2)}) collective-permute-start(bf16[64,1152]{1,0:T(8,128)(2,1)S(1)} %pad_maximum_fusion.9), channel_id=1, source_target_pairs={{8,0},{57,1},{16,8},{1,9},{24,16},{9,17},{32,24},{17,25},{40,32},{... | collective-permute-start | bytes 442376 | tf_op jit(solution)/shard_map/ppermute | solution.py:52
  43.7 8.7 %collective-permute-start.7 = (bf16[64,1152]{1,0:T(8,128)(2,1)S(1)}, bf16[64,1152]{1,0:T(8,128)(2,1)S(1)}, u32[]{:S(2)}, u32[]{:S(2)}) collective-permute-start(bf16[64,1152]{1,0:T(8,128)(2,1)S(1)} %collective-permute-done.6), channel_id=1, source_target_pairs={{8,0},{57,1},{16,8},{1,9},{24,16},{9,17},{32,24},{17,25},{40,32},{... | collective-permute-start | bytes 442376 | tf_op jit(solution)/shard_map/ppermute | solution.py:52
  46.0 6.5 %collective-permute-start.8 = (bf16[32,1152]{1,0:T(8,128)(2,1)S(1)}, bf16[32,1152]{1,0:T(8,128)(2,1)S(1)}, u32[]{:S(2)}, u32[]{:S(2)}) collective-permute-start(bf16[32,1152]{1,0:T(8,128)(2,1)S(1)} %constant_dynamic-slice_fusion), channel_id=1, source_target_pairs={{16,0},{49,1},{24,8},{57,9},{32,16},{1,17},{40,24},{9,25},{48,32},... | collective-permute-start | bytes 221192 | tf_op jit(solution)/shard_map/ppermute | solution.py:52
  52.5 3.5 %collective-permute-start.9 = (bf16[224,1152]{1,0:T(8,128)(2,1)S(1)}, bf16[224,1152]{1,0:T(8,128)(2,1)S(1)}, u32[]{:S(2)}, u32[]{:S(2)}) collective-permute-start(bf16[224,1152]{1,0:T(8,128)(2,1)S(1)} %pad_maximum_fusion.4), channel_id=1, source_target_pairs={{0,1},{1,0},{2,3},{3,2},{4,5},{5,4},{6,7},{7,6},{8,9},{9,8},{10,11... | collective-permute-start | bytes 1548296 | tf_op jit(solution)/shard_map/ppermute | solution.py:60
  59.6 7.0 %collective-permute-start.10 = (bf16[224,1152]{1,0:T(8,128)(2,1)S(1)}, bf16[224,1152]{1,0:T(8,128)(2,1)}, u32[]{:S(2)}, u32[]{:S(2)}) collective-permute-start(bf16[224,1152]{1,0:T(8,128)(2,1)S(1)} %get-tuple-element.33), channel_id=1, source_target_pairs={{0,1},{1,0},{2,3},{3,2},{4,5},{5,4},{6,7},{7,6},{8,9},{9,8},{10,11... | collective-permute-start | bytes 1548296 | tf_op jit(solution)/shard_map/ppermute | solution.py:60
  59.6 23.9 %all-to-all-start.1 = ((bf16[16,32,1152]{2,1,0:T(8,128)(2,1)}), bf16[16,32,1152]{2,1,0:T(8,128)(2,1)S(1)}, u32[]{:S(2)}, u32[]{:S(2)}) async-start(bf16[16,32,1152]{2,1,0:T(8,128)(2,1)} %bitcast.23), calls=%async_computation.1 | async-start | bytes 2359296 | tf_op jit(solution)/shard_map/all_to_all | solution.py:56
  67.8 5.3 %collective-permute-start.11 = (bf16[32,1152]{1,0:T(8,128)(2,1)S(1)}, bf16[32,1152]{1,0:T(8,128)(2,1)S(1)}, u32[]{:S(2)}, u32[]{:S(2)}) collective-permute-start(bf16[32,1152]{1,0:T(8,128)(2,1)S(1)} %split.20), channel_id=1, source_target_pairs={{48,0},{17,1},{56,8},{25,9},{0,16},{33,17},{8,24},{41,25},{16,32},... | collective-permute-start | bytes 221192 | tf_op jit(solution)/shard_map/ppermute | solution.py:52
  71.1 5.8 %collective-permute-start.13 = (bf16[64,1152]{1,0:T(8,128)(2,1)S(1)}, bf16[64,1152]{1,0:T(8,128)(2,1)S(1)}, u32[]{:S(2)}, u32[]{:S(2)}) collective-permute-start(bf16[64,1152]{1,0:T(8,128)(2,1)S(1)} %get-tuple-element.47), channel_id=1, source_target_pairs={{56,0},{9,1},{0,8},{17,9},{8,16},{25,17},{16,24},{33,25},{24,32},{... | collective-permute-start | bytes 442376 | tf_op jit(solution)/shard_map/ppermute | solution.py:52
  73.0 5.9 %collective-permute-start.12 = (bf16[64,1152]{1,0:T(8,128)(2,1)S(1)}, bf16[64,1152]{1,0:T(8,128)(2,1)S(1)}, u32[]{:S(2)}, u32[]{:S(2)}) collective-permute-start(bf16[64,1152]{1,0:T(8,128)(2,1)S(1)} %get-tuple-element.34), channel_id=1, source_target_pairs={{56,0},{9,1},{0,8},{17,9},{8,16},{25,17},{16,24},{33,25},{24,32},{... | collective-permute-start | bytes 442376 | tf_op jit(solution)/shard_map/ppermute | solution.py:52
  77.0 6.5 %collective-permute-start.14 = (bf16[64,1152]{1,0:T(8,128)(2,1)S(1)}, bf16[64,1152]{1,0:T(8,128)(2,1)S(1)}, u32[]{:S(2)}, u32[]{:S(2)}) collective-permute-start(bf16[64,1152]{1,0:T(8,128)(2,1)S(1)} %fusion.42), channel_id=1, source_target_pairs={{48,0},{17,1},{56,8},{25,9},{0,16},{33,17},{8,24},{41,25},{16,32},... | collective-permute-start | bytes 442376 | tf_op jit(solution)/shard_map/ppermute | solution.py:52
  83.6 3.5 %collective-permute-start.15 = (bf16[32,1152]{1,0:T(8,128)(2,1)S(1)}, bf16[32,1152]{1,0:T(8,128)(2,1)S(1)}, u32[]{:S(2)}, u32[]{:S(2)}) collective-permute-start(bf16[32,1152]{1,0:T(8,128)(2,1)S(1)} %fusion.52), channel_id=1, source_target_pairs={{0,1},{1,0},{2,3},{3,2},{4,5},{5,4},{6,7},{7,6},{8,9},{9,8},{10,11... | collective-permute-start | bytes 221192 | tf_op jit(solution)/shard_map/ppermute | solution.py:60
  87.2 9.5 %copy-start.5 = (f32[2,128,1076]{1,2,0:T(8,128)S(1)}, f32[2,128,1076]{1,2,0:T(8,128)}, u32[]{:S(2)}) copy-start(f32[2,128,1076]{1,2,0:T(8,128)} %copy-done.4) | copy-start | bytes 3305476
  87.2 7.1 %collective-permute-start.16 = (bf16[2,32,1152]{2,1,0:T(8,128)(2,1)S(1)}, bf16[2,32,1152]{2,1,0:T(8,128)(2,1)S(1)}, u32[]{:S(2)}, u32[]{:S(2)}) collective-permute-start(bf16[2,32,1152]{2,1,0:T(8,128)(2,1)S(1)} %fusion.18), channel_id=1, source_target_pairs={{0,2},{2,0},{1,3},{3,1},{4,6},{6,4},{5,7},{7,5},{8,10},{10,8},{9,1... | collective-permute-start | bytes 442376 | tf_op jit(solution)/shard_map/ppermute | solution.py:60
  94.4 2.3 %collective-permute-start.17 = (bf16[2,64,1152]{2,1,0:T(8,128)(2,1)S(1)}, bf16[2,64,1152]{2,1,0:T(8,128)(2,1)S(1)}, u32[]{:S(2)}, u32[]{:S(2)}) collective-permute-start(bf16[2,64,1152]{2,1,0:T(8,128)(2,1)S(1)} %pad_maximum_fusion.7), channel_id=1, source_target_pairs={{0,1},{1,0},{2,3},{3,2},{4,5},{5,4},{6,7},{7,6},{8,9},{9,8},{10,11... | collective-permute-start | bytes 884744 | tf_op jit(solution)/shard_map/ppermute | solution.py:60
  104.2 1.7 %collective-permute-start.18 = (bf16[2,2,288,128]{3,2,1,0:T(8,128)(2,1)S(1)}, bf16[2,2,288,128]{3,2,1,0:T(8,128)(2,1)S(1)}, u32[]{:S(2)}, u32[]{:S(2)}) collective-permute-start(bf16[2,2,288,128]{3,2,1,0:T(8,128)(2,1)S(1)} %fusion.40), channel_id=1, source_target_pairs={{0,1},{1,0},{2,3},{3,2},{4,5},{5,4},{6,7},{7,6},{8,9},{9,8},{10,11... | collective-permute-start | bytes 884744 | tf_op jit(solution)/shard_map/ppermute | solution.py:60
  106.0 6.7 %collective-permute-start.19 = (bf16[2,288,128]{2,1,0:T(8,128)(2,1)S(1)}, bf16[2,288,128]{2,1,0:T(8,128)(2,1)S(1)}, u32[]{:S(2)}, u32[]{:S(2)}) collective-permute-start(bf16[2,288,128]{2,1,0:T(8,128)(2,1)S(1)} %fusion.50), channel_id=1, source_target_pairs={{0,2},{2,0},{1,3},{3,1},{4,6},{6,4},{5,7},{7,5},{8,10},{10,8},{9,1... | collective-permute-start | bytes 442376 | tf_op jit(solution)/shard_map/ppermute | solution.py:60
  (8 other events, 17.9 us)

commit v4 on v3

--- a/solution.py
+++ b/solution.py
@@ -203,10 +203,15 @@
 
     block_own = through_normalise(jnp.stack([image_grad, text_grad]), units, lengths)
     block_own = as_lies(block_own)
-    block_low = as_lies(swap_join(as_lies(swap_join(block_own, "xh", 1)), "c", 1))
+    block_own, preact = lax.optimization_barrier((block_own, preact))
+    far = swap(block_own, "xh")
+    _, gelu_back = jax.vjp(gelu_tanh, preact)
+    slope = gelu_back(jnp.ones_like(preact))[0]
+    far, slope = lax.optimization_barrier((far, slope))
+    block_low = as_lies(in_order(block_own, far, "xh", 1))
+    block_low = as_lies(swap_join(block_low, "c", 1))
     hidden_grad = jnp.einsum("kte,kfe->ktf", block_low, fc2, preferred_element_type=F32)
-    _, gelu_back = jax.vjp(gelu_tanh, preact)
-    preact_grad = lax.optimization_barrier(gelu_back(hidden_grad)[0].astype(BF))
+    preact_grad = lax.optimization_barrier((hidden_grad * slope).astype(BF))
     normed_grad = jnp.einsum("ktf,kdf->ktd", preact_grad, fc1, preferred_element_type=F32)
     scaled = normed_grad * gains
     norm_term = (

time: 114 us -> 113 us (level)
  transfers between devices with their start and end apart: 22 -> 22, of which waited for: 15 -> 15; matrix products, arithmetic and copies ran while one was open for 4% -> 5% of each run, Pallas kernels for 0% -> 0%
where the time goes in v4:
time: 113 us
  starting transfers between devices  50.9 us (45%)
  waiting for transfers between devices  35.3 us (31%)
  matrix products  12.3 us (11%)
  other arithmetic  5.93 us (5%)
  Pallas kernels  3.5 us (3%)
  local copies, waits for them, and re-layouts  2.58 us (2%)
  between operations  2.41 us (2%)
    ppermute x12, starting transfers between devices, swap(): return as_lies(lax.ppermute(as_lies(block), axis, [(0, 1), (1, 0)]))  22.4 us
    ppermute x12, waiting for transfers between devices, swap(): return as_lies(lax.ppermute(as_lies(block), axis, [(0, 1), (1, 0)]))  18.1 us
    ppermute x8, waiting for transfers between devices, hop(): return as_lies(lax.ppermute(as_lies(block), ('z', 'c'), pairs))  17.2 us
    ppermute x8, starting transfers between devices, hop(): return as_lies(lax.ppermute(as_lies(block), ('z', 'c'), pairs))  16.1 us
    all_to_all x2, starting transfers between devices, exchange(): return lax.all_to_all(parts, axes, 0, 0, tiled=True)  12.4 us
    dot_general x1, matrix products, on_device(): preact = jnp.einsum('ktd,kdf->ktf', normed, fc1, preferred_element_type=F32)  4.43 us
    dot_general x1, matrix products, on_device(): jnp.einsum('kte,kfe->ktf', block_low, fc2, preferred_element_type=F32)  4.17 us
    pallas_call x1, Pallas kernels, loss_block(): pl.pallas_call(functools.partial(loss_kernel, part_rows), in_specs=[small...  3.5 us
  transfers between devices with their start and end apart: 22, of which 15 were waited for; matrix products, arithmetic and copies ran while one was open for 5% of the time, Pallas kernels for 0%

profile of v4, /device:TPU:1, one launch (start us, length us, event | category | flops | bytes accessed | tf_op | source)
XLA Modules:
  0.0 112.9 jit_solution(10672037357609977366)
XLA Ops:
  0.0 3.6 %collective-permute-start = (bf16[2,288,128]{2,1,0:T(8,128)(2,1)}, bf16[2,288,128]{2,1,0:T(8,128)(2,1)S(1)}, u32[]{:S(2)}, u32[]{:S(2)}) collective-permute-start(bf16[2,288,128]{2,1,0:T(8,128)(2,1)} %bitcast.129), channel_id=1, source_target_pairs={{0,2},{2,0},{1,3},{3,1},{4,6},{6,4},{5,7},{7,5},{8,10},{10,8},{9,1... | collective-permute-start | bytes 442376 | tf_op jit(solution)/shard_map/ppermute | solution.py:60
  4.6 1.8 %collective-permute-done = bf16[2,288,128]{2,1,0:T(8,128)(2,1)S(1)} collective-permute-done((bf16[2,288,128]{2,1,0:T(8,128)(2,1)}, bf16[2,288,128]{2,1,0:T(8,128)(2,1)S(1)}, u32[]{:S(2)}, u32[]{:S(2)}) %collective-permute-start) | collective-permute-done | bytes 147488 | tf_op jit(solution)/shard_map/ppermute | solution.py:60
  6.5 3.8 %collective-permute-start.1 = (bf16[2,2,1,288,128]{4,3,2,1,0:T(8,128)(2,1)S(1)}, bf16[2,2,1,288,128]{4,3,2,1,0:T(8,128)(2,1)S(1)}, u32[]{:S(2)}, u32[]{:S(2)}) collective-permute-start(bf16[2,2,1,288,128]{4,3,2,1,0:T(8,128)(2,1)S(1)} %maximum_add_fusion), channel_id=1, source_target_pairs={{0,1},{1,0},{2,3},{3,2},{4,5},{5,4},{6,7},{7,6},{8,9},{9,8},{10,11... | collective-permute-start | bytes 884744 | tf_op jit(solution)/shard_map/ppermute | solution.py:60
  12.3 4.4 %fusion.9 = f32[2,128,1076]{1,2,0:T(8,128)S(1)} fusion(bf16[2,1152,1076]{1,0,2:T(2,128)(2,1)} %param.13, bf16[2,1152,128]{2,1,0:T(8,128)(2,1)S(1)} %bitcast.116, f32[2,1152]{1,0:T(2,128)S(1)} %convert_element_type.118, f32[2,1152]{1,0:T(2,128)S(1)} %convert_element_type.117, f32[2,128]{1,0:T(2,128)S(1)} %add_rsqrt_fusion, ...), kind=kOutput, calls=%fused_computation.9 | convolution fusion | flops 636695552 | bytes 6678944 | tf_op jit(solution)/shard_map/ktd,kdf->ktf/dot_general | solution.py:179
  19.8 1.5 %collective-permute-start.3 = (bf16[2,32,1152]{2,1,0:T(8,128)(2,1)S(1)}, bf16[2,32,1152]{2,1,0:T(8,128)(2,1)S(1)}, u32[]{:S(2)}, u32[]{:S(2)}) collective-permute-start(bf16[2,32,1152]{2,1,0:T(8,128)(2,1)S(1)} %fusion.61), channel_id=1, source_target_pairs={{0,2},{2,0},{1,3},{3,1},{4,6},{6,4},{5,7},{7,5},{8,10},{10,8},{9,1... | collective-permute-start | bytes 442376 | tf_op jit(solution)/shard_map/ppermute | solution.py:60
  22.1 4.4 %collective-permute-done.3 = bf16[2,32,1152]{2,1,0:T(8,128)(2,1)S(1)} collective-permute-done((bf16[2,32,1152]{2,1,0:T(8,128)(2,1)S(1)}, bf16[2,32,1152]{2,1,0:T(8,128)(2,1)S(1)}, u32[]{:S(2)}, u32[]{:S(2)}) %collective-permute-start.3) | collective-permute-done | bytes 147488 | tf_op jit(solution)/shard_map/ppermute | solution.py:60
  29.2 5.5 %all-to-all-start = ((bf16[16,32,1152]{2,1,0:T(8,128)(2,1)}), bf16[16,32,1152]{2,1,0:T(8,128)(2,1)S(1)}, u32[]{:S(2)}, u32[]{:S(2)}) async-start(bf16[16,32,1152]{2,1,0:T(8,128)(2,1)} %broadcast_in_dim.4), calls=%async_computation | async-start | bytes 2359296 | tf_op jit(solution)/shard_map/all_to_all | solution.py:56
  34.7 3.1 %collective-permute-start.6 = (bf16[64,1152]{1,0:T(8,128)(2,1)S(1)}, bf16[64,1152]{1,0:T(8,128)(2,1)S(1)}, u32[]{:S(2)}, u32[]{:S(2)}) collective-permute-start(bf16[64,1152]{1,0:T(8,128)(2,1)S(1)} %pad_maximum_fusion.9), channel_id=1, source_target_pairs={{16,0},{49,1},{24,8},{57,9},{32,16},{1,17},{40,24},{9,25},{48,32},... | collective-permute-start | bytes 442376 | tf_op jit(solution)/shard_map/ppermute | solution.py:52
  37.8 1.6 %collective-permute-start.5 = (bf16[64,1152]{1,0:T(8,128)(2,1)S(1)}, bf16[64,1152]{1,0:T(8,128)(2,1)S(1)}, u32[]{:S(2)}, u32[]{:S(2)}) collective-permute-start(bf16[64,1152]{1,0:T(8,128)(2,1)S(1)} %pad_maximum_fusion.9), channel_id=1, source_target_pairs={{8,0},{57,1},{16,8},{1,9},{24,16},{9,17},{32,24},{17,25},{40,32},{... | collective-permute-start | bytes 442376 | tf_op jit(solution)/shard_map/ppermute | solution.py:52
  39.4 4.3 %collective-permute-done.6 = bf16[64,1152]{1,0:T(8,128)(2,1)S(1)} collective-permute-done((bf16[64,1152]{1,0:T(8,128)(2,1)S(1)}, bf16[64,1152]{1,0:T(8,128)(2,1)S(1)}, u32[]{:S(2)}, u32[]{:S(2)}) %collective-permute-start.6) | collective-permute-done | bytes 147488 | tf_op jit(solution)/shard_map/ppermute | solution.py:52
  43.7 2.3 %collective-permute-start.7 = (bf16[64,1152]{1,0:T(8,128)(2,1)S(1)}, bf16[64,1152]{1,0:T(8,128)(2,1)S(1)}, u32[]{:S(2)}, u32[]{:S(2)}) collective-permute-start(bf16[64,1152]{1,0:T(8,128)(2,1)S(1)} %collective-permute-done.6), channel_id=1, source_target_pairs={{8,0},{57,1},{16,8},{1,9},{24,16},{9,17},{32,24},{17,25},{40,32},{... | collective-permute-start | bytes 442376 | tf_op jit(solution)/shard_map/ppermute | solution.py:52
  46.4 6.1 %collective-permute-done.8 = bf16[32,1152]{1,0:T(8,128)(2,1)S(1)} collective-permute-done((bf16[32,1152]{1,0:T(8,128)(2,1)S(1)}, bf16[32,1152]{1,0:T(8,128)(2,1)S(1)}, u32[]{:S(2)}, u32[]{:S(2)}) %collective-permute-start.8) | collective-permute-done | bytes 73760 | tf_op jit(solution)/shard_map/ppermute | solution.py:52
  56.1 3.5 %shard_map.100 = (f32[64,1152]{1,0:T(8,128)S(1)}, bf16[224,1152]{1,0:T(8,128)(2,1)S(1)}, bf16[224,1152]{1,0:T(8,128)(2,1)S(1)}, bf16[512,1152]{1,0:T(8,128)(2,1)}) custom-call(f32[3]{0:T(128)S(1)} %pad_maximum_fusion.10.scalars, s32[2]{0:T(128)S(1)} %add_multiply_fusion.first, bf16[512,1152]{1,0:T(8,128)(2,1)S(1)} %pad_maximum_fusion.images, ...), custom_call_target="tpu_custom_call" | custom-call | flops 1811939328 | bytes 5898240 | tf_op jit(solution)/shard_map/pallas_call | solution.py:137
  59.6 6.9 %all-to-all-start.1 = ((bf16[16,32,1152]{2,1,0:T(8,128)(2,1)}), bf16[16,32,1152]{2,1,0:T(8,128)(2,1)S(1)}, u32[]{:S(2)}, u32[]{:S(2)}) async-start(bf16[16,32,1152]{2,1,0:T(8,128)(2,1)} %bitcast.23), calls=%async_computation.1 | async-start | bytes 2359296 | tf_op jit(solution)/shard_map/all_to_all | solution.py:56
  67.8 3.3 %collective-permute-start.11 = (bf16[32,1152]{1,0:T(8,128)(2,1)S(1)}, bf16[32,1152]{1,0:T(8,128)(2,1)S(1)}, u32[]{:S(2)}, u32[]{:S(2)}) collective-permute-start(bf16[32,1152]{1,0:T(8,128)(2,1)S(1)} %split.20), channel_id=1, source_target_pairs={{48,0},{17,1},{56,8},{25,9},{0,16},{33,17},{8,24},{41,25},{16,32},... | collective-permute-start | bytes 221192 | tf_op jit(solution)/shard_map/ppermute | solution.py:52
  73.0 3.8 %collective-permute-start.12 = (bf16[64,1152]{1,0:T(8,128)(2,1)S(1)}, bf16[64,1152]{1,0:T(8,128)(2,1)S(1)}, u32[]{:S(2)}, u32[]{:S(2)}) collective-permute-start(bf16[64,1152]{1,0:T(8,128)(2,1)S(1)} %get-tuple-element.38), channel_id=1, source_target_pairs={{56,0},{9,1},{0,8},{17,9},{8,16},{25,17},{16,24},{33,25},{24,32},{... | collective-permute-start | bytes 442376 | tf_op jit(solution)/shard_map/ppermute | solution.py:52
  79.0 4.5 %collective-permute-done.14 = bf16[64,1152]{1,0:T(8,128)(2,1)S(1)} collective-permute-done((bf16[64,1152]{1,0:T(8,128)(2,1)S(1)}, bf16[64,1152]{1,0:T(8,128)(2,1)S(1)}, u32[]{:S(2)}, u32[]{:S(2)}) %collective-permute-start.14) | collective-permute-done | bytes 147488 | tf_op jit(solution)/shard_map/ppermute | solution.py:52
  83.6 2.5 %collective-permute-start.15 = (bf16[32,1152]{1,0:T(8,128)(2,1)S(1)}, bf16[32,1152]{1,0:T(8,128)(2,1)S(1)}, u32[]{:S(2)}, u32[]{:S(2)}) collective-permute-start(bf16[32,1152]{1,0:T(8,128)(2,1)S(1)} %fusion.64), channel_id=1, source_target_pairs={{0,1},{1,0},{2,3},{3,2},{4,5},{5,4},{6,7},{7,6},{8,9},{9,8},{10,11... | collective-permute-start | bytes 221192 | tf_op jit(solution)/shard_map/ppermute | solution.py:60
  87.2 3.2 %collective-permute-start.16 = (bf16[2,32,1152]{2,1,0:T(8,128)(2,1)S(1)}, bf16[2,32,1152]{2,1,0:T(8,128)(2,1)S(1)}, u32[]{:S(2)}, u32[]{:S(2)}) collective-permute-start(bf16[2,32,1152]{2,1,0:T(8,128)(2,1)S(1)} %fusion.24), channel_id=1, source_target_pairs={{0,2},{2,0},{1,3},{3,1},{4,6},{6,4},{5,7},{7,5},{8,10},{10,8},{9,1... | collective-permute-start | bytes 442376 | tf_op jit(solution)/shard_map/ppermute | solution.py:60
  91.1 3.2 %collective-permute-done.16 = bf16[2,32,1152]{2,1,0:T(8,128)(2,1)S(1)} collective-permute-done((bf16[2,32,1152]{2,1,0:T(8,128)(2,1)S(1)}, bf16[2,32,1152]{2,1,0:T(8,128)(2,1)S(1)}, u32[]{:S(2)}, u32[]{:S(2)}) %collective-permute-start.16) | collective-permute-done | bytes 147488 | tf_op jit(solution)/shard_map/ppermute | solution.py:60
  96.8 4.2 %fusion.18 = bf16[2,128,1076]{1,2,0:T(8,128)(2,1)S(1)} fusion(f32[2,128,1076]{1,2,0:T(8,128)S(1)} %fusion.32, bf16[2,1076,1152]{2,0,1:T(2,128)(2,1)} %param.15, bf16[2,64,1152]{2,1,0:T(8,128)(2,1)S(1)} %get-tuple-element.52, bf16[2,64,1152]{2,1,0:T(8,128)(2,1)S(1)} %get-tuple-element.51), kind=kOutput, calls=%fused_computation.12 | convolution fusion | flops 636381184 | bytes 7200768 | tf_op jit(solution)/shard_map/kte,kfe->ktf/dot_general | solution.py:213
  101.0 2.4 %fusion.72 = (f32[2,128]{1,0:T(2,128)S(1)}, f32[2,128]{1,0:T(2,128)S(1)}, f32[2,128,1152]{1,2,0:T(8,128)S(1)}) fusion(f32[2,128]{1,0:T(2,128)S(1)} %add_rsqrt_fusion, f32[2,128]{1,0:T(2,128)S(1)} %broadcast_multiply_fusion.2, bf16[2,1152,128]{2,1,0:T(8,128)(2,1)S(1)} %bitcast.118, f32[2,1152]{1,0:T(2,128)S(1)} %convert_element_type.117, ...), kind=kOutput, calls=%fused_computation.125 | convolution fusion | flops 636714496 | bytes 7291904 | tf_op jit(solution)/shard_map/ktf,kdf->ktd/dot_general | solution.py:215
  105.5 3.1 %collective-permute-start.19 = (bf16[2,288,128]{2,1,0:T(8,128)(2,1)S(1)}, bf16[2,288,128]{2,1,0:T(8,128)(2,1)S(1)}, u32[]{:S(2)}, u32[]{:S(2)}) collective-permute-start(bf16[2,288,128]{2,1,0:T(8,128)(2,1)S(1)} %fusion.62), channel_id=1, source_target_pairs={{0,2},{2,0},{1,3},{3,1},{4,6},{6,4},{5,7},{7,5},{8,10},{10,8},{9,1... | collective-permute-start | bytes 442376 | tf_op jit(solution)/shard_map/ppermute | solution.py:60
  108.9 3.3 %collective-permute-done.19 = bf16[2,288,128]{2,1,0:T(8,128)(2,1)S(1)} collective-permute-done((bf16[2,288,128]{2,1,0:T(8,128)(2,1)S(1)}, bf16[2,288,128]{2,1,0:T(8,128)(2,1)S(1)}, u32[]{:S(2)}, u32[]{:S(2)}) %collective-permute-start.19) | collective-permute-done | bytes 147488 | tf_op jit(solution)/shard_map/ppermute | solution.py:60
  (101 shorter events, 24.2 us)
Async XLA Ops:
  0.0 6.4 %collective-permute-start = (bf16[2,288,128]{2,1,0:T(8,128)(2,1)}, bf16[2,288,128]{2,1,0:T(8,128)(2,1)S(1)}, u32[]{:S(2)}, u32[]{:S(2)}) collective-permute-start(bf16[2,288,128]{2,1,0:T(8,128)(2,1)} %bitcast.129), channel_id=1, source_target_pairs={{0,2},{2,0},{1,3},{3,1},{4,6},{6,4},{5,7},{7,5},{8,10},{10,8},{9,1... | collective-permute-start | bytes 442376 | tf_op jit(solution)/shard_map/ppermute | solution.py:60
  6.5 5.0 %collective-permute-start.1 = (bf16[2,2,1,288,128]{4,3,2,1,0:T(8,128)(2,1)S(1)}, bf16[2,2,1,288,128]{4,3,2,1,0:T(8,128)(2,1)S(1)}, u32[]{:S(2)}, u32[]{:S(2)}) collective-permute-start(bf16[2,2,1,288,128]{4,3,2,1,0:T(8,128)(2,1)S(1)} %maximum_add_fusion), channel_id=1, source_target_pairs={{0,1},{1,0},{2,3},{3,2},{4,5},{5,4},{6,7},{7,6},{8,9},{9,8},{10,11... | collective-permute-start | bytes 884744 | tf_op jit(solution)/shard_map/ppermute | solution.py:60
  11.8 4.9 %slice-start = ((s8[4958208]{0:T(1024)(128)(4,1)}), s8[4194304]{0:T(1024)(128)(4,1)S(1)}, s32[]{:S(2)}) async-start(s8[4958208]{0:T(1024)(128)(4,1)} %bitcast.131), calls=%async_computation.2 | async-start | bytes 8388608
  12.3 4.5 %slice-start.1 = ((s8[4958208]{0:T(1024)(128)(4,1)}), s8[763904]{0:T(1024)(128)(4,1)S(1)}, s32[]{:S(2)}) async-start(s8[4958208]{0:T(1024)(128)(4,1)} %bitcast.131), calls=%async_computation.3 | async-start | bytes 1527808
  18.1 1.7 %collective-permute-start.2 = (bf16[2,64,1152]{2,1,0:T(8,128)(2,1)S(1)}, bf16[2,64,1152]{2,1,0:T(8,128)(2,1)S(1)}, u32[]{:S(2)}, u32[]{:S(2)}) collective-permute-start(bf16[2,64,1152]{2,1,0:T(8,128)(2,1)S(1)} %fusion.51), channel_id=1, source_target_pairs={{0,1},{1,0},{2,3},{3,2},{4,5},{5,4},{6,7},{7,6},{8,9},{9,8},{10,11... | collective-permute-start | bytes 884744 | tf_op jit(solution)/shard_map/ppermute | solution.py:60
  19.8 6.7 %collective-permute-start.3 = (bf16[2,32,1152]{2,1,0:T(8,128)(2,1)S(1)}, bf16[2,32,1152]{2,1,0:T(8,128)(2,1)S(1)}, u32[]{:S(2)}, u32[]{:S(2)}) collective-permute-start(bf16[2,32,1152]{2,1,0:T(8,128)(2,1)S(1)} %fusion.61), channel_id=1, source_target_pairs={{0,2},{2,0},{1,3},{3,1},{4,6},{6,4},{5,7},{7,5},{8,10},{10,8},{9,1... | collective-permute-start | bytes 442376 | tf_op jit(solution)/shard_map/ppermute | solution.py:60
  26.8 7.9 %collective-permute-start.4 = (bf16[32,1152]{1,0:T(8,128)(2,1)S(1)}, bf16[32,1152]{1,0:T(8,128)(2,1)S(1)}, u32[]{:S(2)}, u32[]{:S(2)}) collective-permute-start(bf16[32,1152]{1,0:T(8,128)(2,1)S(1)} %get-tuple-element.62), channel_id=1, source_target_pairs={{0,1},{1,0},{2,3},{3,2},{4,5},{5,4},{6,7},{7,6},{8,9},{9,8},{10,11... | collective-permute-start | bytes 221192 | tf_op jit(solution)/shard_map/ppermute | solution.py:60
  29.2 23.3 %all-to-all-start = ((bf16[16,32,1152]{2,1,0:T(8,128)(2,1)}), bf16[16,32,1152]{2,1,0:T(8,128)(2,1)S(1)}, u32[]{:S(2)}, u32[]{:S(2)}) async-start(bf16[16,32,1152]{2,1,0:T(8,128)(2,1)} %broadcast_in_dim.4), calls=%async_computation | async-start | bytes 2359296 | tf_op jit(solution)/shard_map/all_to_all | solution.py:56
  34.7 9.0 %collective-permute-start.6 = (bf16[64,1152]{1,0:T(8,128)(2,1)S(1)}, bf16[64,1152]{1,0:T(8,128)(2,1)S(1)}, u32[]{:S(2)}, u32[]{:S(2)}) collective-permute-start(bf16[64,1152]{1,0:T(8,128)(2,1)S(1)} %pad_maximum_fusion.9), channel_id=1, source_target_pairs={{16,0},{49,1},{24,8},{57,9},{32,16},{1,17},{40,24},{9,25},{48,32},... | collective-permute-start | bytes 442376 | tf_op jit(solution)/shard_map/ppermute | solution.py:52
  37.8 8.6 %collective-permute-start.5 = (bf16[64,1152]{1,0:T(8,128)(2,1)S(1)}, bf16[64,1152]{1,0:T(8,128)(2,1)S(1)}, u32[]{:S(2)}, u32[]{:S(2)}) collective-permute-start(bf16[64,1152]{1,0:T(8,128)(2,1)S(1)} %pad_maximum_fusion.9), channel_id=1, source_target_pairs={{8,0},{57,1},{16,8},{1,9},{24,16},{9,17},{32,24},{17,25},{40,32},{... | collective-permute-start | bytes 442376 | tf_op jit(solution)/shard_map/ppermute | solution.py:52
  43.7 8.7 %collective-permute-start.7 = (bf16[64,1152]{1,0:T(8,128)(2,1)S(1)}, bf16[64,1152]{1,0:T(8,128)(2,1)S(1)}, u32[]{:S(2)}, u32[]{:S(2)}) collective-permute-start(bf16[64,1152]{1,0:T(8,128)(2,1)S(1)} %collective-permute-done.6), channel_id=1, source_target_pairs={{8,0},{57,1},{16,8},{1,9},{24,16},{9,17},{32,24},{17,25},{40,32},{... | collective-permute-start | bytes 442376 | tf_op jit(solution)/shard_map/ppermute | solution.py:52
  46.0 6.5 %collective-permute-start.8 = (bf16[32,1152]{1,0:T(8,128)(2,1)S(1)}, bf16[32,1152]{1,0:T(8,128)(2,1)S(1)}, u32[]{:S(2)}, u32[]{:S(2)}) collective-permute-start(bf16[32,1152]{1,0:T(8,128)(2,1)S(1)} %constant_dynamic-slice_fusion), channel_id=1, source_target_pairs={{16,0},{49,1},{24,8},{57,9},{32,16},{1,17},{40,24},{9,25},{48,32},... | collective-permute-start | bytes 221192 | tf_op jit(solution)/shard_map/ppermute | solution.py:52
  52.5 3.5 %collective-permute-start.9 = (bf16[224,1152]{1,0:T(8,128)(2,1)S(1)}, bf16[224,1152]{1,0:T(8,128)(2,1)S(1)}, u32[]{:S(2)}, u32[]{:S(2)}) collective-permute-start(bf16[224,1152]{1,0:T(8,128)(2,1)S(1)} %pad_maximum_fusion.4), channel_id=1, source_target_pairs={{0,1},{1,0},{2,3},{3,2},{4,5},{5,4},{6,7},{7,6},{8,9},{9,8},{10,11... | collective-permute-start | bytes 1548296 | tf_op jit(solution)/shard_map/ppermute | solution.py:60
  59.6 7.0 %collective-permute-start.10 = (bf16[224,1152]{1,0:T(8,128)(2,1)S(1)}, bf16[224,1152]{1,0:T(8,128)(2,1)}, u32[]{:S(2)}, u32[]{:S(2)}) collective-permute-start(bf16[224,1152]{1,0:T(8,128)(2,1)S(1)} %get-tuple-element.37), channel_id=1, source_target_pairs={{0,1},{1,0},{2,3},{3,2},{4,5},{5,4},{6,7},{7,6},{8,9},{9,8},{10,11... | collective-permute-start | bytes 1548296 | tf_op jit(solution)/shard_map/ppermute | solution.py:60
  59.6 23.9 %all-to-all-start.1 = ((bf16[16,32,1152]{2,1,0:T(8,128)(2,1)}), bf16[16,32,1152]{2,1,0:T(8,128)(2,1)S(1)}, u32[]{:S(2)}, u32[]{:S(2)}) async-start(bf16[16,32,1152]{2,1,0:T(8,128)(2,1)} %bitcast.23), calls=%async_computation.1 | async-start | bytes 2359296 | tf_op jit(solution)/shard_map/all_to_all | solution.py:56
  67.8 5.3 %collective-permute-start.11 = (bf16[32,1152]{1,0:T(8,128)(2,1)S(1)}, bf16[32,1152]{1,0:T(8,128)(2,1)S(1)}, u32[]{:S(2)}, u32[]{:S(2)}) collective-permute-start(bf16[32,1152]{1,0:T(8,128)(2,1)S(1)} %split.20), channel_id=1, source_target_pairs={{48,0},{17,1},{56,8},{25,9},{0,16},{33,17},{8,24},{41,25},{16,32},... | collective-permute-start | bytes 221192 | tf_op jit(solution)/shard_map/ppermute | solution.py:52
  71.1 5.8 %collective-permute-start.13 = (bf16[64,1152]{1,0:T(8,128)(2,1)S(1)}, bf16[64,1152]{1,0:T(8,128)(2,1)S(1)}, u32[]{:S(2)}, u32[]{:S(2)}) collective-permute-start(bf16[64,1152]{1,0:T(8,128)(2,1)S(1)} %get-tuple-element.55), channel_id=1, source_target_pairs={{56,0},{9,1},{0,8},{17,9},{8,16},{25,17},{16,24},{33,25},{24,32},{... | collective-permute-start | bytes 442376 | tf_op jit(solution)/shard_map/ppermute | solution.py:52
  73.0 5.9 %collective-permute-start.12 = (bf16[64,1152]{1,0:T(8,128)(2,1)S(1)}, bf16[64,1152]{1,0:T(8,128)(2,1)S(1)}, u32[]{:S(2)}, u32[]{:S(2)}) collective-permute-start(bf16[64,1152]{1,0:T(8,128)(2,1)S(1)} %get-tuple-element.38), channel_id=1, source_target_pairs={{56,0},{9,1},{0,8},{17,9},{8,16},{25,17},{16,24},{33,25},{24,32},{... | collective-permute-start | bytes 442376 | tf_op jit(solution)/shard_map/ppermute | solution.py:52
  77.0 6.5 %collective-permute-start.14 = (bf16[64,1152]{1,0:T(8,128)(2,1)S(1)}, bf16[64,1152]{1,0:T(8,128)(2,1)S(1)}, u32[]{:S(2)}, u32[]{:S(2)}) collective-permute-start(bf16[64,1152]{1,0:T(8,128)(2,1)S(1)} %fusion.54), channel_id=1, source_target_pairs={{48,0},{17,1},{56,8},{25,9},{0,16},{33,17},{8,24},{41,25},{16,32},... | collective-permute-start | bytes 442376 | tf_op jit(solution)/shard_map/ppermute | solution.py:52
  83.6 3.5 %collective-permute-start.15 = (bf16[32,1152]{1,0:T(8,128)(2,1)S(1)}, bf16[32,1152]{1,0:T(8,128)(2,1)S(1)}, u32[]{:S(2)}, u32[]{:S(2)}) collective-permute-start(bf16[32,1152]{1,0:T(8,128)(2,1)S(1)} %fusion.64), channel_id=1, source_target_pairs={{0,1},{1,0},{2,3},{3,2},{4,5},{5,4},{6,7},{7,6},{8,9},{9,8},{10,11... | collective-permute-start | bytes 221192 | tf_op jit(solution)/shard_map/ppermute | solution.py:60
  87.2 7.1 %collective-permute-start.16 = (bf16[2,32,1152]{2,1,0:T(8,128)(2,1)S(1)}, bf16[2,32,1152]{2,1,0:T(8,128)(2,1)S(1)}, u32[]{:S(2)}, u32[]{:S(2)}) collective-permute-start(bf16[2,32,1152]{2,1,0:T(8,128)(2,1)S(1)} %fusion.24), channel_id=1, source_target_pairs={{0,2},{2,0},{1,3},{3,1},{4,6},{6,4},{5,7},{7,5},{8,10},{10,8},{9,1... | collective-permute-start | bytes 442376 | tf_op jit(solution)/shard_map/ppermute | solution.py:60
  94.4 2.3 %collective-permute-start.17 = (bf16[2,64,1152]{2,1,0:T(8,128)(2,1)S(1)}, bf16[2,64,1152]{2,1,0:T(8,128)(2,1)S(1)}, u32[]{:S(2)}, u32[]{:S(2)}) collective-permute-start(bf16[2,64,1152]{2,1,0:T(8,128)(2,1)S(1)} %pad_maximum_fusion.7), channel_id=1, source_target_pairs={{0,1},{1,0},{2,3},{3,2},{4,5},{5,4},{6,7},{7,6},{8,9},{9,8},{10,11... | collective-permute-start | bytes 884744 | tf_op jit(solution)/shard_map/ppermute | solution.py:60
  103.7 1.7 %collective-permute-start.18 = (bf16[2,2,288,128]{3,2,1,0:T(8,128)(2,1)S(1)}, bf16[2,2,288,128]{3,2,1,0:T(8,128)(2,1)S(1)}, u32[]{:S(2)}, u32[]{:S(2)}) collective-permute-start(bf16[2,2,288,128]{3,2,1,0:T(8,128)(2,1)S(1)} %fusion.52), channel_id=1, source_target_pairs={{0,1},{1,0},{2,3},{3,2},{4,5},{5,4},{6,7},{7,6},{8,9},{9,8},{10,11... | collective-permute-start | bytes 884744 | tf_op jit(solution)/shard_map/ppermute | solution.py:60
  105.5 6.7 %collective-permute-start.19 = (bf16[2,288,128]{2,1,0:T(8,128)(2,1)S(1)}, bf16[2,288,128]{2,1,0:T(8,128)(2,1)S(1)}, u32[]{:S(2)}, u32[]{:S(2)}) collective-permute-start(bf16[2,288,128]{2,1,0:T(8,128)(2,1)S(1)} %fusion.62), channel_id=1, source_target_pairs={{0,2},{2,0},{1,3},{3,1},{4,6},{6,4},{5,7},{7,5},{8,10},{10,8},{9,1... | collective-permute-start | bytes 442376 | tf_op jit(solution)/shard_map/ppermute | solution.py:60
  (8 other events, 16.7 us)

commit v5 on v4

--- a/solution.py
+++ b/solution.py
@@ -97,15 +97,14 @@
     fetched = fetched.astype(F32) + swap(other, "c").astype(F32)
     one, two, three, four = jnp.split(fetched, [2 * half, 4 * half, 6 * half], axis=0)
     three = hop(three.astype(BF), -1).astype(F32)
-    four = hop(four.astype(BF), -2)
-    one, four = lax.optimization_barrier((one.astype(BF), four))
-    one = hop(one, -1).astype(F32)
-    four = four.astype(F32)
+    four = hop(four.astype(BF), -2).astype(F32)
     first = lax.axis_index("c") == 0
     none = jnp.zeros_like(four)
     two = two + three
     two = two + jnp.concatenate([jnp.where(first, four, none), jnp.where(first, none, four)])
-    two = hop(two.astype(BF), -2).astype(F32)
+    two, one = lax.optimization_barrier((two.astype(BF), one.astype(BF)))
+    two = hop(two, -2).astype(F32)
+    one = hop(one, -1).astype(F32)
     own, texts = lax.optimization_barrier((chip + one + two, texts))
     return swap_sum(own.reshape(2, half, -1), "c", 0), texts
 

time: 113 us -> 114 us (level)
  waiting for transfers between devices: 35.3 us -> 38.2 us
  starting transfers between devices: 50.9 us -> 48.4 us
    ppermute x8, waiting for transfers between devices: 17.2 us -> 20.1 us  [hop(): return as_lies(lax.ppermute(as_lies(block), ('z', 'c'), pairs))]
    ppermute x8, starting transfers between devices: 16.1 us -> 13.9 us  [hop(): return as_lies(lax.ppermute(as_lies(block), ('z', 'c'), pairs))]
  transfers between devices with their start and end apart: 22 -> 22, of which waited for: 15 -> 16; matrix products, arithmetic and copies ran while one was open for 5% -> 5% of each run, Pallas kernels for 0% -> 0%
where the time goes in v5:
time: 114 us; the launch traced here: 113 us
  starting transfers between devices  48.4 us (42%)
  waiting for transfers between devices  38.2 us (34%)
  matrix products  12.3 us (11%)
  other arithmetic  5.93 us (5%)
  Pallas kernels  3.5 us (3%)
  local copies, waits for them, and re-layouts  2.58 us (2%)
  between operations  2.4 us (2%)
    ppermute x12, starting transfers between devices, swap(): return as_lies(lax.ppermute(as_lies(block), axis, [(0, 1), (1, 0)]))  22.1 us
    ppermute x8, waiting for transfers between devices, hop(): return as_lies(lax.ppermute(as_lies(block), ('z', 'c'), pairs))  20.1 us
    ppermute x12, waiting for transfers between devices, swap(): return as_lies(lax.ppermute(as_lies(block), axis, [(0, 1), (1, 0)]))  18.1 us
    ppermute x8, starting transfers between devices, hop(): return as_lies(lax.ppermute(as_lies(block), ('z', 'c'), pairs))  13.9 us
    all_to_all x2, starting transfers between devices, exchange(): return lax.all_to_all(parts, axes, 0, 0, tiled=True)  12.4 us
    dot_general x1, matrix products, on_device(): preact = jnp.einsum('ktd,kdf->ktf', normed, fc1, preferred_element_type=F32)  4.43 us
    dot_general x1, matrix products, on_device(): jnp.einsum('kte,kfe->ktf', block_low, fc2, preferred_element_type=F32)  4.16 us
    pallas_call x1, Pallas kernels, loss_block(): pl.pallas_call(functools.partial(loss_kernel, part_rows), in_specs=[small...  3.5 us
  transfers between devices with their start and end apart: 22, of which 16 were waited for; matrix products, arithmetic and copies ran while one was open for 5% of the time, Pallas kernels for 0%

profile of v5, /device:TPU:1, one launch (start us, length us, event | category | flops | bytes accessed | tf_op | source)
XLA Modules:
  0.0 113.3 jit_solution(7337694234680706644)
XLA Ops:
  0.0 3.6 %collective-permute-start = (bf16[2,288,128]{2,1,0:T(8,128)(2,1)}, bf16[2,288,128]{2,1,0:T(8,128)(2,1)S(1)}, u32[]{:S(2)}, u32[]{:S(2)}) collective-permute-start(bf16[2,288,128]{2,1,0:T(8,128)(2,1)} %bitcast.129), channel_id=1, source_target_pairs={{0,2},{2,0},{1,3},{3,1},{4,6},{6,4},{5,7},{7,5},{8,10},{10,8},{9,1... | collective-permute-start | bytes 442376 | tf_op jit(solution)/shard_map/ppermute | solution.py:60
  4.6 1.8 %collective-permute-done = bf16[2,288,128]{2,1,0:T(8,128)(2,1)S(1)} collective-permute-done((bf16[2,288,128]{2,1,0:T(8,128)(2,1)}, bf16[2,288,128]{2,1,0:T(8,128)(2,1)S(1)}, u32[]{:S(2)}, u32[]{:S(2)}) %collective-permute-start) | collective-permute-done | bytes 147488 | tf_op jit(solution)/shard_map/ppermute | solution.py:60
  6.5 3.8 %collective-permute-start.1 = (bf16[2,2,1,288,128]{4,3,2,1,0:T(8,128)(2,1)S(1)}, bf16[2,2,1,288,128]{4,3,2,1,0:T(8,128)(2,1)S(1)}, u32[]{:S(2)}, u32[]{:S(2)}) collective-permute-start(bf16[2,2,1,288,128]{4,3,2,1,0:T(8,128)(2,1)S(1)} %maximum_add_fusion), channel_id=1, source_target_pairs={{0,1},{1,0},{2,3},{3,2},{4,5},{5,4},{6,7},{7,6},{8,9},{9,8},{10,11... | collective-permute-start | bytes 884744 | tf_op jit(solution)/shard_map/ppermute | solution.py:60
  12.3 4.4 %fusion.9 = f32[2,128,1076]{1,2,0:T(8,128)S(1)} fusion(bf16[2,1152,1076]{1,0,2:T(2,128)(2,1)} %param.13, bf16[2,1152,128]{2,1,0:T(8,128)(2,1)S(1)} %bitcast.116, f32[2,1152]{1,0:T(2,128)S(1)} %convert_element_type.118, f32[2,1152]{1,0:T(2,128)S(1)} %convert_element_type.117, f32[2,128]{1,0:T(2,128)S(1)} %add_rsqrt_fusion, ...), kind=kOutput, calls=%fused_computation.9 | convolution fusion | flops 636695552 | bytes 6678944 | tf_op jit(solution)/shard_map/ktd,kdf->ktf/dot_general | solution.py:178
  22.1 4.4 %collective-permute-done.3 = bf16[2,32,1152]{2,1,0:T(8,128)(2,1)S(1)} collective-permute-done((bf16[2,32,1152]{2,1,0:T(8,128)(2,1)S(1)}, bf16[2,32,1152]{2,1,0:T(8,128)(2,1)S(1)}, u32[]{:S(2)}, u32[]{:S(2)}) %collective-permute-start.3) | collective-permute-done | bytes 147488 | tf_op jit(solution)/shard_map/ppermute | solution.py:60
  29.2 5.5 %all-to-all-start = ((bf16[16,32,1152]{2,1,0:T(8,128)(2,1)}), bf16[16,32,1152]{2,1,0:T(8,128)(2,1)S(1)}, u32[]{:S(2)}, u32[]{:S(2)}) async-start(bf16[16,32,1152]{2,1,0:T(8,128)(2,1)} %broadcast_in_dim.4), calls=%async_computation | async-start | bytes 2359296 | tf_op jit(solution)/shard_map/all_to_all | solution.py:56
  34.7 3.1 %collective-permute-start.6 = (bf16[64,1152]{1,0:T(8,128)(2,1)S(1)}, bf16[64,1152]{1,0:T(8,128)(2,1)S(1)}, u32[]{:S(2)}, u32[]{:S(2)}) collective-permute-start(bf16[64,1152]{1,0:T(8,128)(2,1)S(1)} %pad_maximum_fusion.9), channel_id=1, source_target_pairs={{16,0},{49,1},{24,8},{57,9},{32,16},{1,17},{40,24},{9,25},{48,32},... | collective-permute-start | bytes 442376 | tf_op jit(solution)/shard_map/ppermute | solution.py:52
  39.4 4.3 %collective-permute-done.6 = bf16[64,1152]{1,0:T(8,128)(2,1)S(1)} collective-permute-done((bf16[64,1152]{1,0:T(8,128)(2,1)S(1)}, bf16[64,1152]{1,0:T(8,128)(2,1)S(1)}, u32[]{:S(2)}, u32[]{:S(2)}) %collective-permute-start.6) | collective-permute-done | bytes 147488 | tf_op jit(solution)/shard_map/ppermute | solution.py:52
  43.7 2.3 %collective-permute-start.7 = (bf16[64,1152]{1,0:T(8,128)(2,1)S(1)}, bf16[64,1152]{1,0:T(8,128)(2,1)S(1)}, u32[]{:S(2)}, u32[]{:S(2)}) collective-permute-start(bf16[64,1152]{1,0:T(8,128)(2,1)S(1)} %collective-permute-done.6), channel_id=1, source_target_pairs={{8,0},{57,1},{16,8},{1,9},{24,16},{9,17},{32,24},{17,25},{40,32},{... | collective-permute-start | bytes 442376 | tf_op jit(solution)/shard_map/ppermute | solution.py:52
  46.4 6.1 %collective-permute-done.8 = bf16[32,1152]{1,0:T(8,128)(2,1)S(1)} collective-permute-done((bf16[32,1152]{1,0:T(8,128)(2,1)S(1)}, bf16[32,1152]{1,0:T(8,128)(2,1)S(1)}, u32[]{:S(2)}, u32[]{:S(2)}) %collective-permute-start.8) | collective-permute-done | bytes 73760 | tf_op jit(solution)/shard_map/ppermute | solution.py:52
  56.1 3.5 %shard_map.100 = (f32[64,1152]{1,0:T(8,128)S(1)}, bf16[224,1152]{1,0:T(8,128)(2,1)S(1)}, bf16[224,1152]{1,0:T(8,128)(2,1)S(1)}, bf16[512,1152]{1,0:T(8,128)(2,1)}) custom-call(f32[3]{0:T(128)S(1)} %pad_maximum_fusion.10.scalars, s32[2]{0:T(128)S(1)} %add_multiply_fusion.first, bf16[512,1152]{1,0:T(8,128)(2,1)S(1)} %pad_maximum_fusion.images, ...), custom_call_target="tpu_custom_call" | custom-call | flops 1811939328 | bytes 5898240 | tf_op jit(solution)/shard_map/pallas_call | solution.py:136
  59.6 6.9 %all-to-all-start.1 = ((bf16[16,32,1152]{2,1,0:T(8,128)(2,1)}), bf16[16,32,1152]{2,1,0:T(8,128)(2,1)S(1)}, u32[]{:S(2)}, u32[]{:S(2)}) async-start(bf16[16,32,1152]{2,1,0:T(8,128)(2,1)} %bitcast.23), calls=%async_computation.1 | async-start | bytes 2359296 | tf_op jit(solution)/shard_map/all_to_all | solution.py:56
  67.8 3.3 %collective-permute-start.12 = (bf16[32,1152]{1,0:T(8,128)(2,1)S(1)}, bf16[32,1152]{1,0:T(8,128)(2,1)S(1)}, u32[]{:S(2)}, u32[]{:S(2)}) collective-permute-start(bf16[32,1152]{1,0:T(8,128)(2,1)S(1)} %split.21), channel_id=1, source_target_pairs={{48,0},{17,1},{56,8},{25,9},{0,16},{33,17},{8,24},{41,25},{16,32},... | collective-permute-start | bytes 221192 | tf_op jit(solution)/shard_map/ppermute | solution.py:52
  73.1 3.0 %collective-permute-done.11 = bf16[64,1152]{1,0:T(8,128)(2,1)S(1)} collective-permute-done((bf16[64,1152]{1,0:T(8,128)(2,1)S(1)}, bf16[64,1152]{1,0:T(8,128)(2,1)S(1)}, u32[]{:S(2)}, u32[]{:S(2)}) %collective-permute-start.11) | collective-permute-done | bytes 147488 | tf_op jit(solution)/shard_map/ppermute | solution.py:52
  76.1 2.5 %collective-permute-start.13 = (bf16[64,1152]{1,0:T(8,128)(2,1)S(1)}, bf16[64,1152]{1,0:T(8,128)(2,1)S(1)}, u32[]{:S(2)}, u32[]{:S(2)}) collective-permute-start(bf16[64,1152]{1,0:T(8,128)(2,1)S(1)} %get-tuple-element.38), channel_id=1, source_target_pairs={{56,0},{9,1},{0,8},{17,9},{8,16},{25,17},{16,24},{33,25},{24,32},{... | collective-permute-start | bytes 442376 | tf_op jit(solution)/shard_map/ppermute | solution.py:52
  78.6 3.6 %collective-permute-done.13 = bf16[64,1152]{1,0:T(8,128)(2,1)S(1)} collective-permute-done((bf16[64,1152]{1,0:T(8,128)(2,1)S(1)}, bf16[64,1152]{1,0:T(8,128)(2,1)S(1)}, u32[]{:S(2)}, u32[]{:S(2)}) %collective-permute-start.13) | collective-permute-done | bytes 147488 | tf_op jit(solution)/shard_map/ppermute | solution.py:52
  82.2 2.0 %collective-permute-done.14 = bf16[64,1152]{1,0:T(8,128)(2,1)S(1)} collective-permute-done((bf16[64,1152]{1,0:T(8,128)(2,1)S(1)}, bf16[64,1152]{1,0:T(8,128)(2,1)S(1)}, u32[]{:S(2)}, u32[]{:S(2)}) %collective-permute-start.14) | collective-permute-done | bytes 147488 | tf_op jit(solution)/shard_map/ppermute | solution.py:52
  84.3 2.2 %collective-permute-start.15 = (bf16[32,1152]{1,0:T(8,128)(2,1)S(1)}, bf16[32,1152]{1,0:T(8,128)(2,1)S(1)}, u32[]{:S(2)}, u32[]{:S(2)}) collective-permute-start(bf16[32,1152]{1,0:T(8,128)(2,1)S(1)} %fusion.64), channel_id=1, source_target_pairs={{0,1},{1,0},{2,3},{3,2},{4,5},{5,4},{6,7},{7,6},{8,9},{9,8},{10,11... | collective-permute-start | bytes 221192 | tf_op jit(solution)/shard_map/ppermute | solution.py:60
  87.6 3.2 %collective-permute-start.16 = (bf16[2,32,1152]{2,1,0:T(8,128)(2,1)S(1)}, bf16[2,32,1152]{2,1,0:T(8,128)(2,1)S(1)}, u32[]{:S(2)}, u32[]{:S(2)}) collective-permute-start(bf16[2,32,1152]{2,1,0:T(8,128)(2,1)S(1)} %fusion.24), channel_id=1, source_target_pairs={{0,2},{2,0},{1,3},{3,1},{4,6},{6,4},{5,7},{7,5},{8,10},{10,8},{9,1... | collective-permute-start | bytes 442376 | tf_op jit(solution)/shard_map/ppermute | solution.py:60
  91.5 3.2 %collective-permute-done.16 = bf16[2,32,1152]{2,1,0:T(8,128)(2,1)S(1)} collective-permute-done((bf16[2,32,1152]{2,1,0:T(8,128)(2,1)S(1)}, bf16[2,32,1152]{2,1,0:T(8,128)(2,1)S(1)}, u32[]{:S(2)}, u32[]{:S(2)}) %collective-permute-start.16) | collective-permute-done | bytes 147488 | tf_op jit(solution)/shard_map/ppermute | solution.py:60
  97.1 4.2 %fusion.18 = bf16[2,128,1076]{1,2,0:T(8,128)(2,1)S(1)} fusion(f32[2,128,1076]{1,2,0:T(8,128)S(1)} %fusion.32, bf16[2,1076,1152]{2,0,1:T(2,128)(2,1)} %param.15, bf16[2,64,1152]{2,1,0:T(8,128)(2,1)S(1)} %get-tuple-element.52, bf16[2,64,1152]{2,1,0:T(8,128)(2,1)S(1)} %get-tuple-element.51), kind=kOutput, calls=%fused_computation.12 | convolution fusion | flops 636381184 | bytes 7200768 | tf_op jit(solution)/shard_map/kte,kfe->ktf/dot_general | solution.py:212
  101.3 2.4 %fusion.72 = (f32[2,128]{1,0:T(2,128)S(1)}, f32[2,128]{1,0:T(2,128)S(1)}, f32[2,128,1152]{1,2,0:T(8,128)S(1)}) fusion(f32[2,128]{1,0:T(2,128)S(1)} %add_rsqrt_fusion, f32[2,128]{1,0:T(2,128)S(1)} %broadcast_multiply_fusion.2, bf16[2,1152,128]{2,1,0:T(8,128)(2,1)S(1)} %bitcast.118, f32[2,1152]{1,0:T(2,128)S(1)} %convert_element_type.117, ...), kind=kOutput, calls=%fused_computation.125 | convolution fusion | flops 636714496 | bytes 7291904 | tf_op jit(solution)/shard_map/ktf,kdf->ktd/dot_general | solution.py:214
  105.9 3.1 %collective-permute-start.19 = (bf16[2,288,128]{2,1,0:T(8,128)(2,1)S(1)}, bf16[2,288,128]{2,1,0:T(8,128)(2,1)S(1)}, u32[]{:S(2)}, u32[]{:S(2)}) collective-permute-start(bf16[2,288,128]{2,1,0:T(8,128)(2,1)S(1)} %fusion.62), channel_id=1, source_target_pairs={{0,2},{2,0},{1,3},{3,1},{4,6},{6,4},{5,7},{7,5},{8,10},{10,8},{9,1... | collective-permute-start | bytes 442376 | tf_op jit(solution)/shard_map/ppermute | solution.py:60
  109.3 3.3 %collective-permute-done.19 = bf16[2,288,128]{2,1,0:T(8,128)(2,1)S(1)} collective-permute-done((bf16[2,288,128]{2,1,0:T(8,128)(2,1)S(1)}, bf16[2,288,128]{2,1,0:T(8,128)(2,1)S(1)}, u32[]{:S(2)}, u32[]{:S(2)}) %collective-permute-start.19) | collective-permute-done | bytes 147488 | tf_op jit(solution)/shard_map/ppermute | solution.py:60
  (101 shorter events, 25.4 us)
Async XLA Ops:
  0.0 6.4 %collective-permute-start = (bf16[2,288,128]{2,1,0:T(8,128)(2,1)}, bf16[2,288,128]{2,1,0:T(8,128)(2,1)S(1)}, u32[]{:S(2)}, u32[]{:S(2)}) collective-permute-start(bf16[2,288,128]{2,1,0:T(8,128)(2,1)} %bitcast.129), channel_id=1, source_target_pairs={{0,2},{2,0},{1,3},{3,1},{4,6},{6,4},{5,7},{7,5},{8,10},{10,8},{9,1... | collective-permute-start | bytes 442376 | tf_op jit(solution)/shard_map/ppermute | solution.py:60
  6.5 5.0 %collective-permute-start.1 = (bf16[2,2,1,288,128]{4,3,2,1,0:T(8,128)(2,1)S(1)}, bf16[2,2,1,288,128]{4,3,2,1,0:T(8,128)(2,1)S(1)}, u32[]{:S(2)}, u32[]{:S(2)}) collective-permute-start(bf16[2,2,1,288,128]{4,3,2,1,0:T(8,128)(2,1)S(1)} %maximum_add_fusion), channel_id=1, source_target_pairs={{0,1},{1,0},{2,3},{3,2},{4,5},{5,4},{6,7},{7,6},{8,9},{9,8},{10,11... | collective-permute-start | bytes 884744 | tf_op jit(solution)/shard_map/ppermute | solution.py:60
  11.8 4.9 %slice-start = ((s8[4958208]{0:T(1024)(128)(4,1)}), s8[4194304]{0:T(1024)(128)(4,1)S(1)}, s32[]{:S(2)}) async-start(s8[4958208]{0:T(1024)(128)(4,1)} %bitcast.131), calls=%async_computation.2 | async-start | bytes 8388608
  12.3 4.5 %slice-start.1 = ((s8[4958208]{0:T(1024)(128)(4,1)}), s8[763904]{0:T(1024)(128)(4,1)S(1)}, s32[]{:S(2)}) async-start(s8[4958208]{0:T(1024)(128)(4,1)} %bitcast.131), calls=%async_computation.3 | async-start | bytes 1527808
  18.1 1.7 %collective-permute-start.2 = (bf16[2,64,1152]{2,1,0:T(8,128)(2,1)S(1)}, bf16[2,64,1152]{2,1,0:T(8,128)(2,1)S(1)}, u32[]{:S(2)}, u32[]{:S(2)}) collective-permute-start(bf16[2,64,1152]{2,1,0:T(8,128)(2,1)S(1)} %fusion.51), channel_id=1, source_target_pairs={{0,1},{1,0},{2,3},{3,2},{4,5},{5,4},{6,7},{7,6},{8,9},{9,8},{10,11... | collective-permute-start | bytes 884744 | tf_op jit(solution)/shard_map/ppermute | solution.py:60
  19.8 6.7 %collective-permute-start.3 = (bf16[2,32,1152]{2,1,0:T(8,128)(2,1)S(1)}, bf16[2,32,1152]{2,1,0:T(8,128)(2,1)S(1)}, u32[]{:S(2)}, u32[]{:S(2)}) collective-permute-start(bf16[2,32,1152]{2,1,0:T(8,128)(2,1)S(1)} %fusion.61), channel_id=1, source_target_pairs={{0,2},{2,0},{1,3},{3,1},{4,6},{6,4},{5,7},{7,5},{8,10},{10,8},{9,1... | collective-permute-start | bytes 442376 | tf_op jit(solution)/shard_map/ppermute | solution.py:60
  26.8 7.9 %collective-permute-start.4 = (bf16[32,1152]{1,0:T(8,128)(2,1)S(1)}, bf16[32,1152]{1,0:T(8,128)(2,1)S(1)}, u32[]{:S(2)}, u32[]{:S(2)}) collective-permute-start(bf16[32,1152]{1,0:T(8,128)(2,1)S(1)} %get-tuple-element.62), channel_id=1, source_target_pairs={{0,1},{1,0},{2,3},{3,2},{4,5},{5,4},{6,7},{7,6},{8,9},{9,8},{10,11... | collective-permute-start | bytes 221192 | tf_op jit(solution)/shard_map/ppermute | solution.py:60
  29.2 23.3 %all-to-all-start = ((bf16[16,32,1152]{2,1,0:T(8,128)(2,1)}), bf16[16,32,1152]{2,1,0:T(8,128)(2,1)S(1)}, u32[]{:S(2)}, u32[]{:S(2)}) async-start(bf16[16,32,1152]{2,1,0:T(8,128)(2,1)} %broadcast_in_dim.4), calls=%async_computation | async-start | bytes 2359296 | tf_op jit(solution)/shard_map/all_to_all | solution.py:56
  34.7 9.0 %collective-permute-start.6 = (bf16[64,1152]{1,0:T(8,128)(2,1)S(1)}, bf16[64,1152]{1,0:T(8,128)(2,1)S(1)}, u32[]{:S(2)}, u32[]{:S(2)}) collective-permute-start(bf16[64,1152]{1,0:T(8,128)(2,1)S(1)} %pad_maximum_fusion.9), channel_id=1, source_target_pairs={{16,0},{49,1},{24,8},{57,9},{32,16},{1,17},{40,24},{9,25},{48,32},... | collective-permute-start | bytes 442376 | tf_op jit(solution)/shard_map/ppermute | solution.py:52
  37.8 8.6 %collective-permute-start.5 = (bf16[64,1152]{1,0:T(8,128)(2,1)S(1)}, bf16[64,1152]{1,0:T(8,128)(2,1)S(1)}, u32[]{:S(2)}, u32[]{:S(2)}) collective-permute-start(bf16[64,1152]{1,0:T(8,128)(2,1)S(1)} %pad_maximum_fusion.9), channel_id=1, source_target_pairs={{8,0},{57,1},{16,8},{1,9},{24,16},{9,17},{32,24},{17,25},{40,32},{... | collective-permute-start | bytes 442376 | tf_op jit(solution)/shard_map/ppermute | solution.py:52
  43.7 8.7 %collective-permute-start.7 = (bf16[64,1152]{1,0:T(8,128)(2,1)S(1)}, bf16[64,1152]{1,0:T(8,128)(2,1)S(1)}, u32[]{:S(2)}, u32[]{:S(2)}) collective-permute-start(bf16[64,1152]{1,0:T(8,128)(2,1)S(1)} %collective-permute-done.6), channel_id=1, source_target_pairs={{8,0},{57,1},{16,8},{1,9},{24,16},{9,17},{32,24},{17,25},{40,32},{... | collective-permute-start | bytes 442376 | tf_op jit(solution)/shard_map/ppermute | solution.py:52
  46.0 6.5 %collective-permute-start.8 = (bf16[32,1152]{1,0:T(8,128)(2,1)S(1)}, bf16[32,1152]{1,0:T(8,128)(2,1)S(1)}, u32[]{:S(2)}, u32[]{:S(2)}) collective-permute-start(bf16[32,1152]{1,0:T(8,128)(2,1)S(1)} %constant_dynamic-slice_fusion), channel_id=1, source_target_pairs={{16,0},{49,1},{24,8},{57,9},{32,16},{1,17},{40,24},{9,25},{48,32},... | collective-permute-start | bytes 221192 | tf_op jit(solution)/shard_map/ppermute | solution.py:52
  52.5 3.5 %collective-permute-start.9 = (bf16[224,1152]{1,0:T(8,128)(2,1)S(1)}, bf16[224,1152]{1,0:T(8,128)(2,1)S(1)}, u32[]{:S(2)}, u32[]{:S(2)}) collective-permute-start(bf16[224,1152]{1,0:T(8,128)(2,1)S(1)} %pad_maximum_fusion.4), channel_id=1, source_target_pairs={{0,1},{1,0},{2,3},{3,2},{4,5},{5,4},{6,7},{7,6},{8,9},{9,8},{10,11... | collective-permute-start | bytes 1548296 | tf_op jit(solution)/shard_map/ppermute | solution.py:60
  59.6 7.0 %collective-permute-start.10 = (bf16[224,1152]{1,0:T(8,128)(2,1)S(1)}, bf16[224,1152]{1,0:T(8,128)(2,1)}, u32[]{:S(2)}, u32[]{:S(2)}) collective-permute-start(bf16[224,1152]{1,0:T(8,128)(2,1)S(1)} %get-tuple-element.37), channel_id=1, source_target_pairs={{0,1},{1,0},{2,3},{3,2},{4,5},{5,4},{6,7},{7,6},{8,9},{9,8},{10,11... | collective-permute-start | bytes 1548296 | tf_op jit(solution)/shard_map/ppermute | solution.py:60
  59.6 24.6 %all-to-all-start.1 = ((bf16[16,32,1152]{2,1,0:T(8,128)(2,1)}), bf16[16,32,1152]{2,1,0:T(8,128)(2,1)S(1)}, u32[]{:S(2)}, u32[]{:S(2)}) async-start(bf16[16,32,1152]{2,1,0:T(8,128)(2,1)} %bitcast.23), calls=%async_computation.1 | async-start | bytes 2359296 | tf_op jit(solution)/shard_map/all_to_all | solution.py:56
  67.8 5.3 %collective-permute-start.12 = (bf16[32,1152]{1,0:T(8,128)(2,1)S(1)}, bf16[32,1152]{1,0:T(8,128)(2,1)S(1)}, u32[]{:S(2)}, u32[]{:S(2)}) collective-permute-start(bf16[32,1152]{1,0:T(8,128)(2,1)S(1)} %split.21), channel_id=1, source_target_pairs={{48,0},{17,1},{56,8},{25,9},{0,16},{33,17},{8,24},{41,25},{16,32},... | collective-permute-start | bytes 221192 | tf_op jit(solution)/shard_map/ppermute | solution.py:52
  71.1 5.0 %collective-permute-start.11 = (bf16[64,1152]{1,0:T(8,128)(2,1)S(1)}, bf16[64,1152]{1,0:T(8,128)(2,1)S(1)}, u32[]{:S(2)}, u32[]{:S(2)}) collective-permute-start(bf16[64,1152]{1,0:T(8,128)(2,1)S(1)} %get-tuple-element.56), channel_id=1, source_target_pairs={{56,0},{9,1},{0,8},{17,9},{8,16},{25,17},{16,24},{33,25},{24,32},{... | collective-permute-start | bytes 442376 | tf_op jit(solution)/shard_map/ppermute | solution.py:52
  76.1 6.1 %collective-permute-start.13 = (bf16[64,1152]{1,0:T(8,128)(2,1)S(1)}, bf16[64,1152]{1,0:T(8,128)(2,1)S(1)}, u32[]{:S(2)}, u32[]{:S(2)}) collective-permute-start(bf16[64,1152]{1,0:T(8,128)(2,1)S(1)} %get-tuple-element.38), channel_id=1, source_target_pairs={{56,0},{9,1},{0,8},{17,9},{8,16},{25,17},{16,24},{33,25},{24,32},{... | collective-permute-start | bytes 442376 | tf_op jit(solution)/shard_map/ppermute | solution.py:52
  78.6 5.6 %collective-permute-start.14 = (bf16[64,1152]{1,0:T(8,128)(2,1)S(1)}, bf16[64,1152]{1,0:T(8,128)(2,1)S(1)}, u32[]{:S(2)}, u32[]{:S(2)}) collective-permute-start(bf16[64,1152]{1,0:T(8,128)(2,1)S(1)} %fusion.54), channel_id=1, source_target_pairs={{48,0},{17,1},{56,8},{25,9},{0,16},{33,17},{8,24},{41,25},{16,32},... | collective-permute-start | bytes 442376 | tf_op jit(solution)/shard_map/ppermute | solution.py:52
  84.3 3.1 %collective-permute-start.15 = (bf16[32,1152]{1,0:T(8,128)(2,1)S(1)}, bf16[32,1152]{1,0:T(8,128)(2,1)S(1)}, u32[]{:S(2)}, u32[]{:S(2)}) collective-permute-start(bf16[32,1152]{1,0:T(8,128)(2,1)S(1)} %fusion.64), channel_id=1, source_target_pairs={{0,1},{1,0},{2,3},{3,2},{4,5},{5,4},{6,7},{7,6},{8,9},{9,8},{10,11... | collective-permute-start | bytes 221192 | tf_op jit(solution)/shard_map/ppermute | solution.py:60
  87.6 7.1 %collective-permute-start.16 = (bf16[2,32,1152]{2,1,0:T(8,128)(2,1)S(1)}, bf16[2,32,1152]{2,1,0:T(8,128)(2,1)S(1)}, u32[]{:S(2)}, u32[]{:S(2)}) collective-permute-start(bf16[2,32,1152]{2,1,0:T(8,128)(2,1)S(1)} %fusion.24), channel_id=1, source_target_pairs={{0,2},{2,0},{1,3},{3,1},{4,6},{6,4},{5,7},{7,5},{8,10},{10,8},{9,1... | collective-permute-start | bytes 442376 | tf_op jit(solution)/shard_map/ppermute | solution.py:60
  94.7 2.3 %collective-permute-start.17 = (bf16[2,64,1152]{2,1,0:T(8,128)(2,1)S(1)}, bf16[2,64,1152]{2,1,0:T(8,128)(2,1)S(1)}, u32[]{:S(2)}, u32[]{:S(2)}) collective-permute-start(bf16[2,64,1152]{2,1,0:T(8,128)(2,1)S(1)} %pad_maximum_fusion.7), channel_id=1, source_target_pairs={{0,1},{1,0},{2,3},{3,2},{4,5},{5,4},{6,7},{7,6},{8,9},{9,8},{10,11... | collective-permute-start | bytes 884744 | tf_op jit(solution)/shard_map/ppermute | solution.py:60
  104.1 1.7 %collective-permute-start.18 = (bf16[2,2,288,128]{3,2,1,0:T(8,128)(2,1)S(1)}, bf16[2,2,288,128]{3,2,1,0:T(8,128)(2,1)S(1)}, u32[]{:S(2)}, u32[]{:S(2)}) collective-permute-start(bf16[2,2,288,128]{3,2,1,0:T(8,128)(2,1)S(1)} %fusion.52), channel_id=1, source_target_pairs={{0,1},{1,0},{2,3},{3,2},{4,5},{5,4},{6,7},{7,6},{8,9},{9,8},{10,11... | collective-permute-start | bytes 884744 | tf_op jit(solution)/shard_map/ppermute | solution.py:60
  105.9 6.7 %collective-permute-start.19 = (bf16[2,288,128]{2,1,0:T(8,128)(2,1)S(1)}, bf16[2,288,128]{2,1,0:T(8,128)(2,1)S(1)}, u32[]{:S(2)}, u32[]{:S(2)}) collective-permute-start(bf16[2,288,128]{2,1,0:T(8,128)(2,1)S(1)} %fusion.62), channel_id=1, source_target_pairs={{0,2},{2,0},{1,3},{3,1},{4,6},{6,4},{5,7},{7,5},{8,10},{10,8},{9,1... | collective-permute-start | bytes 442376 | tf_op jit(solution)/shard_map/ppermute | solution.py:60
  (8 other events, 16.7 us)

commit v6 on v4

--- a/solution.py
+++ b/solution.py
@@ -82,11 +82,10 @@
 
 
 def gather_ring(own, texts):
-    half = own.shape[0]
     chip = swap_join(own, "c", 0)
     one, two = hop(chip, 1), hop(chip, 2)
     three = hop(two, 1)
-    four = hop(lax.dynamic_slice_in_dim(two, lax.axis_index("c") * half, half, 0), 2)
+    four = hop(own, 4)
     fetched = jnp.concatenate([one, two, three, four], axis=0)
     fetched, texts = lax.optimization_barrier((fetched, texts))
     return jnp.concatenate([chip, fetched, swap(fetched, "c")], axis=0), texts

time: 113 us -> 115 us (1.018)
  starting transfers between devices: 50.9 us -> 53.7 us
    ppermute x12, starting transfers between devices: 22.4 us -> 24 us  [swap(): return as_lies(lax.ppermute(as_lies(block), axis, [(0, 1), (1, 0)]))]
    ppermute x8, waiting for transfers between devices: 17.2 us -> 15.9 us  [hop(): return as_lies(lax.ppermute(as_lies(block), ('z', 'c'), pairs))]
    ppermute x8, starting transfers between devices: 16.1 us -> 17.3 us  [hop(): return as_lies(lax.ppermute(as_lies(block), ('z', 'c'), pairs))]
where the time goes in v6:
time: 115 us
  starting transfers between devices  53.7 us (47%)
  waiting for transfers between devices  34.4 us (30%)
  matrix products  12.3 us (11%)
  other arithmetic  5.93 us (5%)
  Pallas kernels  3.5 us (3%)
  local copies, waits for them, and re-layouts  2.57 us (2%)
  between operations  2.4 us (2%)
    ppermute x12, starting transfers between devices, swap(): return as_lies(lax.ppermute(as_lies(block), axis, [(0, 1), (1, 0)]))  24 us
    ppermute x12, waiting for transfers between devices, swap(): return as_lies(lax.ppermute(as_lies(block), axis, [(0, 1), (1, 0)]))  18.2 us
    ppermute x8, starting transfers between devices, hop(): return as_lies(lax.ppermute(as_lies(block), ('z', 'c'), pairs))  17.3 us
    ppermute x8, waiting for transfers between devices, hop(): return as_lies(lax.ppermute(as_lies(block), ('z', 'c'), pairs))  15.9 us
    all_to_all x2, starting transfers between devices, exchange(): return lax.all_to_all(parts, axes, 0, 0, tiled=True)  12.3 us
    dot_general x1, matrix products, on_device(): preact = jnp.einsum('ktd,kdf->ktf', normed, fc1, preferred_element_type=F32)  4.43 us
    dot_general x1, matrix products, on_device(): jnp.einsum('kte,kfe->ktf', block_low, fc2, preferred_element_type=F32)  4.16 us
    pallas_call x1, Pallas kernels, loss_block(): pl.pallas_call(functools.partial(loss_kernel, part_rows), in_specs=[small...  3.5 us
  transfers between devices with their start and end apart: 22, of which 15 were waited for; matrix products, arithmetic and copies ran while one was open for 5% of the time, Pallas kernels for 0%

profile of v6, /device:TPU:1, one launch (start us, length us, event | category | flops | bytes accessed | tf_op | source)
XLA Modules:
  0.0 114.7 jit_solution(7123686949041079567)
XLA Ops:
  0.0 3.6 %collective-permute-start = (bf16[2,288,128]{2,1,0:T(8,128)(2,1)}, bf16[2,288,128]{2,1,0:T(8,128)(2,1)S(1)}, u32[]{:S(2)}, u32[]{:S(2)}) collective-permute-start(bf16[2,288,128]{2,1,0:T(8,128)(2,1)} %bitcast.129), channel_id=1, source_target_pairs={{0,2},{2,0},{1,3},{3,1},{4,6},{6,4},{5,7},{7,5},{8,10},{10,8},{9,1... | collective-permute-start | bytes 442376 | tf_op jit(solution)/shard_map/ppermute | solution.py:60
  4.6 1.8 %collective-permute-done = bf16[2,288,128]{2,1,0:T(8,128)(2,1)S(1)} collective-permute-done((bf16[2,288,128]{2,1,0:T(8,128)(2,1)}, bf16[2,288,128]{2,1,0:T(8,128)(2,1)S(1)}, u32[]{:S(2)}, u32[]{:S(2)}) %collective-permute-start) | collective-permute-done | bytes 147488 | tf_op jit(solution)/shard_map/ppermute | solution.py:60
  6.5 3.8 %collective-permute-start.1 = (bf16[2,2,1,288,128]{4,3,2,1,0:T(8,128)(2,1)S(1)}, bf16[2,2,1,288,128]{4,3,2,1,0:T(8,128)(2,1)S(1)}, u32[]{:S(2)}, u32[]{:S(2)}) collective-permute-start(bf16[2,2,1,288,128]{4,3,2,1,0:T(8,128)(2,1)S(1)} %maximum_add_fusion), channel_id=1, source_target_pairs={{0,1},{1,0},{2,3},{3,2},{4,5},{5,4},{6,7},{7,6},{8,9},{9,8},{10,11... | collective-permute-start | bytes 884744 | tf_op jit(solution)/shard_map/ppermute | solution.py:60
  12.3 4.4 %fusion.9 = f32[2,128,1076]{1,2,0:T(8,128)S(1)} fusion(bf16[2,1152,1076]{1,0,2:T(2,128)(2,1)} %param.13, bf16[2,1152,128]{2,1,0:T(8,128)(2,1)S(1)} %bitcast.116, f32[2,1152]{1,0:T(2,128)S(1)} %convert_element_type.118, f32[2,1152]{1,0:T(2,128)S(1)} %convert_element_type.117, f32[2,128]{1,0:T(2,128)S(1)} %add_rsqrt_fusion, ...), kind=kOutput, calls=%fused_computation.9 | convolution fusion | flops 636695552 | bytes 6678944 | tf_op jit(solution)/shard_map/ktd,kdf->ktf/dot_general | solution.py:178
  22.1 4.4 %collective-permute-done.3 = bf16[2,32,1152]{2,1,0:T(8,128)(2,1)S(1)} collective-permute-done((bf16[2,32,1152]{2,1,0:T(8,128)(2,1)S(1)}, bf16[2,32,1152]{2,1,0:T(8,128)(2,1)S(1)}, u32[]{:S(2)}, u32[]{:S(2)}) %collective-permute-start.3) | collective-permute-done | bytes 147488 | tf_op jit(solution)/shard_map/ppermute | solution.py:60
  29.2 5.5 %all-to-all-start = ((bf16[16,32,1152]{2,1,0:T(8,128)(2,1)}), bf16[16,32,1152]{2,1,0:T(8,128)(2,1)S(1)}, u32[]{:S(2)}, u32[]{:S(2)}) async-start(bf16[16,32,1152]{2,1,0:T(8,128)(2,1)} %broadcast_in_dim.4), calls=%async_computation | async-start | bytes 2359296 | tf_op jit(solution)/shard_map/all_to_all | solution.py:56
  34.7 3.1 %collective-permute-start.6 = (bf16[64,1152]{1,0:T(8,128)(2,1)S(1)}, bf16[64,1152]{1,0:T(8,128)(2,1)S(1)}, u32[]{:S(2)}, u32[]{:S(2)}) collective-permute-start(bf16[64,1152]{1,0:T(8,128)(2,1)S(1)} %pad_maximum_fusion.9), channel_id=1, source_target_pairs={{16,0},{49,1},{24,8},{57,9},{32,16},{1,17},{40,24},{9,25},{48,32},... | collective-permute-start | bytes 442376 | tf_op jit(solution)/shard_map/ppermute | solution.py:52
  39.4 4.3 %collective-permute-done.6 = bf16[64,1152]{1,0:T(8,128)(2,1)S(1)} collective-permute-done((bf16[64,1152]{1,0:T(8,128)(2,1)S(1)}, bf16[64,1152]{1,0:T(8,128)(2,1)S(1)}, u32[]{:S(2)}, u32[]{:S(2)}) %collective-permute-start.6) | collective-permute-done | bytes 147488 | tf_op jit(solution)/shard_map/ppermute | solution.py:52
  43.7 2.3 %collective-permute-start.7 = (bf16[64,1152]{1,0:T(8,128)(2,1)S(1)}, bf16[64,1152]{1,0:T(8,128)(2,1)S(1)}, u32[]{:S(2)}, u32[]{:S(2)}) collective-permute-start(bf16[64,1152]{1,0:T(8,128)(2,1)S(1)} %collective-permute-done.6), channel_id=1, source_target_pairs={{8,0},{57,1},{16,8},{1,9},{24,16},{9,17},{32,24},{17,25},{40,32},{... | collective-permute-start | bytes 442376 | tf_op jit(solution)/shard_map/ppermute | solution.py:52
  46.0 3.2 %collective-permute-start.8 = (bf16[32,1152]{1,0:T(8,128)(2,1)S(1)}, bf16[32,1152]{1,0:T(8,128)(2,1)S(1)}, u32[]{:S(2)}, u32[]{:S(2)}) collective-permute-start(bf16[32,1152]{1,0:T(8,128)(2,1)S(1)} %get-tuple-element.62), channel_id=1, source_target_pairs={{32,0},{33,1},{40,8},{41,9},{48,16},{49,17},{56,24},{57,25},{0,32}... | collective-permute-start | bytes 221192 | tf_op jit(solution)/shard_map/ppermute | solution.py:52
  49.2 4.0 %collective-permute-done.8 = bf16[32,1152]{1,0:T(8,128)(2,1)S(1)} collective-permute-done((bf16[32,1152]{1,0:T(8,128)(2,1)S(1)}, bf16[32,1152]{1,0:T(8,128)(2,1)S(1)}, u32[]{:S(2)}, u32[]{:S(2)}) %collective-permute-start.8) | collective-permute-done | bytes 73760 | tf_op jit(solution)/shard_map/ppermute | solution.py:52
  53.2 3.7 %collective-permute-start.9 = (bf16[224,1152]{1,0:T(8,128)(2,1)S(1)}, bf16[224,1152]{1,0:T(8,128)(2,1)S(1)}, u32[]{:S(2)}, u32[]{:S(2)}) collective-permute-start(bf16[224,1152]{1,0:T(8,128)(2,1)S(1)} %pad_maximum_fusion.4), channel_id=1, source_target_pairs={{0,1},{1,0},{2,3},{3,2},{4,5},{5,4},{6,7},{7,6},{8,9},{9,8},{10,11... | collective-permute-start | bytes 1548296 | tf_op jit(solution)/shard_map/ppermute | solution.py:60
  59.2 3.5 %shard_map.100 = (f32[64,1152]{1,0:T(8,128)S(1)}, bf16[224,1152]{1,0:T(8,128)(2,1)S(1)}, bf16[224,1152]{1,0:T(8,128)(2,1)S(1)}, bf16[512,1152]{1,0:T(8,128)(2,1)}) custom-call(f32[3]{0:T(128)S(1)} %pad_maximum_fusion.10.scalars, s32[2]{0:T(128)S(1)} %add_multiply_fusion.first, bf16[512,1152]{1,0:T(8,128)(2,1)S(1)} %pad_maximum_fusion.images, ...), custom_call_target="tpu_custom_call" | custom-call | flops 1811939328 | bytes 5898240 | tf_op jit(solution)/shard_map/pallas_call | solution.py:136
  62.7 6.9 %all-to-all-start.1 = ((bf16[16,32,1152]{2,1,0:T(8,128)(2,1)}), bf16[16,32,1152]{2,1,0:T(8,128)(2,1)S(1)}, u32[]{:S(2)}, u32[]{:S(2)}) async-start(bf16[16,32,1152]{2,1,0:T(8,128)(2,1)} %bitcast.23), calls=%async_computation.1 | async-start | bytes 2359296 | tf_op jit(solution)/shard_map/all_to_all | solution.py:56
  70.8 2.5 %collective-permute-start.11 = (bf16[32,1152]{1,0:T(8,128)(2,1)S(1)}, bf16[32,1152]{1,0:T(8,128)(2,1)S(1)}, u32[]{:S(2)}, u32[]{:S(2)}) collective-permute-start(bf16[32,1152]{1,0:T(8,128)(2,1)S(1)} %split.20), channel_id=1, source_target_pairs={{48,0},{17,1},{56,8},{25,9},{0,16},{33,17},{8,24},{41,25},{16,32},... | collective-permute-start | bytes 221192 | tf_op jit(solution)/shard_map/ppermute | solution.py:52
  73.4 1.8 %collective-permute-done.11 = bf16[32,1152]{1,0:T(8,128)(2,1)S(1)} collective-permute-done((bf16[32,1152]{1,0:T(8,128)(2,1)S(1)}, bf16[32,1152]{1,0:T(8,128)(2,1)S(1)}, u32[]{:S(2)}, u32[]{:S(2)}) %collective-permute-start.11) | collective-permute-done | bytes 73760 | tf_op jit(solution)/shard_map/ppermute | solution.py:52
  75.3 3.4 %collective-permute-start.12 = (bf16[64,1152]{1,0:T(8,128)(2,1)S(1)}, bf16[64,1152]{1,0:T(8,128)(2,1)S(1)}, u32[]{:S(2)}, u32[]{:S(2)}) collective-permute-start(bf16[64,1152]{1,0:T(8,128)(2,1)S(1)} %get-tuple-element.38), channel_id=1, source_target_pairs={{56,0},{9,1},{0,8},{17,9},{8,16},{25,17},{16,24},{33,25},{24,32},{... | collective-permute-start | bytes 442376 | tf_op jit(solution)/shard_map/ppermute | solution.py:52
  80.8 4.9 %collective-permute-done.14 = bf16[64,1152]{1,0:T(8,128)(2,1)S(1)} collective-permute-done((bf16[64,1152]{1,0:T(8,128)(2,1)S(1)}, bf16[64,1152]{1,0:T(8,128)(2,1)S(1)}, u32[]{:S(2)}, u32[]{:S(2)}) %collective-permute-start.14) | collective-permute-done | bytes 147488 | tf_op jit(solution)/shard_map/ppermute | solution.py:52
  88.8 3.5 %collective-permute-start.16 = (bf16[2,32,1152]{2,1,0:T(8,128)(2,1)S(1)}, bf16[2,32,1152]{2,1,0:T(8,128)(2,1)S(1)}, u32[]{:S(2)}, u32[]{:S(2)}) collective-permute-start(bf16[2,32,1152]{2,1,0:T(8,128)(2,1)S(1)} %fusion.24), channel_id=1, source_target_pairs={{0,2},{2,0},{1,3},{3,1},{4,6},{6,4},{5,7},{7,5},{8,10},{10,8},{9,1... | collective-permute-start | bytes 442376 | tf_op jit(solution)/shard_map/ppermute | solution.py:60
  93.0 3.3 %collective-permute-done.16 = bf16[2,32,1152]{2,1,0:T(8,128)(2,1)S(1)} collective-permute-done((bf16[2,32,1152]{2,1,0:T(8,128)(2,1)S(1)}, bf16[2,32,1152]{2,1,0:T(8,128)(2,1)S(1)}, u32[]{:S(2)}, u32[]{:S(2)}) %collective-permute-start.16) | collective-permute-done | bytes 147488 | tf_op jit(solution)/shard_map/ppermute | solution.py:60
  98.6 4.2 %fusion.18 = bf16[2,128,1076]{1,2,0:T(8,128)(2,1)S(1)} fusion(f32[2,128,1076]{1,2,0:T(8,128)S(1)} %fusion.32, bf16[2,1076,1152]{2,0,1:T(2,128)(2,1)} %param.15, bf16[2,64,1152]{2,1,0:T(8,128)(2,1)S(1)} %get-tuple-element.52, bf16[2,64,1152]{2,1,0:T(8,128)(2,1)S(1)} %get-tuple-element.51), kind=kOutput, calls=%fused_computation.12 | convolution fusion | flops 636381184 | bytes 7200768 | tf_op jit(solution)/shard_map/kte,kfe->ktf/dot_general | solution.py:212
  102.8 2.4 %fusion.72 = (f32[2,128]{1,0:T(2,128)S(1)}, f32[2,128]{1,0:T(2,128)S(1)}, f32[2,128,1152]{1,2,0:T(8,128)S(1)}) fusion(f32[2,128]{1,0:T(2,128)S(1)} %add_rsqrt_fusion, f32[2,128]{1,0:T(2,128)S(1)} %broadcast_multiply_fusion.2, bf16[2,1152,128]{2,1,0:T(8,128)(2,1)S(1)} %bitcast.118, f32[2,1152]{1,0:T(2,128)S(1)} %convert_element_type.117, ...), kind=kOutput, calls=%fused_computation.124 | convolution fusion | flops 636714496 | bytes 7291904 | tf_op jit(solution)/shard_map/ktf,kdf->ktd/dot_general | solution.py:214
  107.4 3.1 %collective-permute-start.19 = (bf16[2,288,128]{2,1,0:T(8,128)(2,1)S(1)}, bf16[2,288,128]{2,1,0:T(8,128)(2,1)S(1)}, u32[]{:S(2)}, u32[]{:S(2)}) collective-permute-start(bf16[2,288,128]{2,1,0:T(8,128)(2,1)S(1)} %fusion.62), channel_id=1, source_target_pairs={{0,2},{2,0},{1,3},{3,1},{4,6},{6,4},{5,7},{7,5},{8,10},{10,8},{9,1... | collective-permute-start | bytes 442376 | tf_op jit(solution)/shard_map/ppermute | solution.py:60
  110.7 3.3 %collective-permute-done.19 = bf16[2,288,128]{2,1,0:T(8,128)(2,1)S(1)} collective-permute-done((bf16[2,288,128]{2,1,0:T(8,128)(2,1)S(1)}, bf16[2,288,128]{2,1,0:T(8,128)(2,1)S(1)}, u32[]{:S(2)}, u32[]{:S(2)}) %collective-permute-start.19) | collective-permute-done | bytes 147488 | tf_op jit(solution)/shard_map/ppermute | solution.py:60
  (100 shorter events, 25.6 us)
Async XLA Ops:
  0.0 6.4 %collective-permute-start = (bf16[2,288,128]{2,1,0:T(8,128)(2,1)}, bf16[2,288,128]{2,1,0:T(8,128)(2,1)S(1)}, u32[]{:S(2)}, u32[]{:S(2)}) collective-permute-start(bf16[2,288,128]{2,1,0:T(8,128)(2,1)} %bitcast.129), channel_id=1, source_target_pairs={{0,2},{2,0},{1,3},{3,1},{4,6},{6,4},{5,7},{7,5},{8,10},{10,8},{9,1... | collective-permute-start | bytes 442376 | tf_op jit(solution)/shard_map/ppermute | solution.py:60
  6.5 5.0 %collective-permute-start.1 = (bf16[2,2,1,288,128]{4,3,2,1,0:T(8,128)(2,1)S(1)}, bf16[2,2,1,288,128]{4,3,2,1,0:T(8,128)(2,1)S(1)}, u32[]{:S(2)}, u32[]{:S(2)}) collective-permute-start(bf16[2,2,1,288,128]{4,3,2,1,0:T(8,128)(2,1)S(1)} %maximum_add_fusion), channel_id=1, source_target_pairs={{0,1},{1,0},{2,3},{3,2},{4,5},{5,4},{6,7},{7,6},{8,9},{9,8},{10,11... | collective-permute-start | bytes 884744 | tf_op jit(solution)/shard_map/ppermute | solution.py:60
  11.8 4.9 %slice-start = ((s8[4958208]{0:T(1024)(128)(4,1)}), s8[4194304]{0:T(1024)(128)(4,1)S(1)}, s32[]{:S(2)}) async-start(s8[4958208]{0:T(1024)(128)(4,1)} %bitcast.131), calls=%async_computation.2 | async-start | bytes 8388608
  12.3 4.5 %slice-start.1 = ((s8[4958208]{0:T(1024)(128)(4,1)}), s8[763904]{0:T(1024)(128)(4,1)S(1)}, s32[]{:S(2)}) async-start(s8[4958208]{0:T(1024)(128)(4,1)} %bitcast.131), calls=%async_computation.3 | async-start | bytes 1527808
  18.1 1.7 %collective-permute-start.2 = (bf16[2,64,1152]{2,1,0:T(8,128)(2,1)S(1)}, bf16[2,64,1152]{2,1,0:T(8,128)(2,1)S(1)}, u32[]{:S(2)}, u32[]{:S(2)}) collective-permute-start(bf16[2,64,1152]{2,1,0:T(8,128)(2,1)S(1)} %fusion.51), channel_id=1, source_target_pairs={{0,1},{1,0},{2,3},{3,2},{4,5},{5,4},{6,7},{7,6},{8,9},{9,8},{10,11... | collective-permute-start | bytes 884744 | tf_op jit(solution)/shard_map/ppermute | solution.py:60
  19.8 6.7 %collective-permute-start.3 = (bf16[2,32,1152]{2,1,0:T(8,128)(2,1)S(1)}, bf16[2,32,1152]{2,1,0:T(8,128)(2,1)S(1)}, u32[]{:S(2)}, u32[]{:S(2)}) collective-permute-start(bf16[2,32,1152]{2,1,0:T(8,128)(2,1)S(1)} %fusion.61), channel_id=1, source_target_pairs={{0,2},{2,0},{1,3},{3,1},{4,6},{6,4},{5,7},{7,5},{8,10},{10,8},{9,1... | collective-permute-start | bytes 442376 | tf_op jit(solution)/shard_map/ppermute | solution.py:60
  26.8 7.9 %collective-permute-start.4 = (bf16[32,1152]{1,0:T(8,128)(2,1)S(1)}, bf16[32,1152]{1,0:T(8,128)(2,1)S(1)}, u32[]{:S(2)}, u32[]{:S(2)}) collective-permute-start(bf16[32,1152]{1,0:T(8,128)(2,1)S(1)} %get-tuple-element.62), channel_id=1, source_target_pairs={{0,1},{1,0},{2,3},{3,2},{4,5},{5,4},{6,7},{7,6},{8,9},{9,8},{10,11... | collective-permute-start | bytes 221192 | tf_op jit(solution)/shard_map/ppermute | solution.py:60
  29.2 24.0 %all-to-all-start = ((bf16[16,32,1152]{2,1,0:T(8,128)(2,1)}), bf16[16,32,1152]{2,1,0:T(8,128)(2,1)S(1)}, u32[]{:S(2)}, u32[]{:S(2)}) async-start(bf16[16,32,1152]{2,1,0:T(8,128)(2,1)} %broadcast_in_dim.4), calls=%async_computation | async-start | bytes 2359296 | tf_op jit(solution)/shard_map/all_to_all | solution.py:56
  34.7 9.0 %collective-permute-start.6 = (bf16[64,1152]{1,0:T(8,128)(2,1)S(1)}, bf16[64,1152]{1,0:T(8,128)(2,1)S(1)}, u32[]{:S(2)}, u32[]{:S(2)}) collective-permute-start(bf16[64,1152]{1,0:T(8,128)(2,1)S(1)} %pad_maximum_fusion.9), channel_id=1, source_target_pairs={{16,0},{49,1},{24,8},{57,9},{32,16},{1,17},{40,24},{9,25},{48,32},... | collective-permute-start | bytes 442376 | tf_op jit(solution)/shard_map/ppermute | solution.py:52
  37.8 15.4 %collective-permute-start.5 = (bf16[64,1152]{1,0:T(8,128)(2,1)S(1)}, bf16[64,1152]{1,0:T(8,128)(2,1)S(1)}, u32[]{:S(2)}, u32[]{:S(2)}) collective-permute-start(bf16[64,1152]{1,0:T(8,128)(2,1)S(1)} %pad_maximum_fusion.9), channel_id=1, source_target_pairs={{8,0},{57,1},{16,8},{1,9},{24,16},{9,17},{32,24},{17,25},{40,32},{... | collective-permute-start | bytes 442376 | tf_op jit(solution)/shard_map/ppermute | solution.py:52
  43.7 9.5 %collective-permute-start.7 = (bf16[64,1152]{1,0:T(8,128)(2,1)S(1)}, bf16[64,1152]{1,0:T(8,128)(2,1)S(1)}, u32[]{:S(2)}, u32[]{:S(2)}) collective-permute-start(bf16[64,1152]{1,0:T(8,128)(2,1)S(1)} %collective-permute-done.6), channel_id=1, source_target_pairs={{8,0},{57,1},{16,8},{1,9},{24,16},{9,17},{32,24},{17,25},{40,32},{... | collective-permute-start | bytes 442376 | tf_op jit(solution)/shard_map/ppermute | solution.py:52
  46.0 7.2 %collective-permute-start.8 = (bf16[32,1152]{1,0:T(8,128)(2,1)S(1)}, bf16[32,1152]{1,0:T(8,128)(2,1)S(1)}, u32[]{:S(2)}, u32[]{:S(2)}) collective-permute-start(bf16[32,1152]{1,0:T(8,128)(2,1)S(1)} %get-tuple-element.62), channel_id=1, source_target_pairs={{32,0},{33,1},{40,8},{41,9},{48,16},{49,17},{56,24},{57,25},{0,32}... | collective-permute-start | bytes 221192 | tf_op jit(solution)/shard_map/ppermute | solution.py:52
  53.2 5.8 %collective-permute-start.9 = (bf16[224,1152]{1,0:T(8,128)(2,1)S(1)}, bf16[224,1152]{1,0:T(8,128)(2,1)S(1)}, u32[]{:S(2)}, u32[]{:S(2)}) collective-permute-start(bf16[224,1152]{1,0:T(8,128)(2,1)S(1)} %pad_maximum_fusion.4), channel_id=1, source_target_pairs={{0,1},{1,0},{2,3},{3,2},{4,5},{5,4},{6,7},{7,6},{8,9},{9,8},{10,11... | collective-permute-start | bytes 1548296 | tf_op jit(solution)/shard_map/ppermute | solution.py:60
  62.7 6.9 %collective-permute-start.10 = (bf16[224,1152]{1,0:T(8,128)(2,1)S(1)}, bf16[224,1152]{1,0:T(8,128)(2,1)}, u32[]{:S(2)}, u32[]{:S(2)}) collective-permute-start(bf16[224,1152]{1,0:T(8,128)(2,1)S(1)} %get-tuple-element.37), channel_id=1, source_target_pairs={{0,1},{1,0},{2,3},{3,2},{4,5},{5,4},{6,7},{7,6},{8,9},{9,8},{10,11... | collective-permute-start | bytes 1548296 | tf_op jit(solution)/shard_map/ppermute | solution.py:60
  62.7 23.3 %all-to-all-start.1 = ((bf16[16,32,1152]{2,1,0:T(8,128)(2,1)}), bf16[16,32,1152]{2,1,0:T(8,128)(2,1)S(1)}, u32[]{:S(2)}, u32[]{:S(2)}) async-start(bf16[16,32,1152]{2,1,0:T(8,128)(2,1)} %bitcast.23), calls=%async_computation.1 | async-start | bytes 2359296 | tf_op jit(solution)/shard_map/all_to_all | solution.py:56
  70.8 4.5 %collective-permute-start.11 = (bf16[32,1152]{1,0:T(8,128)(2,1)S(1)}, bf16[32,1152]{1,0:T(8,128)(2,1)S(1)}, u32[]{:S(2)}, u32[]{:S(2)}) collective-permute-start(bf16[32,1152]{1,0:T(8,128)(2,1)S(1)} %split.20), channel_id=1, source_target_pairs={{48,0},{17,1},{56,8},{25,9},{0,16},{33,17},{8,24},{41,25},{16,32},... | collective-permute-start | bytes 221192 | tf_op jit(solution)/shard_map/ppermute | solution.py:52
  73.3 5.4 %collective-permute-start.13 = (bf16[64,1152]{1,0:T(8,128)(2,1)S(1)}, bf16[64,1152]{1,0:T(8,128)(2,1)S(1)}, u32[]{:S(2)}, u32[]{:S(2)}) collective-permute-start(bf16[64,1152]{1,0:T(8,128)(2,1)S(1)} %get-tuple-element.55), channel_id=1, source_target_pairs={{56,0},{9,1},{0,8},{17,9},{8,16},{25,17},{16,24},{33,25},{24,32},{... | collective-permute-start | bytes 442376 | tf_op jit(solution)/shard_map/ppermute | solution.py:52
  75.3 5.5 %collective-permute-start.12 = (bf16[64,1152]{1,0:T(8,128)(2,1)S(1)}, bf16[64,1152]{1,0:T(8,128)(2,1)S(1)}, u32[]{:S(2)}, u32[]{:S(2)}) collective-permute-start(bf16[64,1152]{1,0:T(8,128)(2,1)S(1)} %get-tuple-element.38), channel_id=1, source_target_pairs={{56,0},{9,1},{0,8},{17,9},{8,16},{25,17},{16,24},{33,25},{24,32},{... | collective-permute-start | bytes 442376 | tf_op jit(solution)/shard_map/ppermute | solution.py:52
  78.8 6.9 %collective-permute-start.14 = (bf16[64,1152]{1,0:T(8,128)(2,1)S(1)}, bf16[64,1152]{1,0:T(8,128)(2,1)S(1)}, u32[]{:S(2)}, u32[]{:S(2)}) collective-permute-start(bf16[64,1152]{1,0:T(8,128)(2,1)S(1)} %fusion.54), channel_id=1, source_target_pairs={{48,0},{17,1},{56,8},{25,9},{0,16},{33,17},{8,24},{41,25},{16,32},... | collective-permute-start | bytes 442376 | tf_op jit(solution)/shard_map/ppermute | solution.py:52
  86.0 2.6 %collective-permute-start.15 = (bf16[32,1152]{1,0:T(8,128)(2,1)S(1)}, bf16[32,1152]{1,0:T(8,128)(2,1)S(1)}, u32[]{:S(2)}, u32[]{:S(2)}) collective-permute-start(bf16[32,1152]{1,0:T(8,128)(2,1)S(1)} %fusion.64), channel_id=1, source_target_pairs={{0,1},{1,0},{2,3},{3,2},{4,5},{5,4},{6,7},{7,6},{8,9},{9,8},{10,11... | collective-permute-start | bytes 221192 | tf_op jit(solution)/shard_map/ppermute | solution.py:60
  88.8 7.4 %collective-permute-start.16 = (bf16[2,32,1152]{2,1,0:T(8,128)(2,1)S(1)}, bf16[2,32,1152]{2,1,0:T(8,128)(2,1)S(1)}, u32[]{:S(2)}, u32[]{:S(2)}) collective-permute-start(bf16[2,32,1152]{2,1,0:T(8,128)(2,1)S(1)} %fusion.24), channel_id=1, source_target_pairs={{0,2},{2,0},{1,3},{3,1},{4,6},{6,4},{5,7},{7,5},{8,10},{10,8},{9,1... | collective-permute-start | bytes 442376 | tf_op jit(solution)/shard_map/ppermute | solution.py:60
  96.3 2.2 %collective-permute-start.17 = (bf16[2,64,1152]{2,1,0:T(8,128)(2,1)S(1)}, bf16[2,64,1152]{2,1,0:T(8,128)(2,1)S(1)}, u32[]{:S(2)}, u32[]{:S(2)}) collective-permute-start(bf16[2,64,1152]{2,1,0:T(8,128)(2,1)S(1)} %pad_maximum_fusion.7), channel_id=1, source_target_pairs={{0,1},{1,0},{2,3},{3,2},{4,5},{5,4},{6,7},{7,6},{8,9},{9,8},{10,11... | collective-permute-start | bytes 884744 | tf_op jit(solution)/shard_map/ppermute | solution.py:60
  105.6 1.7 %collective-permute-start.18 = (bf16[2,2,288,128]{3,2,1,0:T(8,128)(2,1)S(1)}, bf16[2,2,288,128]{3,2,1,0:T(8,128)(2,1)S(1)}, u32[]{:S(2)}, u32[]{:S(2)}) collective-permute-start(bf16[2,2,288,128]{3,2,1,0:T(8,128)(2,1)S(1)} %fusion.52), channel_id=1, source_target_pairs={{0,1},{1,0},{2,3},{3,2},{4,5},{5,4},{6,7},{7,6},{8,9},{9,8},{10,11... | collective-permute-start | bytes 884744 | tf_op jit(solution)/shard_map/ppermute | solution.py:60
  107.4 6.7 %collective-permute-start.19 = (bf16[2,288,128]{2,1,0:T(8,128)(2,1)S(1)}, bf16[2,288,128]{2,1,0:T(8,128)(2,1)S(1)}, u32[]{:S(2)}, u32[]{:S(2)}) collective-permute-start(bf16[2,288,128]{2,1,0:T(8,128)(2,1)S(1)} %fusion.62), channel_id=1, source_target_pairs={{0,2},{2,0},{1,3},{3,1},{4,6},{6,4},{5,7},{7,5},{8,10},{10,8},{9,1... | collective-permute-start | bytes 442376 | tf_op jit(solution)/shard_map/ppermute | solution.py:60
  (8 other events, 17.0 us)

commit v7 on v4

--- a/solution.py
+++ b/solution.py
@@ -176,6 +176,7 @@
     standard, inverse = layer_stats(inputs)
     gains = ln_gain.astype(F32)[:, None, :]
     normed = (standard * gains + ln_bias.astype(F32)[:, None, :]).astype(BF)
+    normed = lax.optimization_barrier(normed)
     preact = jnp.einsum("ktd,kdf->ktf", normed, fc1, preferred_element_type=F32)
     preact = preact + fc1_bias.astype(F32)[:, None, :]
     hidden = gelu_tanh(preact).astype(BF)

time: 113 us -> 114 us (level)
  no operation moved by 1% of the time
where the time goes in v7:
time: 114 us; the launch traced here: 113 us
  starting transfers between devices  50.9 us (45%)
  waiting for transfers between devices  35.3 us (31%)
  matrix products  11.9 us (10%)
  other arithmetic  6.71 us (6%)
  Pallas kernels  3.51 us (3%)
  local copies, waits for them, and re-layouts  2.58 us (2%)
  between operations  2.42 us (2%)
    ppermute x12, starting transfers between devices, swap(): return as_lies(lax.ppermute(as_lies(block), axis, [(0, 1), (1, 0)]))  22.4 us
    ppermute x12, waiting for transfers between devices, swap(): return as_lies(lax.ppermute(as_lies(block), axis, [(0, 1), (1, 0)]))  18.1 us
    ppermute x8, waiting for transfers between devices, hop(): return as_lies(lax.ppermute(as_lies(block), ('z', 'c'), pairs))  17.2 us
    ppermute x8, starting transfers between devices, hop(): return as_lies(lax.ppermute(as_lies(block), ('z', 'c'), pairs))  16.1 us
    all_to_all x2, starting transfers between devices, exchange(): return lax.all_to_all(parts, axes, 0, 0, tiled=True)  12.4 us
    dot_general x1, matrix products, on_device(): jnp.einsum('kte,kfe->ktf', block_low, fc2, preferred_element_type=F32)  4.16 us
    dot_general x1, matrix products, on_device(): preact = jnp.einsum('ktd,kdf->ktf', normed, fc1, preferred_element_type=F32)  4.08 us
    pallas_call x1, Pallas kernels, loss_block(): pl.pallas_call(functools.partial(loss_kernel, part_rows), in_specs=[small...  3.51 us
  transfers between devices with their start and end apart: 22, of which 15 were waited for; matrix products, arithmetic and copies ran while one was open for 5% of the time, Pallas kernels for 0%

profile of v7, /device:TPU:1, one launch (start us, length us, event | category | flops | bytes accessed | tf_op | source)
XLA Modules:
  0.0 113.3 jit_solution(10097139100107868648)
XLA Ops:
  0.0 3.6 %collective-permute-start = (bf16[2,288,128]{2,1,0:T(8,128)(2,1)}, bf16[2,288,128]{2,1,0:T(8,128)(2,1)S(1)}, u32[]{:S(2)}, u32[]{:S(2)}) collective-permute-start(bf16[2,288,128]{2,1,0:T(8,128)(2,1)} %bitcast.129), channel_id=1, source_target_pairs={{0,2},{2,0},{1,3},{3,1},{4,6},{6,4},{5,7},{7,5},{8,10},{10,8},{9,1... | collective-permute-start | bytes 442376 | tf_op jit(solution)/shard_map/ppermute | solution.py:60
  4.6 1.8 %collective-permute-done = bf16[2,288,128]{2,1,0:T(8,128)(2,1)S(1)} collective-permute-done((bf16[2,288,128]{2,1,0:T(8,128)(2,1)}, bf16[2,288,128]{2,1,0:T(8,128)(2,1)S(1)}, u32[]{:S(2)}, u32[]{:S(2)}) %collective-permute-start) | collective-permute-done | bytes 147488 | tf_op jit(solution)/shard_map/ppermute | solution.py:60
  6.5 3.8 %collective-permute-start.1 = (bf16[2,2,1,288,128]{4,3,2,1,0:T(8,128)(2,1)S(1)}, bf16[2,2,1,288,128]{4,3,2,1,0:T(8,128)(2,1)S(1)}, u32[]{:S(2)}, u32[]{:S(2)}) collective-permute-start(bf16[2,2,1,288,128]{4,3,2,1,0:T(8,128)(2,1)S(1)} %maximum_add_fusion), channel_id=1, source_target_pairs={{0,1},{1,0},{2,3},{3,2},{4,5},{5,4},{6,7},{7,6},{8,9},{9,8},{10,11... | collective-permute-start | bytes 884744 | tf_op jit(solution)/shard_map/ppermute | solution.py:60
  13.1 4.1 %fusion.9 = f32[2,128,1076]{1,2,0:T(8,128)S(1)} fusion(bf16[2,128,1152]{1,2,0:T(8,128)(2,1)S(1)} %add_convert_fusion, bf16[2,1152,1076]{1,0,2:T(2,128)(2,1)} %param.13, f32[2,1076]{1,0:T(2,128)S(1)} %convert_element_type.120), kind=kOutput, calls=%fused_computation.9 | convolution fusion | flops 634926080 | bytes 6658464 | tf_op jit(solution)/shard_map/ktd,kdf->ktf/dot_general | solution.py:180
  20.3 1.5 %collective-permute-start.3 = (bf16[2,32,1152]{2,1,0:T(8,128)(2,1)S(1)}, bf16[2,32,1152]{2,1,0:T(8,128)(2,1)S(1)}, u32[]{:S(2)}, u32[]{:S(2)}) collective-permute-start(bf16[2,32,1152]{2,1,0:T(8,128)(2,1)S(1)} %fusion.57), channel_id=1, source_target_pairs={{0,2},{2,0},{1,3},{3,1},{4,6},{6,4},{5,7},{7,5},{8,10},{10,8},{9,1... | collective-permute-start | bytes 442376 | tf_op jit(solution)/shard_map/ppermute | solution.py:60
  22.5 4.4 %collective-permute-done.3 = bf16[2,32,1152]{2,1,0:T(8,128)(2,1)S(1)} collective-permute-done((bf16[2,32,1152]{2,1,0:T(8,128)(2,1)S(1)}, bf16[2,32,1152]{2,1,0:T(8,128)(2,1)S(1)}, u32[]{:S(2)}, u32[]{:S(2)}) %collective-permute-start.3) | collective-permute-done | bytes 147488 | tf_op jit(solution)/shard_map/ppermute | solution.py:60
  29.6 5.5 %all-to-all-start = ((bf16[16,32,1152]{2,1,0:T(8,128)(2,1)}), bf16[16,32,1152]{2,1,0:T(8,128)(2,1)S(1)}, u32[]{:S(2)}, u32[]{:S(2)}) async-start(bf16[16,32,1152]{2,1,0:T(8,128)(2,1)} %broadcast_in_dim.4), calls=%async_computation | async-start | bytes 2359296 | tf_op jit(solution)/shard_map/all_to_all | solution.py:56
  35.2 3.1 %collective-permute-start.6 = (bf16[64,1152]{1,0:T(8,128)(2,1)S(1)}, bf16[64,1152]{1,0:T(8,128)(2,1)S(1)}, u32[]{:S(2)}, u32[]{:S(2)}) collective-permute-start(bf16[64,1152]{1,0:T(8,128)(2,1)S(1)} %pad_maximum_fusion.9), channel_id=1, source_target_pairs={{16,0},{49,1},{24,8},{57,9},{32,16},{1,17},{40,24},{9,25},{48,32},... | collective-permute-start | bytes 442376 | tf_op jit(solution)/shard_map/ppermute | solution.py:52
  38.2 1.6 %collective-permute-start.5 = (bf16[64,1152]{1,0:T(8,128)(2,1)S(1)}, bf16[64,1152]{1,0:T(8,128)(2,1)S(1)}, u32[]{:S(2)}, u32[]{:S(2)}) collective-permute-start(bf16[64,1152]{1,0:T(8,128)(2,1)S(1)} %pad_maximum_fusion.9), channel_id=1, source_target_pairs={{8,0},{57,1},{16,8},{1,9},{24,16},{9,17},{32,24},{17,25},{40,32},{... | collective-permute-start | bytes 442376 | tf_op jit(solution)/shard_map/ppermute | solution.py:52
  39.9 4.3 %collective-permute-done.6 = bf16[64,1152]{1,0:T(8,128)(2,1)S(1)} collective-permute-done((bf16[64,1152]{1,0:T(8,128)(2,1)S(1)}, bf16[64,1152]{1,0:T(8,128)(2,1)S(1)}, u32[]{:S(2)}, u32[]{:S(2)}) %collective-permute-start.6) | collective-permute-done | bytes 147488 | tf_op jit(solution)/shard_map/ppermute | solution.py:52
  44.1 2.3 %collective-permute-start.7 = (bf16[64,1152]{1,0:T(8,128)(2,1)S(1)}, bf16[64,1152]{1,0:T(8,128)(2,1)S(1)}, u32[]{:S(2)}, u32[]{:S(2)}) collective-permute-start(bf16[64,1152]{1,0:T(8,128)(2,1)S(1)} %collective-permute-done.6), channel_id=1, source_target_pairs={{8,0},{57,1},{16,8},{1,9},{24,16},{9,17},{32,24},{17,25},{40,32},{... | collective-permute-start | bytes 442376 | tf_op jit(solution)/shard_map/ppermute | solution.py:52
  46.8 6.1 %collective-permute-done.8 = bf16[32,1152]{1,0:T(8,128)(2,1)S(1)} collective-permute-done((bf16[32,1152]{1,0:T(8,128)(2,1)S(1)}, bf16[32,1152]{1,0:T(8,128)(2,1)S(1)}, u32[]{:S(2)}, u32[]{:S(2)}) %collective-permute-start.8) | collective-permute-done | bytes 73760 | tf_op jit(solution)/shard_map/ppermute | solution.py:52
  56.5 3.5 %shard_map.100 = (f32[64,1152]{1,0:T(8,128)S(1)}, bf16[224,1152]{1,0:T(8,128)(2,1)S(1)}, bf16[224,1152]{1,0:T(8,128)(2,1)S(1)}, bf16[512,1152]{1,0:T(8,128)(2,1)}) custom-call(f32[3]{0:T(128)S(1)} %pad_maximum_fusion.10.scalars, s32[2]{0:T(128)S(1)} %add_multiply_fusion.first, bf16[512,1152]{1,0:T(8,128)(2,1)S(1)} %pad_maximum_fusion.images, ...), custom_call_target="tpu_custom_call" | custom-call | flops 1811939328 | bytes 5898240 | tf_op jit(solution)/shard_map/pallas_call | solution.py:137
  60.1 6.9 %all-to-all-start.1 = ((bf16[16,32,1152]{2,1,0:T(8,128)(2,1)}), bf16[16,32,1152]{2,1,0:T(8,128)(2,1)S(1)}, u32[]{:S(2)}, u32[]{:S(2)}) async-start(bf16[16,32,1152]{2,1,0:T(8,128)(2,1)} %bitcast.23), calls=%async_computation.1 | async-start | bytes 2359296 | tf_op jit(solution)/shard_map/all_to_all | solution.py:56
  68.2 3.3 %collective-permute-start.11 = (bf16[32,1152]{1,0:T(8,128)(2,1)S(1)}, bf16[32,1152]{1,0:T(8,128)(2,1)S(1)}, u32[]{:S(2)}, u32[]{:S(2)}) collective-permute-start(bf16[32,1152]{1,0:T(8,128)(2,1)S(1)} %split.20), channel_id=1, source_target_pairs={{48,0},{17,1},{56,8},{25,9},{0,16},{33,17},{8,24},{41,25},{16,32},... | collective-permute-start | bytes 221192 | tf_op jit(solution)/shard_map/ppermute | solution.py:52
  73.5 3.8 %collective-permute-start.12 = (bf16[64,1152]{1,0:T(8,128)(2,1)S(1)}, bf16[64,1152]{1,0:T(8,128)(2,1)S(1)}, u32[]{:S(2)}, u32[]{:S(2)}) collective-permute-start(bf16[64,1152]{1,0:T(8,128)(2,1)S(1)} %get-tuple-element.38), channel_id=1, source_target_pairs={{56,0},{9,1},{0,8},{17,9},{8,16},{25,17},{16,24},{33,25},{24,32},{... | collective-permute-start | bytes 442376 | tf_op jit(solution)/shard_map/ppermute | solution.py:52
  79.4 4.5 %collective-permute-done.14 = bf16[64,1152]{1,0:T(8,128)(2,1)S(1)} collective-permute-done((bf16[64,1152]{1,0:T(8,128)(2,1)S(1)}, bf16[64,1152]{1,0:T(8,128)(2,1)S(1)}, u32[]{:S(2)}, u32[]{:S(2)}) %collective-permute-start.14) | collective-permute-done | bytes 147488 | tf_op jit(solution)/shard_map/ppermute | solution.py:52
  84.0 2.5 %collective-permute-start.15 = (bf16[32,1152]{1,0:T(8,128)(2,1)S(1)}, bf16[32,1152]{1,0:T(8,128)(2,1)S(1)}, u32[]{:S(2)}, u32[]{:S(2)}) collective-permute-start(bf16[32,1152]{1,0:T(8,128)(2,1)S(1)} %fusion.60), channel_id=1, source_target_pairs={{0,1},{1,0},{2,3},{3,2},{4,5},{5,4},{6,7},{7,6},{8,9},{9,8},{10,11... | collective-permute-start | bytes 221192 | tf_op jit(solution)/shard_map/ppermute | solution.py:60
  87.7 3.2 %collective-permute-start.16 = (bf16[2,32,1152]{2,1,0:T(8,128)(2,1)S(1)}, bf16[2,32,1152]{2,1,0:T(8,128)(2,1)S(1)}, u32[]{:S(2)}, u32[]{:S(2)}) collective-permute-start(bf16[2,32,1152]{2,1,0:T(8,128)(2,1)S(1)} %fusion.24), channel_id=1, source_target_pairs={{0,2},{2,0},{1,3},{3,1},{4,6},{6,4},{5,7},{7,5},{8,10},{10,8},{9,1... | collective-permute-start | bytes 442376 | tf_op jit(solution)/shard_map/ppermute | solution.py:60
  91.6 3.2 %collective-permute-done.16 = bf16[2,32,1152]{2,1,0:T(8,128)(2,1)S(1)} collective-permute-done((bf16[2,32,1152]{2,1,0:T(8,128)(2,1)S(1)}, bf16[2,32,1152]{2,1,0:T(8,128)(2,1)S(1)}, u32[]{:S(2)}, u32[]{:S(2)}) %collective-permute-start.16) | collective-permute-done | bytes 147488 | tf_op jit(solution)/shard_map/ppermute | solution.py:60
  97.2 4.2 %fusion.18 = bf16[2,128,1076]{1,2,0:T(8,128)(2,1)S(1)} fusion(f32[2,128,1076]{1,2,0:T(8,128)S(1)} %fusion.32, bf16[2,1076,1152]{2,0,1:T(2,128)(2,1)} %param.15, bf16[2,64,1152]{2,1,0:T(8,128)(2,1)S(1)} %get-tuple-element.52, bf16[2,64,1152]{2,1,0:T(8,128)(2,1)S(1)} %get-tuple-element.51), kind=kOutput, calls=%fused_computation.12 | convolution fusion | flops 636381184 | bytes 7200768 | tf_op jit(solution)/shard_map/kte,kfe->ktf/dot_general | solution.py:214
  101.4 2.4 %fusion.68 = (f32[2,128]{1,0:T(2,128)S(1)}, f32[2,128]{1,0:T(2,128)S(1)}, f32[2,128,1152]{1,2,0:T(8,128)S(1)}) fusion(f32[2,128]{1,0:T(2,128)S(1)} %add_rsqrt_fusion, f32[2,128]{1,0:T(2,128)S(1)} %broadcast_multiply_fusion.2, bf16[2,1152,128]{2,1,0:T(8,128)(2,1)S(1)} %bitcast.118, f32[2,1152]{1,0:T(2,128)S(1)} %convert_element_type.117, ...), kind=kOutput, calls=%fused_computation.121 | convolution fusion | flops 636714496 | bytes 7291904 | tf_op jit(solution)/shard_map/ktf,kdf->ktd/dot_general | solution.py:216
  106.0 3.1 %collective-permute-start.19 = (bf16[2,288,128]{2,1,0:T(8,128)(2,1)S(1)}, bf16[2,288,128]{2,1,0:T(8,128)(2,1)S(1)}, u32[]{:S(2)}, u32[]{:S(2)}) collective-permute-start(bf16[2,288,128]{2,1,0:T(8,128)(2,1)S(1)} %fusion.58), channel_id=1, source_target_pairs={{0,2},{2,0},{1,3},{3,1},{4,6},{6,4},{5,7},{7,5},{8,10},{10,8},{9,1... | collective-permute-start | bytes 442376 | tf_op jit(solution)/shard_map/ppermute | solution.py:60
  109.3 3.3 %collective-permute-done.19 = bf16[2,288,128]{2,1,0:T(8,128)(2,1)S(1)} collective-permute-done((bf16[2,288,128]{2,1,0:T(8,128)(2,1)S(1)}, bf16[2,288,128]{2,1,0:T(8,128)(2,1)S(1)}, u32[]{:S(2)}, u32[]{:S(2)}) %collective-permute-start.19) | collective-permute-done | bytes 147488 | tf_op jit(solution)/shard_map/ppermute | solution.py:60
  (102 shorter events, 25.0 us)
Async XLA Ops:
  0.0 6.4 %collective-permute-start = (bf16[2,288,128]{2,1,0:T(8,128)(2,1)}, bf16[2,288,128]{2,1,0:T(8,128)(2,1)S(1)}, u32[]{:S(2)}, u32[]{:S(2)}) collective-permute-start(bf16[2,288,128]{2,1,0:T(8,128)(2,1)} %bitcast.129), channel_id=1, source_target_pairs={{0,2},{2,0},{1,3},{3,1},{4,6},{6,4},{5,7},{7,5},{8,10},{10,8},{9,1... | collective-permute-start | bytes 442376 | tf_op jit(solution)/shard_map/ppermute | solution.py:60
  6.5 5.0 %collective-permute-start.1 = (bf16[2,2,1,288,128]{4,3,2,1,0:T(8,128)(2,1)S(1)}, bf16[2,2,1,288,128]{4,3,2,1,0:T(8,128)(2,1)S(1)}, u32[]{:S(2)}, u32[]{:S(2)}) collective-permute-start(bf16[2,2,1,288,128]{4,3,2,1,0:T(8,128)(2,1)S(1)} %maximum_add_fusion), channel_id=1, source_target_pairs={{0,1},{1,0},{2,3},{3,2},{4,5},{5,4},{6,7},{7,6},{8,9},{9,8},{10,11... | collective-permute-start | bytes 884744 | tf_op jit(solution)/shard_map/ppermute | solution.py:60
  11.8 5.3 %slice-start = ((s8[4958208]{0:T(1024)(128)(4,1)}), s8[4194304]{0:T(1024)(128)(4,1)S(1)}, s32[]{:S(2)}) async-start(s8[4958208]{0:T(1024)(128)(4,1)} %bitcast.131), calls=%async_computation.2 | async-start | bytes 8388608
  18.5 1.7 %collective-permute-start.2 = (bf16[2,64,1152]{2,1,0:T(8,128)(2,1)S(1)}, bf16[2,64,1152]{2,1,0:T(8,128)(2,1)S(1)}, u32[]{:S(2)}, u32[]{:S(2)}) collective-permute-start(bf16[2,64,1152]{2,1,0:T(8,128)(2,1)S(1)} %fusion.47), channel_id=1, source_target_pairs={{0,1},{1,0},{2,3},{3,2},{4,5},{5,4},{6,7},{7,6},{8,9},{9,8},{10,11... | collective-permute-start | bytes 884744 | tf_op jit(solution)/shard_map/ppermute | solution.py:60
  20.3 6.7 %collective-permute-start.3 = (bf16[2,32,1152]{2,1,0:T(8,128)(2,1)S(1)}, bf16[2,32,1152]{2,1,0:T(8,128)(2,1)S(1)}, u32[]{:S(2)}, u32[]{:S(2)}) collective-permute-start(bf16[2,32,1152]{2,1,0:T(8,128)(2,1)S(1)} %fusion.57), channel_id=1, source_target_pairs={{0,2},{2,0},{1,3},{3,1},{4,6},{6,4},{5,7},{7,5},{8,10},{10,8},{9,1... | collective-permute-start | bytes 442376 | tf_op jit(solution)/shard_map/ppermute | solution.py:60
  27.2 7.9 %collective-permute-start.4 = (bf16[32,1152]{1,0:T(8,128)(2,1)S(1)}, bf16[32,1152]{1,0:T(8,128)(2,1)S(1)}, u32[]{:S(2)}, u32[]{:S(2)}) collective-permute-start(bf16[32,1152]{1,0:T(8,128)(2,1)S(1)} %get-tuple-element.62), channel_id=1, source_target_pairs={{0,1},{1,0},{2,3},{3,2},{4,5},{5,4},{6,7},{7,6},{8,9},{9,8},{10,11... | collective-permute-start | bytes 221192 | tf_op jit(solution)/shard_map/ppermute | solution.py:60
  29.6 23.3 %all-to-all-start = ((bf16[16,32,1152]{2,1,0:T(8,128)(2,1)}), bf16[16,32,1152]{2,1,0:T(8,128)(2,1)S(1)}, u32[]{:S(2)}, u32[]{:S(2)}) async-start(bf16[16,32,1152]{2,1,0:T(8,128)(2,1)} %broadcast_in_dim.4), calls=%async_computation | async-start | bytes 2359296 | tf_op jit(solution)/shard_map/all_to_all | solution.py:56
  35.2 9.0 %collective-permute-start.6 = (bf16[64,1152]{1,0:T(8,128)(2,1)S(1)}, bf16[64,1152]{1,0:T(8,128)(2,1)S(1)}, u32[]{:S(2)}, u32[]{:S(2)}) collective-permute-start(bf16[64,1152]{1,0:T(8,128)(2,1)S(1)} %pad_maximum_fusion.9), channel_id=1, source_target_pairs={{16,0},{49,1},{24,8},{57,9},{32,16},{1,17},{40,24},{9,25},{48,32},... | collective-permute-start | bytes 442376 | tf_op jit(solution)/shard_map/ppermute | solution.py:52
  38.2 8.6 %collective-permute-start.5 = (bf16[64,1152]{1,0:T(8,128)(2,1)S(1)}, bf16[64,1152]{1,0:T(8,128)(2,1)S(1)}, u32[]{:S(2)}, u32[]{:S(2)}) collective-permute-start(bf16[64,1152]{1,0:T(8,128)(2,1)S(1)} %pad_maximum_fusion.9), channel_id=1, source_target_pairs={{8,0},{57,1},{16,8},{1,9},{24,16},{9,17},{32,24},{17,25},{40,32},{... | collective-permute-start | bytes 442376 | tf_op jit(solution)/shard_map/ppermute | solution.py:52
  44.1 8.7 %collective-permute-start.7 = (bf16[64,1152]{1,0:T(8,128)(2,1)S(1)}, bf16[64,1152]{1,0:T(8,128)(2,1)S(1)}, u32[]{:S(2)}, u32[]{:S(2)}) collective-permute-start(bf16[64,1152]{1,0:T(8,128)(2,1)S(1)} %collective-permute-done.6), channel_id=1, source_target_pairs={{8,0},{57,1},{16,8},{1,9},{24,16},{9,17},{32,24},{17,25},{40,32},{... | collective-permute-start | bytes 442376 | tf_op jit(solution)/shard_map/ppermute | solution.py:52
  46.4 6.5 %collective-permute-start.8 = (bf16[32,1152]{1,0:T(8,128)(2,1)S(1)}, bf16[32,1152]{1,0:T(8,128)(2,1)S(1)}, u32[]{:S(2)}, u32[]{:S(2)}) collective-permute-start(bf16[32,1152]{1,0:T(8,128)(2,1)S(1)} %constant_dynamic-slice_fusion), channel_id=1, source_target_pairs={{16,0},{49,1},{24,8},{57,9},{32,16},{1,17},{40,24},{9,25},{48,32},... | collective-permute-start | bytes 221192 | tf_op jit(solution)/shard_map/ppermute | solution.py:52
  52.9 3.5 %collective-permute-start.9 = (bf16[224,1152]{1,0:T(8,128)(2,1)S(1)}, bf16[224,1152]{1,0:T(8,128)(2,1)S(1)}, u32[]{:S(2)}, u32[]{:S(2)}) collective-permute-start(bf16[224,1152]{1,0:T(8,128)(2,1)S(1)} %pad_maximum_fusion.4), channel_id=1, source_target_pairs={{0,1},{1,0},{2,3},{3,2},{4,5},{5,4},{6,7},{7,6},{8,9},{9,8},{10,11... | collective-permute-start | bytes 1548296 | tf_op jit(solution)/shard_map/ppermute | solution.py:60
  60.0 7.0 %collective-permute-start.10 = (bf16[224,1152]{1,0:T(8,128)(2,1)S(1)}, bf16[224,1152]{1,0:T(8,128)(2,1)}, u32[]{:S(2)}, u32[]{:S(2)}) collective-permute-start(bf16[224,1152]{1,0:T(8,128)(2,1)S(1)} %get-tuple-element.37), channel_id=1, source_target_pairs={{0,1},{1,0},{2,3},{3,2},{4,5},{5,4},{6,7},{7,6},{8,9},{9,8},{10,11... | collective-permute-start | bytes 1548296 | tf_op jit(solution)/shard_map/ppermute | solution.py:60
  60.1 23.9 %all-to-all-start.1 = ((bf16[16,32,1152]{2,1,0:T(8,128)(2,1)}), bf16[16,32,1152]{2,1,0:T(8,128)(2,1)S(1)}, u32[]{:S(2)}, u32[]{:S(2)}) async-start(bf16[16,32,1152]{2,1,0:T(8,128)(2,1)} %bitcast.23), calls=%async_computation.1 | async-start | bytes 2359296 | tf_op jit(solution)/shard_map/all_to_all | solution.py:56
  68.2 5.3 %collective-permute-start.11 = (bf16[32,1152]{1,0:T(8,128)(2,1)S(1)}, bf16[32,1152]{1,0:T(8,128)(2,1)S(1)}, u32[]{:S(2)}, u32[]{:S(2)}) collective-permute-start(bf16[32,1152]{1,0:T(8,128)(2,1)S(1)} %split.20), channel_id=1, source_target_pairs={{48,0},{17,1},{56,8},{25,9},{0,16},{33,17},{8,24},{41,25},{16,32},... | collective-permute-start | bytes 221192 | tf_op jit(solution)/shard_map/ppermute | solution.py:52
  71.5 5.8 %collective-permute-start.13 = (bf16[64,1152]{1,0:T(8,128)(2,1)S(1)}, bf16[64,1152]{1,0:T(8,128)(2,1)S(1)}, u32[]{:S(2)}, u32[]{:S(2)}) collective-permute-start(bf16[64,1152]{1,0:T(8,128)(2,1)S(1)} %get-tuple-element.55), channel_id=1, source_target_pairs={{56,0},{9,1},{0,8},{17,9},{8,16},{25,17},{16,24},{33,25},{24,32},{... | collective-permute-start | bytes 442376 | tf_op jit(solution)/shard_map/ppermute | solution.py:52
  73.5 5.9 %collective-permute-start.12 = (bf16[64,1152]{1,0:T(8,128)(2,1)S(1)}, bf16[64,1152]{1,0:T(8,128)(2,1)S(1)}, u32[]{:S(2)}, u32[]{:S(2)}) collective-permute-start(bf16[64,1152]{1,0:T(8,128)(2,1)S(1)} %get-tuple-element.38), channel_id=1, source_target_pairs={{56,0},{9,1},{0,8},{17,9},{8,16},{25,17},{16,24},{33,25},{24,32},{... | collective-permute-start | bytes 442376 | tf_op jit(solution)/shard_map/ppermute | solution.py:52
  77.4 6.5 %collective-permute-start.14 = (bf16[64,1152]{1,0:T(8,128)(2,1)S(1)}, bf16[64,1152]{1,0:T(8,128)(2,1)S(1)}, u32[]{:S(2)}, u32[]{:S(2)}) collective-permute-start(bf16[64,1152]{1,0:T(8,128)(2,1)S(1)} %fusion.50), channel_id=1, source_target_pairs={{48,0},{17,1},{56,8},{25,9},{0,16},{33,17},{8,24},{41,25},{16,32},... | collective-permute-start | bytes 442376 | tf_op jit(solution)/shard_map/ppermute | solution.py:52
  84.0 3.4 %collective-permute-start.15 = (bf16[32,1152]{1,0:T(8,128)(2,1)S(1)}, bf16[32,1152]{1,0:T(8,128)(2,1)S(1)}, u32[]{:S(2)}, u32[]{:S(2)}) collective-permute-start(bf16[32,1152]{1,0:T(8,128)(2,1)S(1)} %fusion.60), channel_id=1, source_target_pairs={{0,1},{1,0},{2,3},{3,2},{4,5},{5,4},{6,7},{7,6},{8,9},{9,8},{10,11... | collective-permute-start | bytes 221192 | tf_op jit(solution)/shard_map/ppermute | solution.py:60
  87.7 7.1 %collective-permute-start.16 = (bf16[2,32,1152]{2,1,0:T(8,128)(2,1)S(1)}, bf16[2,32,1152]{2,1,0:T(8,128)(2,1)S(1)}, u32[]{:S(2)}, u32[]{:S(2)}) collective-permute-start(bf16[2,32,1152]{2,1,0:T(8,128)(2,1)S(1)} %fusion.24), channel_id=1, source_target_pairs={{0,2},{2,0},{1,3},{3,1},{4,6},{6,4},{5,7},{7,5},{8,10},{10,8},{9,1... | collective-permute-start | bytes 442376 | tf_op jit(solution)/shard_map/ppermute | solution.py:60
  94.8 2.3 %collective-permute-start.17 = (bf16[2,64,1152]{2,1,0:T(8,128)(2,1)S(1)}, bf16[2,64,1152]{2,1,0:T(8,128)(2,1)S(1)}, u32[]{:S(2)}, u32[]{:S(2)}) collective-permute-start(bf16[2,64,1152]{2,1,0:T(8,128)(2,1)S(1)} %pad_maximum_fusion.7), channel_id=1, source_target_pairs={{0,1},{1,0},{2,3},{3,2},{4,5},{5,4},{6,7},{7,6},{8,9},{9,8},{10,11... | collective-permute-start | bytes 884744 | tf_op jit(solution)/shard_map/ppermute | solution.py:60
  97.1 4.3 %slice-start.2 = ((s8[4958208]{0:T(1024)(128)(4,1)}), s8[4194304]{0:T(1024)(128)(4,1)S(1)}, s32[]{:S(2)}) async-start(s8[4958208]{0:T(1024)(128)(4,1)} %bitcast.133), calls=%async_computation.4 | async-start | bytes 8388608
  104.2 1.7 %collective-permute-start.18 = (bf16[2,2,288,128]{3,2,1,0:T(8,128)(2,1)S(1)}, bf16[2,2,288,128]{3,2,1,0:T(8,128)(2,1)S(1)}, u32[]{:S(2)}, u32[]{:S(2)}) collective-permute-start(bf16[2,2,288,128]{3,2,1,0:T(8,128)(2,1)S(1)} %fusion.48), channel_id=1, source_target_pairs={{0,1},{1,0},{2,3},{3,2},{4,5},{5,4},{6,7},{7,6},{8,9},{9,8},{10,11... | collective-permute-start | bytes 884744 | tf_op jit(solution)/shard_map/ppermute | solution.py:60
  106.0 6.7 %collective-permute-start.19 = (bf16[2,288,128]{2,1,0:T(8,128)(2,1)S(1)}, bf16[2,288,128]{2,1,0:T(8,128)(2,1)S(1)}, u32[]{:S(2)}, u32[]{:S(2)}) collective-permute-start(bf16[2,288,128]{2,1,0:T(8,128)(2,1)S(1)} %fusion.58), channel_id=1, source_target_pairs={{0,2},{2,0},{1,3},{3,1},{4,6},{6,4},{5,7},{7,5},{8,10},{10,8},{9,1... | collective-permute-start | bytes 442376 | tf_op jit(solution)/shard_map/ppermute | solution.py:60
  (8 other events, 16.5 us)
